TPU v7x, 256 devices: a whole 4x4x8 slice. The times are simulated.
256 devices in a mesh: pool: 8 (over z), head: 32 (over y, x, core).
Axes of the slice: x: 4, y: 4, z: 8, core: 2. Of those that a mesh axis runs over, the one named last changes fastest.
Arguments:
- queries: bfloat16 [4096, 24576], P('pool', 'head'), may hold values from -8 to 8
- new_latent: bfloat16 [4096, 576], P('pool'), may hold values from -6 to 6
- latent_pool: bfloat16 [4096, 4608], P(('pool', 'head')), may hold values from -6 to 6
- w_ukv: bfloat16 [512, 32768], P(None, 'head'), may hold values from -0.25 to 0.25
- w_out: bfloat16 [16384, 7168], P('head'), may hold values from -0.375 to 0.375
- cached_len: int32 [8], replicated, may hold values from 1 to 2048, 5461 in all
- page_loc: int32 [8, 256], replicated, may hold values from 0 to 4095, as said below
Outputs:
- output: bfloat16 [4096, 7168], P('pool', 'head')
Inputs may be any that keep to these rules, and one draw needn't show every extreme that they name: `page_loc`: page slot s of every request lies on a device whose head index is s mod 32 (the pool's pages are laid out device after device, 16 on each, devices in pool-major order); every device holds exactly 1 of the page slots of each request; no page is named twice.
All inputs are finite; a program needn't handle non-finite values.
Results may differ from a plain program's by a relative error of at most 0.02.
Values may be sent and summed in bfloat16 or wider, within the bound.
No kernel may reach another device: no remote copies, remote signals or barrier semaphores. Data moves between devices by JAX's collectives and lax.ppermute only.
A program may use at most 64 MiB of HBM per device.

v0:
```python
import jax
import jax.numpy as jnp
from jax import lax
from jax.sharding import PartitionSpec as P

NOPE = 128
ROPE = 64
VD = 128
KV = 512
NEW = 512
PAGE = 8
MAXP = 256


def per_device(queries, new_latent, latent_pool, w_ukv, w_out, cached_len, page_loc):
    n_pool = lax.axis_size("pool")
    n_head = lax.axis_size("head")
    pool_id = lax.axis_index("pool")
    head_id = lax.axis_index("head")
    latent_width = KV + ROPE
    heads_here = w_out.shape[0] // VD
    lifted_cols = heads_here * (NOPE + VD)
    lifted_width = lifted_cols + ROPE
    pages_dev = latent_pool.shape[0]
    slot_count = MAXP // n_head
    capacity = slot_count // n_pool
    page_table = page_loc.reshape(n_pool, slot_count, n_head)
    owner_pool = page_table // pages_dev // n_head
    local_page = page_table % pages_dev
    positions = jnp.arange(slot_count, dtype=jnp.int32)
    same_owner = owner_pool[:, :, None, :] == owner_pool[:, None, :, :]
    before = positions[None, None, :, None] < positions[None, :, None, None]
    ranks = jnp.sum(same_owner & before, axis=2)
    my_owner = lax.dynamic_index_in_dim(owner_pool, head_id, 2, keepdims=False)
    my_rank = lax.dynamic_index_in_dim(ranks, head_id, 2, keepdims=False)
    my_local = lax.dynamic_index_in_dim(local_page, head_id, 2, keepdims=False)
    matches = my_owner == pool_id
    chosen = matches[:, :, None] & (
        my_rank[:, :, None] == jnp.arange(capacity, dtype=jnp.int32)[None, None, :]
    )
    send_index = jnp.sum(jnp.where(chosen, my_local[:, :, None], 0), axis=1)
    outgoing = latent_pool[send_index]
    request_owner = lax.dynamic_index_in_dim(owner_pool, pool_id, 0, keepdims=False)
    request_rank = lax.dynamic_index_in_dim(ranks, pool_id, 0, keepdims=False)
    length = lax.dynamic_index_in_dim(cached_len, pool_id, 0, keepdims=False)

    def lift(latent_rows):
        lifted = jnp.dot(latent_rows[:, :KV], w_ukv, preferred_element_type=jnp.float32).astype(
            jnp.bfloat16
        )
        return jnp.concatenate([lifted, latent_rows[:, KV:]], 1)

    arrived = lax.all_to_all(outgoing, "pool", split_axis=0, concat_axis=0, tiled=True)
    own_owner = lax.dynamic_index_in_dim(request_owner, head_id, 1, keepdims=False)
    own_rank = lax.dynamic_index_in_dim(request_rank, head_id, 1, keepdims=False)
    flat_index = own_owner * capacity + own_rank
    held_pages = arrived.reshape(n_pool * capacity, PAGE * latent_width)[flat_index]
    portion = lax.all_gather(held_pages[:, None, :], "head", axis=1, tiled=True)
    columns = portion.shape[1]
    latent_rows = portion.reshape(slot_count * columns * PAGE, latent_width)
    spread = lift(latent_rows).reshape(slot_count, columns, PAGE * lifted_width)
    prefix_keys = spread.reshape(slot_count * n_head * PAGE, lifted_width)
    prefix_count = MAXP * PAGE
    keys_all = jnp.concatenate([prefix_keys, lift(new_latent)], 0)
    key_count = keys_all.shape[0]
    head_keys_all = keys_all[:, :lifted_cols].reshape(key_count, heads_here, NOPE + VD)
    rope_keys = keys_all[:, lifted_cols:]
    query_heads = queries.reshape(NEW, heads_here, NOPE + ROPE)
    key_pos = jnp.arange(key_count, dtype=jnp.int32)[None, :]
    query_pos = jnp.arange(NEW, dtype=jnp.int32)[:, None]
    allowed = (key_pos < length) | (key_pos >= prefix_count) & (key_pos - prefix_count <= query_pos)
    score_scale = (NOPE + ROPE) ** (-0.5)

    def one_head(head_slot):
        head_query = lax.dynamic_index_in_dim(query_heads, head_slot, 1, keepdims=False)
        head_keys = lax.dynamic_index_in_dim(head_keys_all, head_slot, 1, keepdims=False)
        scores = jnp.einsum(
            "qd,kd->qk",
            head_query[:, :NOPE],
            head_keys[:, :NOPE],
            preferred_element_type=jnp.float32,
        )
        scores = scores + jnp.einsum(
            "qd,kd->qk", head_query[:, NOPE:], rope_keys, preferred_element_type=jnp.float32
        )
        scores = jnp.where(allowed, scores * score_scale, -jnp.inf)
        row_max = jnp.max(scores, axis=1, keepdims=True)
        raised = jnp.exp(scores - row_max)
        weights = (raised / jnp.sum(raised, axis=1, keepdims=True)).astype(jnp.bfloat16)
        return jnp.dot(weights, head_keys[:, NOPE:], preferred_element_type=jnp.float32).astype(
            jnp.bfloat16
        )

    per_head = lax.map(one_head, jnp.arange(heads_here, dtype=jnp.int32))
    attended = jnp.transpose(per_head, (1, 0, 2)).reshape(NEW, heads_here * VD)
    own_cols = (
        lax.psum_scatter(
            lax.dot_general(
                w_out, attended, (((0,), (1,)), ((), ())), preferred_element_type=jnp.float32
            ).astype(jnp.bfloat16),
            "head",
            scatter_dimension=0,
            tiled=True,
        )
        .astype(jnp.float32)
        .T
    )
    return own_cols.astype(jnp.bfloat16)


def solution(mesh):
    placed = (
        P("pool", "head"),
        P("pool", None),
        P(("pool", "head"), None),
        P(None, "head"),
        P("head", None),
        P(),
        P(),
    )
    return jax.shard_map(
        per_device, mesh=mesh, in_specs=placed, out_specs=P("pool", "head"), check_vma=False
    )
```

profile of v0, /device:TPU:32, one launch (start us, length us, event | category | flops | bytes accessed | tf_op | source)
XLA Modules:
  0.0 283.0 jit_solution(17788833532326083198)
XLA Ops:
  8.0 1.6 gather_fusion
  11.4 8.6 %all-to-all-start = ((bf16[8,2,2304]{2,1,0:T(2,128)(2,1)}), bf16[8,2,2304]{2,1,0:T(2,128)(2,1)S(1)}, u32[]{:S(2)}, u32[]{:S(2)}) async-start(bf16[8,2,2304]{2,1,0:T(2,128)(2,1)} %reshape.218), calls=%async_computation | async-start | bytes 147456 | tf_op jit(solution)/shard_map/all_to_all | solution.py:53
  20.2 6.8 %all-to-all-done = bf16[8,2,2304]{2,1,0:T(2,128)(2,1)S(1)} async-done(((bf16[8,2,2304]{2,1,0:T(2,128)(2,1)}), bf16[8,2,2304]{2,1,0:T(2,128)(2,1)S(1)}, u32[]{:S(2)}, u32[]{:S(2)}) %all-to-all-start) | async-done | bytes 73760 | tf_op jit(solution)/shard_map/all_to_all | solution.py:53
  30.5 2.3 copy.67
  33.4 2.8 convolution_convert_fusion.2
  36.2 38.9 %all-gather.3.cloned.1.call-done = bf16[8,147456]{1,0:T(8,128)(2,1)} async-done(((bf16[8,4608]{1,0:T(8,128)(2,1)}), bf16[8,147456]{1,0:T(8,128)(2,1)}) %all-gather.3.cloned.1.call-update) | async-done | bytes 2359312 | tf_op jit(solution)/shard_map/all_gather | solution.py:58
  75.1 2.7 reshape.216
  77.8 3.4 %reshape.192 = bf16[2048,576]{1,0:T(8,128)(2,1)} reshape(bf16[1179648]{0:T(1024)(128)(2,1)S(1)} %reshape.216) | data formatting | bytes 4718592 | tf_op jit(solution)/shard_map/reshape | solution.py:60
  81.2 6.0 %convolution_convert_fusion.1 = bf16[2048,1024]{0,1:T(8,128)(2,1)} fusion(bf16[512,1024]{1,0:T(8,128)(2,1)S(1)} %copy-done, bf16[2048,576]{1,0:T(8,128)(2,1)} %reshape.192), kind=kOutput, calls=%fused_computation.24 | convolution fusion | flops 2149580800 | bytes 7340032 | tf_op jit(solution)/shard_map/dot_general | solution.py:48
  87.4 2.1 copy-done.2
  89.6 13.6 %maximum_maximum_fusion = bf16[2560,1088]{0,1:T(8,128)(2,1)S(1)} fusion(bf16[512,64]{0,1:T(8,128)(2,1)S(1)} %slice.33, bf16[512,1024]{0,1:T(8,128)(2,1)S(1)} %copy-done.3, bf16[2048,64]{0,1:T(8,128)(2,1)S(1)} %copy.83, bf16[2048,1024]{0,1:T(8,128)(2,1)S(1)} %copy-done.2), kind=kLoop, calls=%fused_computation.23 | loop fusion | flops 22282240 | bytes 11141120 | tf_op jit(solution)/shard_map/concatenate | solution.py:64
  103.2 2.6 slice.50
  106.2 53.6 %while.11 = (s32[]{:T(128)}, bf16[4,512,128]{1,2,0:T(8,128)(2,1)}, s32[4]{0:T(128)S(1)}, bf16[512,4,192]{0,2,1:T(8,128)(2,1)}, bf16[2560,4,256]{0,2,1:T(8,128)(2...) while((s32[]{:T(128)}, bf16[4,512,128]{1,2,0:T(8,128)(2,1)}, ...), condition=%wide.region_5.6_spmd.clone, body=%wide.region_2.5_spmd.clone.sunk | while | flops 854653952 | bytes 39940308 | solution.py:94
  112.7 2.0 fusion.42
  114.6 2.0 fusion.43
  126.1 2.0 fusion.42
  128.0 2.0 fusion.43
  139.4 2.0 fusion.42
  141.4 2.0 fusion.43
  152.8 2.0 fusion.42
  154.7 2.0 fusion.43
  159.8 10.2 %fusion.13 = bf16[7168,512]{0,1:T(8,128)(2,1)} fusion(bf16[512,512]{0,1:T(8,128)(2,1)} %bitcast.49, bf16[512,7168]{1,0:T(8,128)(2,1)} %param.13), kind=kOutput, calls=%fused_computation.22 | convolution fusion | flops 3761766400 | bytes 15204352 | tf_op jit(solution)/shard_map/dot_general | solution.py:98
  170.0 10.4 %copy.76 = bf16[7168,512]{1,0:T(8,128)(2,1)} copy(bf16[7168,512]{0,1:T(8,128)(2,1)} %fusion.13) | data formatting | bytes 14680064
  180.5 95.7 %reduce-scatter.4.cloned.1.call-done = bf16[224,512]{1,0:T(8,128)(2,1)} async-done(((bf16[7168,512]{1,0:T(8,128)(2,1)}), bf16[224,512]{1,0:T(8,128)(2,1)}) %reduce-scatter.4.cloned.1.call-update) | async-done | bytes 229392
  (77 shorter events, 37.9 us)
Async XLA Ops:
  6.5 26.9 %copy-start = (bf16[512,1024]{1,0:T(8,128)(2,1)S(1)}, bf16[512,1024]{1,0:T(8,128)(2,1)}, u32[]{:S(2)}) copy-start(bf16[512,1024]{1,0:T(8,128)(2,1)} %param.12) | copy-start | bytes 3145732
  11.4 15.6 %all-to-all-start = ((bf16[8,2,2304]{2,1,0:T(2,128)(2,1)}), bf16[8,2,2304]{2,1,0:T(2,128)(2,1)S(1)}, u32[]{:S(2)}, u32[]{:S(2)}) async-start(bf16[8,2,2304]{2,1,0:T(2,128)(2,1)} %reshape.218), calls=%async_computation | async-start | bytes 147456 | tf_op jit(solution)/shard_map/all_to_all | solution.py:53
  20.0 55.1 %all-gather.3.cloned.1.call-start = ((), (), s32[]{:S(2)}) async-start(), calls=%async_computation.2 | async-start | bytes 2433024 | tf_op jit(solution)/shard_map/all_gather | solution.py:58
  28.3 247.9 %reduce-scatter.4.cloned.1.call-start = ((), (), s32[]{:S(2)}) async-start(), calls=%async_computation.3 | async-start | bytes 7569408
  81.1 6.0 %slice-start = ((bf16[2048,576]{1,0:T(8,128)(2,1)}), bf16[2048,64]{1,0:T(8,128)(2,1)S(1)}, s32[]{:S(2)}) async-start(bf16[2048,576]{1,0:T(8,128)(2,1)} %reshape.192), calls=%async_computation.4 | async-start | bytes 1048576 | tf_op jit(solution)/shard_map/slice | solution.py:51
  81.2 6.2 %copy-start.3 = (bf16[512,1024]{0,1:T(8,128)(2,1)S(1)}, bf16[512,1024]{0,1:T(8,128)(2,1)}, u32[]{:S(2)}) copy-start(bf16[512,1024]{0,1:T(8,128)(2,1)} %convolution_convert_fusion.2) | copy-start | bytes 3145732
  87.4 2.2 copy-start.2
  116.6 1.3 copy-start.1
  130.0 1.3 copy-start.1
  143.3 1.3 copy-start.1
  156.7 1.3 copy-start.1
Sparse Core Ops, SparseCore 0:
  28.4 46.5 all-gather.2
  180.6 95.5 reduce-scatter.3
where the time goes:
time: 284 us; the launch traced here: 283 us
  waiting for transfers between devices  141 us (50%)
  local copies, waits for them, and re-layouts  53.7 us (19%)
  matrix products  38.7 us (14%)
  other arithmetic  18.9 us (7%)
  between operations  13.6 us (5%)
  starting transfers between devices  8.61 us (3%)
  loops' own time  8.08 us (3%)
    unnamed x3, waiting for transfers between devices  95.7 us
    all_gather x1, waiting for transfers between devices, per_device(): portion = lax.all_gather(held_pages[:, None, :], 'head', axis=1, tiled=True)  38.9 us
    unnamed x14, local copies, waits for them, and re-layouts  18.9 us
    concatenate x1, other arithmetic, per_device(): keys_all = jnp.concatenate([prefix_keys, lift(new_latent)], 0)  13.6 us
    dynamic_slice x8, local copies, waits for them, and re-layouts, one_head(): lax.dynamic_index_in_dim(head_keys_all, head_slot, 1, keepdims=False)  11.4 us
    dot_general x1, matrix products, per_device(): lax.dot_general(w_out, attended, (((0,), (1,)), ((), ())), preferred_elem...  10.2 us
    dot_general x2, matrix products, lift(): jnp.dot(latent_rows[:, :KV], w_ukv, preferred_element_type=jnp.float32)  8.78 us
    all_to_all x1, starting transfers between devices, per_device(): lax.all_to_all(outgoing, 'pool', split_axis=0, concat_axis=0, tiled=True)  8.57 us
  transfers between devices with their start and end apart: 3, of which 3 were waited for; matrix products, arithmetic and copies ran while one was open for 3% of the time, Pallas kernels for 0%

commit v1 on v0

v1 whole, which is shorter than its diff:
```python
import functools

import jax
import jax.numpy as jnp
from jax import lax
from jax.experimental import pallas as pl
from jax.experimental.pallas import tpu as pltpu
from jax.sharding import PartitionSpec as P

NOPE = 128
ROPE = 64
VD = 128
KV = 512
NEW = 512
PAGE = 8
MAXP = 256
HPD = 4
REQ = 8
N_HEAD = 32
PAGES_DEV = 16
D = 7168
COLS = D // N_HEAD
WIDTH = KV + ROPE
PAY = KV + 128
HALF = NEW // 2
SIDE = 4
BLOCKED = -1e30
SCALE = (NOPE + ROPE) ** -0.5 * 1.4426950408889634
BF = jnp.bfloat16
F32 = jnp.float32
NT = (((1,), (1,)), ((), ()))
VMEM = pl.BlockSpec(memory_space=pltpu.VMEM)
SMEM = pl.BlockSpec(memory_space=pltpu.SMEM)


def head_index(y, x, c):
    return ((y % SIDE) * SIDE + x % SIDE) * 2 + c


def plane_perm(move):
    return [
        (head_index(y, x, c), head_index(*move(y, x, c)))
        for y in range(SIDE)
        for x in range(SIDE)
        for c in range(2)
    ]


SWAP = plane_perm(lambda y, x, c: (y, x, 1 - c))


def along_x(d):
    return plane_perm(lambda y, x, c: (y, x + d, c))


def along_y(d):
    return plane_perm(lambda y, x, c: (y + d, x, c))


def send(value, perm):
    return lax.ppermute(value, "head", perm)


def params(mib):
    return pltpu.CompilerParams(vmem_limit_bytes=mib << 20)


def cost(flops, nbytes, trans=0):
    return pl.CostEstimate(flops=flops, bytes_accessed=nbytes, transcendentals=trans)


def pages_kernel(place, lens, locs, pool_ref, out_ref, wide, rows):
    wide[...] = pool_ref[...].astype(F32)
    pool_id = place[0]
    head_id = place[1]
    lane = lax.broadcasted_iota(jnp.int32, (1, 128), 1)

    def one_request(r, carry):
        sel = jnp.int32(0)
        slot = jnp.int32(0)
        for i in range(MAXP // N_HEAD):
            loc = locs[r, head_id + i * N_HEAD]
            mine = lax.shift_right_logical(loc, 9) == pool_id
            sel = jnp.where(mine, loc & (PAGES_DEV - 1), sel)
            slot = jnp.where(mine, head_id + i * N_HEAD, slot)
        length = lens[r]
        for u in range(PAGE // 2):
            two = wide[pl.ds(sel, 1), 2 * WIDTH * u : 2 * WIDTH * (u + 1)]
            for odd in range(2):
                t = 2 * u + odd
                token = pltpu.roll(two, WIDTH, 1) if odd else two
                extra = jnp.where(slot * PAGE + t < length, 0.0, BLOCKED)
                tail = jnp.where(lane < ROPE, token[:, KV:PAY], jnp.where(lane == ROPE, extra, 0.0))
                rows[r, t : t + 1, :KV] = token[:, :KV]
                rows[r, t : t + 1, KV:] = tail
        return carry

    lax.fori_loop(0, REQ, one_request, 0)
    out_ref[...] = rows[...].astype(BF)


def own_pages(place, cached_len, page_loc, latent_pool):
    return pl.pallas_call(
        pages_kernel,
        out_shape=jax.ShapeDtypeStruct((REQ, PAGE, PAY), BF),
        in_specs=[SMEM, SMEM, SMEM, VMEM],
        out_specs=VMEM,
        scratch_shapes=[
            pltpu.VMEM((PAGES_DEV, PAGE * WIDTH), F32),
            pltpu.VMEM((REQ, PAGE, PAY), F32),
        ],
        compiler_params=params(8),
        cost_estimate=cost(0, 1 << 20),
        name="own_pages",
    )(place, cached_len, page_loc, latent_pool)


def new_kernel(q_ref, lat_ref, w_ref, q_out, kv_out, rope_out):
    lane = lax.broadcasted_iota(jnp.int32, (NEW, 128), 1)
    for pair in range(HPD // 2):
        two = q_ref[:, 384 * pair : 384 * (pair + 1)].astype(F32)
        for odd in range(2):
            head = 2 * pair + odd
            one = pltpu.roll(two, NOPE + ROPE, 1) if odd else two
            tail = jnp.where(lane < ROPE, one[:, NOPE : NOPE + 128], jnp.where(lane == ROPE, 1.0, 0.0))
            q_out[:, 256 * head : 256 * head + 128] = one[:, :NOPE].astype(BF)
            q_out[:, 256 * head + 128 : 256 * head + 256] = tail.astype(BF)
    rope = jnp.concatenate([lat_ref[KV:, :].astype(F32), jnp.zeros((128 - ROPE, NEW), F32)], 0)
    rope_out[...] = rope.T.astype(BF)
    latent = lat_ref[:KV, :].astype(F32).T.astype(BF)
    kv_out[...] = jnp.dot(latent, w_ref[...], preferred_element_type=F32).astype(BF)


def new_tokens(queries, latent_t, w_ukv):
    return pl.pallas_call(
        new_kernel,
        out_shape=[
            jax.ShapeDtypeStruct((NEW, HPD * 256), BF),
            jax.ShapeDtypeStruct((NEW, HPD * 256), BF),
            jax.ShapeDtypeStruct((NEW, 128), BF),
        ],
        in_specs=[VMEM] * 3,
        out_specs=[VMEM] * 3,
        compiler_params=params(24),
        cost_estimate=cost(2 * NEW * KV * 1024, 4 << 20),
        name="new_tokens",
    )(queries, latent_t, w_ukv)


def turn_kernel(place, w_ref, keep_ref, give_ref, turned):
    width = 2 * SIDE * COLS
    for k in range(width // 256):
        turned[256 * k : 256 * (k + 1), :] = w_ref[:, 256 * k : 256 * (k + 1)].T
    head_id = place[1]
    core = head_id & 1
    x = lax.shift_right_logical(head_id, 1) & (SIDE - 1)
    for d in range(SIDE):
        at = ((x + d) & (SIDE - 1)) * 2
        keep_ref[d, 0] = turned[pl.ds(pl.multiple_of((at + core) * COLS, 32), COLS), :]
        give_ref[d, 0] = turned[pl.ds(pl.multiple_of((at + 1 - core) * COLS, 32), COLS), :]


def turned_weights(place, w_out):
    rows = HPD * VD
    part = jax.ShapeDtypeStruct((SIDE, SIDE, COLS, rows), BF)
    block = pl.BlockSpec((SIDE, 1, COLS, rows), lambda g, s: (0, g, 0, 0))
    return pl.pallas_call(
        turn_kernel,
        out_shape=[part, part],
        grid_spec=pltpu.PrefetchScalarGridSpec(
            num_scalar_prefetch=1,
            grid=(SIDE,),
            in_specs=[
                pl.BlockSpec(
                    (rows, 2 * SIDE * COLS),
                    lambda g, s: (0, (lax.shift_right_logical(s[1], 3) + g) & (SIDE - 1)),
                )
            ],
            out_specs=[block, block],
            scratch_shapes=[pltpu.VMEM((2 * SIDE * COLS, rows), BF)],
        ),
        compiler_params=params(24),
        cost_estimate=cost(0, 24 << 20),
        name="turned_weights",
    )(place, w_out)


def lift_kernel(count, *refs):
    w_ref = refs[count]
    kv_out, rope_out = refs[count + 1 :]
    for i in range(count):
        rows = refs[i].shape[0]
        kv_out[rows * i : rows * (i + 1), :] = jnp.dot(
            refs[i][:, :KV], w_ref[...], preferred_element_type=F32
        ).astype(BF)
        rope_out[rows * i : rows * (i + 1), :] = refs[i][:, KV:]


def lift(pieces, w_ukv):
    count = len(pieces)
    rows = count * pieces[0].shape[0]
    return pl.pallas_call(
        functools.partial(lift_kernel, count),
        out_shape=[
            jax.ShapeDtypeStruct((rows, HPD * 256), BF),
            jax.ShapeDtypeStruct((rows, 128), BF),
        ],
        in_specs=[VMEM] * (count + 1),
        out_specs=[VMEM] * 2,
        compiler_params=params(24),
        cost_estimate=cost(2 * rows * KV * 1024, rows * 4096),
        name="lift",
    )(*pieces, w_ukv)


def attend_kernel(half, groups, q_ref, *refs):
    q = q_ref[...]
    out_ref = refs[-1]
    scores, values = [], []
    for g in range(groups):
        kv = refs[2 * g][...]
        keys = jnp.concatenate([kv[:, :NOPE], refs[2 * g + 1][...]], 1)
        s = lax.dot_general(q, keys, NT, preferred_element_type=F32)
        if g == groups - 1:
            key = lax.broadcasted_iota(jnp.int32, s.shape, 1)
            row = lax.broadcasted_iota(jnp.int32, s.shape, 0) + half * HALF
            s = jnp.where(key <= row, s, BLOCKED)
        scores.append(s)
        values.append(jnp.concatenate([kv[:, NOPE:], jnp.ones((kv.shape[0], 128), BF)], 1))
    top = functools.reduce(jnp.maximum, [jnp.max(s, axis=1, keepdims=True) for s in scores])
    total = None
    for s, v in zip(scores, values):
        weight = jnp.exp2((s - top) * SCALE).astype(BF)
        part = jnp.dot(weight, v, preferred_element_type=F32)
        total = part if total is None else total + part
    out_ref[...] = (total[:, :VD] / total[:, VD:]).astype(BF)


def attend(half, q_ext, prefix, new):
    groups = len(prefix) + 1
    new_rows = HALF * (half + 1)
    specs, operands, keys = [], [], 0
    for kv, rope in prefix + [new]:
        rows = new_rows if kv is new[0] else kv.shape[0]
        keys += rows
        specs += [
            pl.BlockSpec((rows, 256), lambda h: (0, h)),
            pl.BlockSpec((rows, 128), lambda h: (0, 0)),
        ]
        operands += [kv, rope]
    return pl.pallas_call(
        functools.partial(attend_kernel, half, groups),
        out_shape=jax.ShapeDtypeStruct((HALF, HPD * VD), BF),
        grid=(HPD,),
        in_specs=[pl.BlockSpec((HALF, 256), lambda h: (half, h))] + specs,
        out_specs=pl.BlockSpec((HALF, VD), lambda h: (0, h)),
        compiler_params=params(32),
        cost_estimate=cost(HPD * HALF * keys * 1024, keys * 2048, HPD * HALF * keys),
        name="attend",
    )(q_ext, *operands)


def project_kernel(att_ref, other_ref, keep_ref, got_ref, out_ref):
    rows = keep_ref.shape[0] * keep_ref.shape[1] * COLS
    out = lax.dot_general(
        keep_ref[...].reshape(rows, HPD * VD), att_ref[...], NT, preferred_element_type=F32
    ) + lax.dot_general(
        got_ref[...].reshape(rows, HPD * VD), other_ref[...], NT, preferred_element_type=F32
    )
    out_ref[...] = out.reshape(1, rows // COLS, COLS, HALF).astype(BF)


def project(first_x, distances, att, other, keep, got):
    count = len(distances)

    def distance(g):
        if count == 1:
            return distances[0]
        return jnp.where(g == 2, 0, 1 + 2 * g)

    if first_x:
        spec = pl.BlockSpec((1, 2, COLS, HPD * VD), lambda g, k: (distance(g), k, 0, 0))
    else:
        spec = pl.BlockSpec((2, 1, COLS, HPD * VD), lambda g, k: (k, distance(g), 0, 0))
    whole = pl.BlockSpec((HALF, HPD * VD), lambda g, k: (0, 0))
    rows = count * SIDE * COLS
    return pl.pallas_call(
        project_kernel,
        out_shape=jax.ShapeDtypeStruct((count, SIDE, COLS, HALF), BF),
        grid=(count, 2),
        in_specs=[whole, whole, spec, spec],
        out_specs=pl.BlockSpec((1, 2, COLS, HALF), lambda g, k: (g, k, 0, 0)),
        compiler_params=params(16),
        cost_estimate=cost(2 * rows * 1024 * HALF, rows * 2560),
        name="project",
    )(att, other, keep, got)


def add(*terms):
    total = terms[0].astype(F32)
    for term in terms[1:]:
        total = total + term.astype(F32)
    return total.astype(BF)


def summed(first_x, att, other, keep, got):
    one, two = (along_x, along_y) if first_x else (along_y, along_x)
    far = project(first_x, (2,), att, other, keep, got)[0]
    low = send(far[:2], one(1))
    high = send(far[2:], one(-1))
    near = project(first_x, (1, 3, 0), att, other, keep, got)
    up = jnp.concatenate([add(near[0, :2], low), near[0, 2:]], 0)
    down = jnp.concatenate([near[1, :2], add(near[1, 2:], high)], 0)
    part = add(near[2], send(up, one(1)), send(down, one(-1)))
    return add(part[0], send(part[2], two(2)), send(part[1], two(1)), send(part[3], two(-1)))


def per_device(queries, new_latent, latent_pool, w_ukv, w_out, cached_len, page_loc):
    place = jnp.stack([lax.axis_index("pool"), lax.axis_index("head")]).astype(jnp.int32)
    outgoing = own_pages(place, cached_len, page_loc, latent_pool)
    arrived = lax.all_to_all(outgoing, "pool", split_axis=0, concat_axis=0, tiled=True)
    own = arrived.reshape(REQ * PAGE, PAY)
    keep, give = turned_weights(place, w_out)
    got = send(give, SWAP)
    q_ext, kv_new, rope_new = new_tokens(queries, new_latent.T, w_ukv)
    line = jnp.concatenate(
        [own, send(own, along_x(1)), send(own, along_x(-1)), send(own, along_x(2))], 0
    )
    plane = [send(line, along_y(2)), send(line, along_y(1)), send(line, along_y(-1))]
    near = lift([line, send(line, SWAP)], w_ukv)
    far = lift(plane + [send(piece, SWAP) for piece in plane], w_ukv)
    halves = []
    for half in range(2):
        att = attend(half, q_ext, [near, far], (kv_new, rope_new))
        halves.append(summed(half == 0, att, send(att, SWAP), keep, got))
    return jnp.concatenate(halves, 1).T


def solution(mesh):
    placed = (
        P("pool", "head"),
        P("pool", None),
        P(("pool", "head"), None),
        P(None, "head"),
        P("head", None),
        P(),
        P(),
    )
    return jax.shard_map(
        per_device, mesh=mesh, in_specs=placed, out_specs=P("pool", "head"), check_vma=False
    )
```

time: 284 us -> 116 us (0.41)
  waiting for transfers between devices: 141 us -> 32.1 us
  local copies, waits for them, and re-layouts: 53.7 us -> 3.29 us
  matrix products: 38.7 us -> 0 us
  Pallas kernels: 0 us -> 31.6 us
  starting transfers between devices: 8.61 us -> 30.9 us
  other arithmetic: 18.9 us -> 1.68 us
  blocking collectives: 0 us -> 15.6 us
  between operations: 13.6 us -> 0.37 us
  loops' own time: 8.08 us -> 0 us
    unnamed x3 -> x0, waiting for transfers between devices: 95.7 us -> none
    all_gather x1 -> x0, waiting for transfers between devices: 38.9 us -> none  [per_device(): portion = lax.all_gather(held_pages[:, None, :], 'head', axis=1, tiled=True)]
    dot_general x15 -> x0, matrix products: 38.7 us -> none  [the longest x1 10.2 us: per_device(): lax.dot_general(w_out, attended, (((0,), (1,)), ((), ())), preferred_elem...]
    ppermute x0 -> x27, waiting for transfers between devices: none -> 32.1 us  [send(): return lax.ppermute(value, 'head', perm)]
    pallas_call x0 -> x11, Pallas kernels: none -> 31.6 us  [the longest x2 14.6 us: attend(): pl.pallas_call(functools.partial(attend_kernel, half, groups), out_shape=...]
    ppermute x0 -> x27, starting transfers between devices: none -> 30.9 us  [send(): return lax.ppermute(value, 'head', perm)]
    unnamed x14, local copies, waits for them, and re-layouts: 18.9 us -> 3.11 us
    all_to_all x0 -> x1, blocking collectives: none -> 15.6 us  [per_device(): lax.all_to_all(outgoing, 'pool', split_axis=0, concat_axis=0, tiled=True)]
  transfers between devices with their start and end apart: 3 -> 27, of which waited for: 3 -> 10; matrix products, arithmetic and copies ran while one was open for 3% -> 1% of each run, Pallas kernels for 0% -> 24%
where the time goes in v1:
time: 116 us
  waiting for transfers between devices  32.1 us (28%)
  Pallas kernels  31.6 us (27%)
  starting transfers between devices  30.9 us (27%)
  blocking collectives  15.6 us (13%)
  local copies, waits for them, and re-layouts  3.29 us (3%)
  other arithmetic  1.68 us (1%)
    ppermute x27, waiting for transfers between devices, send(): return lax.ppermute(value, 'head', perm)  32.1 us
    ppermute x27, starting transfers between devices, send(): return lax.ppermute(value, 'head', perm)  30.9 us
    all_to_all x1, blocking collectives, per_device(): lax.all_to_all(outgoing, 'pool', split_axis=0, concat_axis=0, tiled=True)  15.6 us
    pallas_call x2, Pallas kernels, attend(): pl.pallas_call(functools.partial(attend_kernel, half, groups), out_shape=...  14.6 us
    pallas_call x4, Pallas kernels, project(): pl.pallas_call(project_kernel, out_shape=jax.ShapeDtypeStruct((count, SID...  7.68 us
    pallas_call x1, Pallas kernels, turned_weights(): pl.pallas_call(turn_kernel, out_shape=[part, part], grid_spec=pltpu.Prefe...  4.31 us
    unnamed x14, local copies, waits for them, and re-layouts  3.11 us
    pallas_call x2, Pallas kernels, lift(): pl.pallas_call(functools.partial(lift_kernel, count), out_shape=[jax.Shap...  2.51 us
  transfers between devices with their start and end apart: 27, of which 10 were waited for; matrix products, arithmetic and copies ran while one was open for 1% of the time, Pallas kernels for 24%

profile of v1, /device:TPU:32, one launch (start us, length us, event | category | flops | bytes accessed | tf_op | source)
XLA Modules:
  0.0 115.6 jit_solution(4381666274401892144)
XLA Ops:
  0.1 3.1 %copy-done = bf16[512,7168]{1,0:T(8,128)(2,1)S(1)} copy-done((bf16[512,7168]{1,0:T(8,128)(2,1)S(1)}, bf16[512,7168]{1,0:T(8,128)(2,1)}, u32[]{:S(2)}) %copy-start) | copy-done | bytes 7340056
  3.2 4.3 %turned_weights.1 = (bf16[4,4,224,512]{3,2,1,0:T(8,128)(2,1)S(1)}, bf16[4,4,224,512]{3,2,1,0:T(8,128)(2,1)S(1)}) custom-call(s32[2]{0:T(128)S(1)} %pad_add_fusion.place, bf16[512,7168]{1,0:T(8,128)(2,1)S(1)} %copy-done), custom_call_target="tpu_custom_call" | custom-call | bytes 25165824 | tf_op jit(solution)/shard_map/turned_weights/pallas_call | solution.py:167
  9.3 15.6 %all_to_all.5 = bf16[8,8,640]{2,1,0:T(8,128)(2,1)S(1)} all-to-all(bf16[8,8,640]{2,1,0:T(8,128)(2,1)S(1)} %own_pages.1), channel_id=1, replica_groups=mesh['pool'=8,'head'=32] {'pool'}, dimensions={0} | all-to-all | bytes 163840 | tf_op jit(solution)/shard_map/all_to_all | solution.py:321
  24.9 3.0 %collective-permute-start.2 = (bf16[64,640]{1,0:T(8,128)(2,1)S(1)}, bf16[64,640]{1,0:T(8,128)(2,1)S(1)}, u32[]{:S(2)}, u32[]{:S(2)}) collective-permute-start(bf16[64,640]{1,0:T(8,128)(2,1)S(1)} %bitcast.75), channel_id=1, source_target_pairs={{0,4},{1,5},{2,6},{3,7},{4,0},{5,1},{6,2},{7,3},{8,12},{9,13},{10,... | collective-permute-start | bytes 245768 | tf_op jit(solution)/shard_map/ppermute | solution.py:61
  29.9 1.8 %collective-permute-done.2 = bf16[64,640]{1,0:T(8,128)(2,1)S(1)} collective-permute-done((bf16[64,640]{1,0:T(8,128)(2,1)S(1)}, bf16[64,640]{1,0:T(8,128)(2,1)S(1)}, u32[]{:S(2)}, u32[]{:S(2)}) %collective-permute-start.2) | collective-permute-done | bytes 81952 | tf_op jit(solution)/shard_map/ppermute | solution.py:61
  32.3 2.4 %collective-permute-done = bf16[64,640]{1,0:T(8,128)(2,1)S(1)} collective-permute-done((bf16[64,640]{1,0:T(8,128)(2,1)S(1)}, bf16[64,640]{1,0:T(8,128)(2,1)S(1)}, u32[]{:S(2)}, u32[]{:S(2)}) %collective-permute-start) | collective-permute-done | bytes 81952 | tf_op jit(solution)/shard_map/ppermute | solution.py:61
  34.7 3.1 %collective-permute-start.6 = (bf16[256,640]{1,0:T(8,128)(2,1)S(1)}, bf16[256,640]{1,0:T(8,128)(2,1)S(1)}, u32[]{:S(2)}, u32[]{:S(2)}) collective-permute-start(bf16[256,640]{1,0:T(8,128)(2,1)S(1)} %pad_maximum_fusion.4.refs_0_), channel_id=1, source_target_pairs={{0,24},{1,25},{2,26},{3,27},{4,28},{5,29},{6,30},{7,31},{8,0},{9,1... | collective-permute-start | bytes 983048 | tf_op jit(solution)/shard_map/ppermute | solution.py:61
  37.8 2.2 %collective-permute-start.4 = (bf16[256,640]{1,0:T(8,128)(2,1)S(1)}, bf16[256,640]{1,0:T(8,128)(2,1)S(1)}, u32[]{:S(2)}, u32[]{:S(2)}) collective-permute-start(bf16[256,640]{1,0:T(8,128)(2,1)S(1)} %pad_maximum_fusion.4.refs_0_), channel_id=1, source_target_pairs={{0,16},{1,17},{2,18},{3,19},{4,20},{5,21},{6,22},{7,23},{8,24},{9,... | collective-permute-start | bytes 983048 | tf_op jit(solution)/shard_map/ppermute | solution.py:61
  40.0 9.5 %collective-permute-done.6.refs_2_ = bf16[256,640]{1,0:T(8,128)(2,1)S(1)} collective-permute-done((bf16[256,640]{1,0:T(8,128)(2,1)S(1)}, bf16[256,640]{1,0:T(8,128)(2,1)S(1)}, u32[]{:S(2)}, u32[]{:S(2)}) %collective-permute-start.6) | collective-permute-done | bytes 327712 | tf_op jit(solution)/shard_map/ppermute | solution.py:61
  49.5 3.4 %collective-permute-done.5.refs_1_ = bf16[256,640]{1,0:T(8,128)(2,1)S(1)} collective-permute-done((bf16[256,640]{1,0:T(8,128)(2,1)S(1)}, bf16[256,640]{1,0:T(8,128)(2,1)S(1)}, u32[]{:S(2)}, u32[]{:S(2)}) %collective-permute-start.5) | collective-permute-done | bytes 327712 | tf_op jit(solution)/shard_map/ppermute | solution.py:61
  55.0 1.8 %lift.3 = (bf16[1536,1024]{1,0:T(8,128)(2,1)S(1)}, bf16[1536,128]{1,0:T(8,128)(2,1)S(1)}) custom-call(bf16[256,640]{1,0:T(8,128)(2,1)S(1)} %collective-permute-done.4.refs_0_, bf16[256,640]{1,0:T(8,128)(2,1)S(1)} %collective-permute-done.5.refs_1_, bf16[256,640]{1,0:T(8,128)(2,1)S(1)} %collective-permute-done.6.refs_2_, ...), custom_call_target="tpu_custom_call" | custom-call | flops 1610612736 | bytes 6291456 | tf_op jit(solution)/shard_map/lift/pallas_call | solution.py:202
  56.8 7.6 %attend.3.att_ref = bf16[256,512]{1,0:T(8,128)(2,1)S(1)} custom-call(bf16[512,1024]{1,0:T(8,128)(2,1)S(1)} %get-tuple-element.14.q_ref, bf16[512,1024]{1,0:T(8,128)(2,1)S(1)} %get-tuple-element.15.refs_0_, bf16[512,128]{1,0:T(8,128)(2,1)S(1)} %get-tuple-element.16.refs_1_, bf16[1536,1024]{1,0:T(8,128)(2,1)S(1)} %get-tuple-element.17.refs_2_, ...), custom_call_target="tpu_custom_call" | custom-call | flops 2684354560 | bytes 5242880 | tf_op jit(solution)/shard_map/attend/pallas_call | solution.py:251
  64.7 7.0 %attend.2.att_ref = bf16[256,512]{1,0:T(8,128)(2,1)S(1)} custom-call(bf16[512,1024]{1,0:T(8,128)(2,1)S(1)} %get-tuple-element.14.q_ref, bf16[512,1024]{1,0:T(8,128)(2,1)S(1)} %get-tuple-element.15.refs_0_, bf16[512,128]{1,0:T(8,128)(2,1)S(1)} %get-tuple-element.16.refs_1_, bf16[1536,1024]{1,0:T(8,128)(2,1)S(1)} %get-tuple-element.17.refs_2_, ...), custom_call_target="tpu_custom_call" | custom-call | flops 2415919104 | bytes 4718592 | tf_op jit(solution)/shard_map/attend/pallas_call | solution.py:251
  73.3 3.2 %collective-permute-start.22 = (bf16[2,224,256]{2,1,0:T(8,128)(2,1)S(1)}, bf16[2,224,256]{2,1,0:T(8,128)(2,1)S(1)}, u32[]{:S(2)}, u32[]{:S(2)}) collective-permute-start(bf16[2,224,256]{2,1,0:T(8,128)(2,1)S(1)} %get-tuple-element.40), channel_id=1, source_target_pairs={{0,24},{1,25},{2,26},{3,27},{4,28},{5,29},{6,30},{7,31},{8,0},{9,1... | collective-permute-start | bytes 688136 | tf_op jit(solution)/shard_map/ppermute | solution.py:61
  77.8 3.0 %collective-permute-start.14 = (bf16[2,224,256]{2,1,0:T(8,128)(2,1)S(1)}, bf16[2,224,256]{2,1,0:T(8,128)(2,1)S(1)}, u32[]{:S(2)}, u32[]{:S(2)}) collective-permute-start(bf16[2,224,256]{2,1,0:T(8,128)(2,1)S(1)} %get-tuple-element.35), channel_id=1, source_target_pairs={{0,6},{1,7},{2,0},{3,1},{4,2},{5,3},{6,4},{7,5},{8,14},{9,15},{10,... | collective-permute-start | bytes 688136 | tf_op jit(solution)/shard_map/ppermute | solution.py:61
  80.8 3.1 %project.6 = bf16[3,4,224,256]{3,2,1,0:T(8,128)(2,1)S(1)} custom-call(bf16[256,512]{1,0:T(8,128)(2,1)S(1)} %attend.3.att_ref, bf16[256,512]{1,0:T(8,128)(2,1)S(1)} %collective-permute-done.19.other_ref, bf16[4,4,224,512]{3,2,1,0:T(8,128)(2,1)S(1)} %get-tuple-element.21.keep_ref, bf16[4,4,224,512]{3,2,1,0:T(8,128)(2,1)S(1)} %collective-permute-done.11.got_ref), custom_call_target="tpu_custom_call" | custom-call | flops 1409286144 | bytes 6881280 | tf_op jit(solution)/shard_map/project/pallas_call | solution.py:287
  84.0 2.7 %project.4 = bf16[3,4,224,256]{3,2,1,0:T(8,128)(2,1)S(1)} custom-call(bf16[256,512]{1,0:T(8,128)(2,1)S(1)} %attend.2.att_ref, bf16[256,512]{1,0:T(8,128)(2,1)S(1)} %collective-permute-done.10.other_ref, bf16[4,4,224,512]{3,2,1,0:T(8,128)(2,1)S(1)} %get-tuple-element.21.keep_ref, bf16[4,4,224,512]{3,2,1,0:T(8,128)(2,1)S(1)} %collective-permute-done.11.got_ref), custom_call_target="tpu_custom_call" | custom-call | flops 1409286144 | bytes 6881280 | tf_op jit(solution)/shard_map/project/pallas_call | solution.py:287
  86.9 2.4 %collective-permute-start.15 = (bf16[4,224,256]{2,1,0:T(8,128)(2,1)S(1)}, bf16[4,224,256]{2,1,0:T(8,128)(2,1)S(1)}, u32[]{:S(2)}, u32[]{:S(2)}) collective-permute-start(bf16[4,224,256]{2,1,0:T(8,128)(2,1)S(1)} %pad_maximum_fusion.1), channel_id=1, source_target_pairs={{0,6},{1,7},{2,0},{3,1},{4,2},{5,3},{6,4},{7,5},{8,14},{9,15},{10,... | collective-permute-start | bytes 1376264 | tf_op jit(solution)/shard_map/ppermute | solution.py:61
  90.0 1.8 %collective-permute-start.21 = (bf16[4,224,256]{2,1,0:T(8,128)(2,1)S(1)}, bf16[4,224,256]{2,1,0:T(8,128)(2,1)S(1)}, u32[]{:S(2)}, u32[]{:S(2)}) collective-permute-start(bf16[4,224,256]{2,1,0:T(8,128)(2,1)S(1)} %pad_maximum_fusion.2), channel_id=1, source_target_pairs={{0,8},{1,9},{2,10},{3,11},{4,12},{5,13},{6,14},{7,15},{8,16},{9,17... | collective-permute-start | bytes 1376264 | tf_op jit(solution)/shard_map/ppermute | solution.py:61
  91.8 6.8 %collective-permute-done.15 = bf16[4,224,256]{2,1,0:T(8,128)(2,1)S(1)} collective-permute-done((bf16[4,224,256]{2,1,0:T(8,128)(2,1)S(1)}, bf16[4,224,256]{2,1,0:T(8,128)(2,1)S(1)}, u32[]{:S(2)}, u32[]{:S(2)}) %collective-permute-start.15) | collective-permute-done | bytes 458784 | tf_op jit(solution)/shard_map/ppermute | solution.py:61
  98.6 2.5 %collective-permute-done.13 = bf16[4,224,256]{2,1,0:T(8,128)(2,1)S(1)} collective-permute-done((bf16[4,224,256]{2,1,0:T(8,128)(2,1)S(1)}, bf16[4,224,256]{2,1,0:T(8,128)(2,1)S(1)}, u32[]{:S(2)}, u32[]{:S(2)}) %collective-permute-start.13) | collective-permute-done | bytes 458784 | tf_op jit(solution)/shard_map/ppermute | solution.py:61
  101.4 2.1 %collective-permute-start.18 = (bf16[224,256]{1,0:T(8,128)(2,1)S(1)}, bf16[224,256]{1,0:T(8,128)(2,1)S(1)}, u32[]{:S(2)}, u32[]{:S(2)}) collective-permute-start(bf16[224,256]{1,0:T(8,128)(2,1)S(1)} %get-tuple-element.32), channel_id=1, source_target_pairs={{0,24},{1,25},{2,26},{3,27},{4,28},{5,29},{6,30},{7,31},{8,0},{9,1... | collective-permute-start | bytes 344072 | tf_op jit(solution)/shard_map/ppermute | solution.py:61
  103.8 5.0 %collective-permute-start.26 = (bf16[224,256]{1,0:T(8,128)(2,1)S(1)}, bf16[224,256]{1,0:T(8,128)(2,1)S(1)}, u32[]{:S(2)}, u32[]{:S(2)}) collective-permute-start(bf16[224,256]{1,0:T(8,128)(2,1)S(1)} %get-tuple-element.37), channel_id=1, source_target_pairs={{0,6},{1,7},{2,0},{3,1},{4,2},{5,3},{6,4},{7,5},{8,14},{9,15},{10,... | collective-permute-start | bytes 344072 | tf_op jit(solution)/shard_map/ppermute | solution.py:61
  110.1 3.5 %collective-permute-done.26 = bf16[224,256]{1,0:T(8,128)(2,1)S(1)} collective-permute-done((bf16[224,256]{1,0:T(8,128)(2,1)S(1)}, bf16[224,256]{1,0:T(8,128)(2,1)S(1)}, u32[]{:S(2)}, u32[]{:S(2)}) %collective-permute-start.26) | collective-permute-done | bytes 114720 | tf_op jit(solution)/shard_map/ppermute | solution.py:61
  (75 shorter events, 14.5 us)
Async XLA Ops:
  7.5 64.7 %collective-permute-start.11 = (bf16[4,4,224,512]{3,2,1,0:T(8,128)(2,1)S(1)}, bf16[4,4,224,512]{3,2,1,0:T(8,128)(2,1)S(1)}, u32[]{:S(2)}, u32[]{:S(2)}) collective-permute-start(bf16[4,4,224,512]{3,2,1,0:T(8,128)(2,1)S(1)} %get-tuple-element.22), channel_id=1, source_target_pairs={{0,1},{1,0},{2,3},{3,2},{4,5},{5,4},{6,7},{7,6},{8,9},{9,8},{10,11... | collective-permute-start | bytes 11010056 | tf_op jit(solution)/shard_map/ppermute | solution.py:61
  24.9 6.9 %collective-permute-start.2 = (bf16[64,640]{1,0:T(8,128)(2,1)S(1)}, bf16[64,640]{1,0:T(8,128)(2,1)S(1)}, u32[]{:S(2)}, u32[]{:S(2)}) collective-permute-start(bf16[64,640]{1,0:T(8,128)(2,1)S(1)} %bitcast.75), channel_id=1, source_target_pairs={{0,4},{1,5},{2,6},{3,7},{4,0},{5,1},{6,2},{7,3},{8,12},{9,13},{10,... | collective-permute-start | bytes 245768 | tf_op jit(solution)/shard_map/ppermute | solution.py:61
  29.0 5.7 %collective-permute-start = (bf16[64,640]{1,0:T(8,128)(2,1)S(1)}, bf16[64,640]{1,0:T(8,128)(2,1)S(1)}, u32[]{:S(2)}, u32[]{:S(2)}) collective-permute-start(bf16[64,640]{1,0:T(8,128)(2,1)S(1)} %bitcast.77), channel_id=1, source_target_pairs={{0,2},{1,3},{2,4},{3,5},{4,6},{5,7},{6,0},{7,1},{8,10},{9,11},{10,... | collective-permute-start | bytes 245768 | tf_op jit(solution)/shard_map/ppermute | solution.py:61
  34.7 14.8 %collective-permute-start.6 = (bf16[256,640]{1,0:T(8,128)(2,1)S(1)}, bf16[256,640]{1,0:T(8,128)(2,1)S(1)}, u32[]{:S(2)}, u32[]{:S(2)}) collective-permute-start(bf16[256,640]{1,0:T(8,128)(2,1)S(1)} %pad_maximum_fusion.4.refs_0_), channel_id=1, source_target_pairs={{0,24},{1,25},{2,26},{3,27},{4,28},{5,29},{6,30},{7,31},{8,0},{9,1... | collective-permute-start | bytes 983048 | tf_op jit(solution)/shard_map/ppermute | solution.py:61
  37.8 15.1 %collective-permute-start.5 = (bf16[256,640]{1,0:T(8,128)(2,1)S(1)}, bf16[256,640]{1,0:T(8,128)(2,1)S(1)}, u32[]{:S(2)}, u32[]{:S(2)}) collective-permute-start(bf16[256,640]{1,0:T(8,128)(2,1)S(1)} %pad_maximum_fusion.4.refs_0_), channel_id=1, source_target_pairs={{0,8},{1,9},{2,10},{3,11},{4,12},{5,13},{6,14},{7,15},{8,16},{9,17... | collective-permute-start | bytes 983048 | tf_op jit(solution)/shard_map/ppermute | solution.py:61
  37.8 15.1 %collective-permute-start.4 = (bf16[256,640]{1,0:T(8,128)(2,1)S(1)}, bf16[256,640]{1,0:T(8,128)(2,1)S(1)}, u32[]{:S(2)}, u32[]{:S(2)}) collective-permute-start(bf16[256,640]{1,0:T(8,128)(2,1)S(1)} %pad_maximum_fusion.4.refs_0_), channel_id=1, source_target_pairs={{0,16},{1,17},{2,18},{3,19},{4,20},{5,21},{6,22},{7,23},{8,24},{9,... | collective-permute-start | bytes 983048 | tf_op jit(solution)/shard_map/ppermute | solution.py:61
  40.0 14.3 %collective-permute-start.3 = (bf16[256,640]{1,0:T(8,128)(2,1)S(1)}, bf16[256,640]{1,0:T(8,128)(2,1)S(1)}, u32[]{:S(2)}, u32[]{:S(2)}) collective-permute-start(bf16[256,640]{1,0:T(8,128)(2,1)S(1)} %pad_maximum_fusion.4.refs_0_), channel_id=1, source_target_pairs={{0,1},{1,0},{2,3},{3,2},{4,5},{5,4},{6,7},{7,6},{8,9},{9,8},{10,11... | collective-permute-start | bytes 983048 | tf_op jit(solution)/shard_map/ppermute | solution.py:61
  49.5 5.5 %collective-permute-start.9 = (bf16[256,640]{1,0:T(8,128)(2,1)S(1)}, bf16[256,640]{1,0:T(8,128)(2,1)S(1)}, u32[]{:S(2)}, u32[]{:S(2)}) collective-permute-start(bf16[256,640]{1,0:T(8,128)(2,1)S(1)} %collective-permute-done.6.refs_2_), channel_id=1, source_target_pairs={{0,1},{1,0},{2,3},{3,2},{4,5},{5,4},{6,7},{7,6},{8,9},{9,8},{10,11... | collective-permute-start | bytes 983048 | tf_op jit(solution)/shard_map/ppermute | solution.py:61
  64.5 7.7 %collective-permute-start.19 = (bf16[256,512]{1,0:T(8,128)(2,1)S(1)}, bf16[256,512]{1,0:T(8,128)(2,1)S(1)}, u32[]{:S(2)}, u32[]{:S(2)}) collective-permute-start(bf16[256,512]{1,0:T(8,128)(2,1)S(1)} %attend.3.att_ref), channel_id=1, source_target_pairs={{0,1},{1,0},{2,3},{3,2},{4,5},{5,4},{6,7},{7,6},{8,9},{9,8},{10,11... | collective-permute-start | bytes 786440 | tf_op jit(solution)/shard_map/ppermute | solution.py:61
  71.7 4.9 %collective-permute-start.10 = (bf16[256,512]{1,0:T(8,128)(2,1)S(1)}, bf16[256,512]{1,0:T(8,128)(2,1)S(1)}, u32[]{:S(2)}, u32[]{:S(2)}) collective-permute-start(bf16[256,512]{1,0:T(8,128)(2,1)S(1)} %attend.2.att_ref), channel_id=1, source_target_pairs={{0,1},{1,0},{2,3},{3,2},{4,5},{5,4},{6,7},{7,6},{8,9},{9,8},{10,11... | collective-permute-start | bytes 786440 | tf_op jit(solution)/shard_map/ppermute | solution.py:61
  73.2 16.1 %collective-permute-start.20 = (bf16[2,224,256]{2,1,0:T(8,128)(2,1)S(1)}, bf16[2,224,256]{2,1,0:T(8,128)(2,1)S(1)}, u32[]{:S(2)}, u32[]{:S(2)}) collective-permute-start(bf16[2,224,256]{2,1,0:T(8,128)(2,1)S(1)} %get-tuple-element.39), channel_id=1, source_target_pairs={{0,8},{1,9},{2,10},{3,11},{4,12},{5,13},{6,14},{7,15},{8,16},{9,17... | collective-permute-start | bytes 688136 | tf_op jit(solution)/shard_map/ppermute | solution.py:61
  73.3 16.1 %collective-permute-start.22 = (bf16[2,224,256]{2,1,0:T(8,128)(2,1)S(1)}, bf16[2,224,256]{2,1,0:T(8,128)(2,1)S(1)}, u32[]{:S(2)}, u32[]{:S(2)}) collective-permute-start(bf16[2,224,256]{2,1,0:T(8,128)(2,1)S(1)} %get-tuple-element.40), channel_id=1, source_target_pairs={{0,24},{1,25},{2,26},{3,27},{4,28},{5,29},{6,30},{7,31},{8,0},{9,1... | collective-permute-start | bytes 688136 | tf_op jit(solution)/shard_map/ppermute | solution.py:61
  77.5 9.2 %collective-permute-start.12 = (bf16[2,224,256]{2,1,0:T(8,128)(2,1)S(1)}, bf16[2,224,256]{2,1,0:T(8,128)(2,1)S(1)}, u32[]{:S(2)}, u32[]{:S(2)}) collective-permute-start(bf16[2,224,256]{2,1,0:T(8,128)(2,1)S(1)} %get-tuple-element.34), channel_id=1, source_target_pairs={{0,2},{1,3},{2,4},{3,5},{4,6},{5,7},{6,0},{7,1},{8,10},{9,11},{10,... | collective-permute-start | bytes 688136 | tf_op jit(solution)/shard_map/ppermute | solution.py:61
  77.8 8.8 %collective-permute-start.14 = (bf16[2,224,256]{2,1,0:T(8,128)(2,1)S(1)}, bf16[2,224,256]{2,1,0:T(8,128)(2,1)S(1)}, u32[]{:S(2)}, u32[]{:S(2)}) collective-permute-start(bf16[2,224,256]{2,1,0:T(8,128)(2,1)S(1)} %get-tuple-element.35), channel_id=1, source_target_pairs={{0,6},{1,7},{2,0},{3,1},{4,2},{5,3},{6,4},{7,5},{8,14},{9,15},{10,... | collective-permute-start | bytes 688136 | tf_op jit(solution)/shard_map/ppermute | solution.py:61
  86.9 11.7 %collective-permute-start.15 = (bf16[4,224,256]{2,1,0:T(8,128)(2,1)S(1)}, bf16[4,224,256]{2,1,0:T(8,128)(2,1)S(1)}, u32[]{:S(2)}, u32[]{:S(2)}) collective-permute-start(bf16[4,224,256]{2,1,0:T(8,128)(2,1)S(1)} %pad_maximum_fusion.1), channel_id=1, source_target_pairs={{0,6},{1,7},{2,0},{3,1},{4,2},{5,3},{6,4},{7,5},{8,14},{9,15},{10,... | collective-permute-start | bytes 1376264 | tf_op jit(solution)/shard_map/ppermute | solution.py:61
  89.3 11.8 %collective-permute-start.13 = (bf16[4,224,256]{2,1,0:T(8,128)(2,1)S(1)}, bf16[4,224,256]{2,1,0:T(8,128)(2,1)S(1)}, u32[]{:S(2)}, u32[]{:S(2)}) collective-permute-start(bf16[4,224,256]{2,1,0:T(8,128)(2,1)S(1)} %pad_maximum_fusion), channel_id=1, source_target_pairs={{0,2},{1,3},{2,4},{3,5},{4,6},{5,7},{6,0},{7,1},{8,10},{9,11},{10,... | collective-permute-start | bytes 1376264 | tf_op jit(solution)/shard_map/ppermute | solution.py:61
  89.6 13.9 %collective-permute-start.23 = (bf16[4,224,256]{2,1,0:T(8,128)(2,1)S(1)}, bf16[4,224,256]{2,1,0:T(8,128)(2,1)S(1)}, u32[]{:S(2)}, u32[]{:S(2)}) collective-permute-start(bf16[4,224,256]{2,1,0:T(8,128)(2,1)S(1)} %pad_maximum_fusion.3), channel_id=1, source_target_pairs={{0,24},{1,25},{2,26},{3,27},{4,28},{5,29},{6,30},{7,31},{8,0},{9,1... | collective-permute-start | bytes 1376264 | tf_op jit(solution)/shard_map/ppermute | solution.py:61
  90.0 13.5 %collective-permute-start.21 = (bf16[4,224,256]{2,1,0:T(8,128)(2,1)S(1)}, bf16[4,224,256]{2,1,0:T(8,128)(2,1)S(1)}, u32[]{:S(2)}, u32[]{:S(2)}) collective-permute-start(bf16[4,224,256]{2,1,0:T(8,128)(2,1)S(1)} %pad_maximum_fusion.2), channel_id=1, source_target_pairs={{0,8},{1,9},{2,10},{3,11},{4,12},{5,13},{6,14},{7,15},{8,16},{9,17... | collective-permute-start | bytes 1376264 | tf_op jit(solution)/shard_map/ppermute | solution.py:61
  101.3 7.5 %collective-permute-start.16 = (bf16[224,256]{1,0:T(8,128)(2,1)S(1)}, bf16[224,256]{1,0:T(8,128)(2,1)S(1)}, u32[]{:S(2)}, u32[]{:S(2)}) collective-permute-start(bf16[224,256]{1,0:T(8,128)(2,1)S(1)} %get-tuple-element.31), channel_id=1, source_target_pairs={{0,16},{1,17},{2,18},{3,19},{4,20},{5,21},{6,22},{7,23},{8,24},{9,... | collective-permute-start | bytes 344072 | tf_op jit(solution)/shard_map/ppermute | solution.py:61
  101.4 8.2 %collective-permute-start.18 = (bf16[224,256]{1,0:T(8,128)(2,1)S(1)}, bf16[224,256]{1,0:T(8,128)(2,1)S(1)}, u32[]{:S(2)}, u32[]{:S(2)}) collective-permute-start(bf16[224,256]{1,0:T(8,128)(2,1)S(1)} %get-tuple-element.32), channel_id=1, source_target_pairs={{0,24},{1,25},{2,26},{3,27},{4,28},{5,29},{6,30},{7,31},{8,0},{9,1... | collective-permute-start | bytes 344072 | tf_op jit(solution)/shard_map/ppermute | solution.py:61
  103.5 6.1 %collective-permute-start.17 = (bf16[224,256]{1,0:T(8,128)(2,1)S(1)}, bf16[224,256]{1,0:T(8,128)(2,1)S(1)}, u32[]{:S(2)}, u32[]{:S(2)}) collective-permute-start(bf16[224,256]{1,0:T(8,128)(2,1)S(1)} %get-tuple-element.33), channel_id=1, source_target_pairs={{0,8},{1,9},{2,10},{3,11},{4,12},{5,13},{6,14},{7,15},{8,16},{9,17... | collective-permute-start | bytes 344072 | tf_op jit(solution)/shard_map/ppermute | solution.py:61
  103.7 6.4 %collective-permute-start.24 = (bf16[224,256]{1,0:T(8,128)(2,1)S(1)}, bf16[224,256]{1,0:T(8,128)(2,1)S(1)}, u32[]{:S(2)}, u32[]{:S(2)}) collective-permute-start(bf16[224,256]{1,0:T(8,128)(2,1)S(1)} %get-tuple-element.36), channel_id=1, source_target_pairs={{0,4},{1,5},{2,6},{3,7},{4,0},{5,1},{6,2},{7,3},{8,12},{9,13},{10,... | collective-permute-start | bytes 344072 | tf_op jit(solution)/shard_map/ppermute | solution.py:61
  103.8 9.8 %collective-permute-start.26 = (bf16[224,256]{1,0:T(8,128)(2,1)S(1)}, bf16[224,256]{1,0:T(8,128)(2,1)S(1)}, u32[]{:S(2)}, u32[]{:S(2)}) collective-permute-start(bf16[224,256]{1,0:T(8,128)(2,1)S(1)} %get-tuple-element.37), channel_id=1, source_target_pairs={{0,6},{1,7},{2,0},{3,1},{4,2},{5,3},{6,4},{7,5},{8,14},{9,15},{10,... | collective-permute-start | bytes 344072 | tf_op jit(solution)/shard_map/ppermute | solution.py:61
  108.8 6.0 %collective-permute-start.25 = (bf16[224,256]{1,0:T(8,128)(2,1)S(1)}, bf16[224,256]{1,0:T(8,128)(2,1)S(1)}, u32[]{:S(2)}, u32[]{:S(2)}) collective-permute-start(bf16[224,256]{1,0:T(8,128)(2,1)S(1)} %get-tuple-element.38), channel_id=1, source_target_pairs={{0,2},{1,3},{2,4},{3,5},{4,6},{5,7},{6,0},{7,1},{8,10},{9,11},{10,... | collective-permute-start | bytes 344072 | tf_op jit(solution)/shard_map/ppermute | solution.py:61
  (10 other events, 171.6 us)

commit v2 on v1

v2 whole, which is shorter than its diff:
```python
import functools

import jax
import jax.numpy as jnp
from jax import lax
from jax.experimental import pallas as pl
from jax.experimental.pallas import tpu as pltpu
from jax.sharding import PartitionSpec as P

NOPE = 128
ROPE = 64
VD = 128
KV = 512
NEW = 512
PAGE = 8
MAXP = 256
HPD = 4
REQ = 8
N_HEAD = 32
PAGES_DEV = 16
D = 7168
COLS = D // N_HEAD
WIDTH = KV + ROPE
PAY = KV + 128
HALF = NEW // 2
SIDE = 4
BLOCKED = -1e30
SCALE = (NOPE + ROPE) ** -0.5 * 1.4426950408889634
BF = jnp.bfloat16
F32 = jnp.float32
NT = (((1,), (1,)), ((), ()))
VMEM = pl.BlockSpec(memory_space=pltpu.VMEM)
SMEM = pl.BlockSpec(memory_space=pltpu.SMEM)


PLANE = ("y_hi", "y_lo", "x_hi", "x_lo", "core")


def plane_perm(move):
    def index(y, x, c):
        return ((y % SIDE) * SIDE + x % SIDE) * 2 + c

    return [
        (index(y, x, c), index(*move(y, x, c)))
        for y in range(SIDE)
        for x in range(SIDE)
        for c in range(2)
    ]


SWAP = plane_perm(lambda y, x, c: (y, x, 1 - c))


def send_first(value, d):
    perm = plane_perm(lambda y, x, c: (y + d * c, x + d * (1 - c), c))
    return lax.ppermute(value, PLANE, perm)


def send_second(value, d):
    perm = plane_perm(lambda y, x, c: (y + d * (1 - c), x + d * c, c))
    return lax.ppermute(value, PLANE, perm)


def swap(value):
    return lax.ppermute(value, PLANE, SWAP)


def in_hbm(value):
    return pltpu.with_memory_space_constraint(value, pltpu.HBM)


def params(mib):
    return pltpu.CompilerParams(vmem_limit_bytes=mib << 20)


SHORT = pl.CostEstimate(flops=0, bytes_accessed=1024, transcendentals=0)
LONG = pl.CostEstimate(flops=10**11, bytes_accessed=1024, transcendentals=0)


def pages_kernel(place, lens_in, locs_in, pool_in, out_ref, lens, locs, pool_ref, wide, rows, sems):
    copies = [
        pltpu.make_async_copy(source, target, sems.at[k])
        for k, (source, target) in enumerate([(lens_in, lens), (locs_in, locs), (pool_in, pool_ref)])
    ]
    for copy in copies:
        copy.start()
    for copy in copies:
        copy.wait()
    wide[...] = pool_ref[...].astype(F32)
    pool_id = place[0]
    head_id = place[1]
    lane = lax.broadcasted_iota(jnp.int32, (1, 128), 1)

    def one_request(r, carry):
        sel = jnp.int32(0)
        slot = jnp.int32(0)
        for i in range(MAXP // N_HEAD):
            loc = locs[r, head_id + i * N_HEAD]
            mine = lax.shift_right_logical(loc, 9) == pool_id
            sel = jnp.where(mine, loc & (PAGES_DEV - 1), sel)
            slot = jnp.where(mine, head_id + i * N_HEAD, slot)
        length = lens[r]
        for u in range(PAGE // 2):
            two = wide[pl.ds(sel, 1), 2 * WIDTH * u : 2 * WIDTH * (u + 1)]
            for odd in range(2):
                t = 2 * u + odd
                token = pltpu.roll(two, WIDTH, 1) if odd else two
                extra = jnp.where(slot * PAGE + t < length, 0.0, BLOCKED)
                tail = jnp.where(lane < ROPE, token[:, KV:PAY], jnp.where(lane == ROPE, extra, 0.0))
                rows[r, t : t + 1, :KV] = token[:, :KV]
                rows[r, t : t + 1, KV:] = tail
        return carry

    lax.fori_loop(0, REQ, one_request, 0)
    out_ref[...] = rows[...].astype(BF)


def own_pages(place, cached_len, page_loc, latent_pool):
    return pl.pallas_call(
        pages_kernel,
        out_shape=jax.ShapeDtypeStruct((REQ, PAGE, PAY), BF),
        in_specs=[SMEM] + [pl.BlockSpec(memory_space=pltpu.HBM)] * 3,
        out_specs=VMEM,
        scratch_shapes=[
            pltpu.SMEM((REQ,), jnp.int32),
            pltpu.SMEM((REQ, MAXP), jnp.int32),
            pltpu.VMEM((PAGES_DEV, PAGE * WIDTH), BF),
            pltpu.VMEM((PAGES_DEV, PAGE * WIDTH), F32),
            pltpu.VMEM((REQ, PAGE, PAY), F32),
            pltpu.SemaphoreType.DMA((3,)),
        ],
        compiler_params=params(8),
        cost_estimate=SHORT,
        name="own_pages",
    )(place, in_hbm(cached_len), in_hbm(page_loc), in_hbm(latent_pool))


def new_kernel(q_ref, lat_ref, w_ref, q_out, kv_out, rope_out):
    lane = lax.broadcasted_iota(jnp.int32, (NEW, 128), 1)
    for pair in range(HPD // 2):
        two = q_ref[:, 384 * pair : 384 * (pair + 1)].astype(F32)
        for odd in range(2):
            head = 2 * pair + odd
            one = pltpu.roll(two, NOPE + ROPE, 1) if odd else two
            tail = jnp.where(lane < ROPE, one[:, NOPE : NOPE + 128], jnp.where(lane == ROPE, 1.0, 0.0))
            q_out[:, 256 * head : 256 * head + 128] = one[:, :NOPE].astype(BF)
            q_out[:, 256 * head + 128 : 256 * head + 256] = tail.astype(BF)
    rope = jnp.concatenate([lat_ref[KV:, :].astype(F32), jnp.zeros((128 - ROPE, NEW), F32)], 0)
    rope_out[...] = rope.T.astype(BF)
    latent = lat_ref[:KV, :].astype(F32).T.astype(BF)
    kv_out[...] = jnp.dot(latent, w_ref[...], preferred_element_type=F32).astype(BF)


def new_tokens(queries, latent_t, w_ukv):
    return pl.pallas_call(
        new_kernel,
        out_shape=[
            jax.ShapeDtypeStruct((NEW, HPD * 256), BF),
            jax.ShapeDtypeStruct((NEW, HPD * 256), BF),
            jax.ShapeDtypeStruct((NEW, 128), BF),
        ],
        in_specs=[VMEM] * 3,
        out_specs=[VMEM] * 3,
        compiler_params=params(24),
        cost_estimate=SHORT,
        name="new_tokens",
    )(in_hbm(queries), in_hbm(latent_t), w_ukv)


def turn_kernel(place, w_ref, keep_ref, give_ref, flag_ref, turned):
    flag_ref[...] = jnp.zeros_like(flag_ref)
    width = 2 * SIDE * COLS
    for k in range(width // 256):
        turned[256 * k : 256 * (k + 1), :] = w_ref[:, 256 * k : 256 * (k + 1)].T
    head_id = place[1]
    core = head_id & 1
    x = lax.shift_right_logical(head_id, 1) & (SIDE - 1)
    dy = pl.program_id(0)
    for dx in range(SIDE):
        at = ((x + dx) & (SIDE - 1)) * 2
        mine = (jnp.where(core == 0, dx, dy), jnp.where(core == 0, dy + 3, dx + 3) & (SIDE - 1))
        theirs = (jnp.where(core == 0, dy, dx), jnp.where(core == 0, dx + 3, dy + 3) & (SIDE - 1))
        keep_ref[mine] = turned[pl.ds(pl.multiple_of((at + core) * COLS, 32), COLS), :]
        give_ref[theirs] = turned[pl.ds(pl.multiple_of((at + 1 - core) * COLS, 32), COLS), :]


def turned_weights(place, w_out):
    rows = HPD * VD
    part = jax.ShapeDtypeStruct((SIDE, SIDE, COLS, rows), BF)
    whole = pl.BlockSpec((SIDE, SIDE, COLS, rows), lambda g, s: (0, 0, 0, 0))

    def column(g, s):
        return (0, (lax.shift_right_logical(s[1], 3) + g) & (SIDE - 1))

    return pl.pallas_call(
        turn_kernel,
        out_shape=[part, part, jax.ShapeDtypeStruct((8, 128), F32)],
        grid_spec=pltpu.PrefetchScalarGridSpec(
            num_scalar_prefetch=1,
            grid=(SIDE,),
            in_specs=[pl.BlockSpec((rows, 2 * SIDE * COLS), column)],
            out_specs=[whole, whole, pl.BlockSpec((8, 128), lambda g, s: (0, 0))],
            scratch_shapes=[pltpu.VMEM((2 * SIDE * COLS, rows), BF)],
        ),
        compiler_params=params(28),
        cost_estimate=SHORT,
        name="turned_weights",
    )(place, in_hbm(w_out))


def lift_kernel(count, *refs):
    w_ref = refs[count]
    kv_out, rope_out = refs[count + 1 :]
    for i in range(count):
        rows = refs[i].shape[0]
        kv_out[rows * i : rows * (i + 1), :] = jnp.dot(
            refs[i][:, :KV], w_ref[...], preferred_element_type=F32
        ).astype(BF)
        rope_out[rows * i : rows * (i + 1), :] = refs[i][:, KV:]


def lift(pieces, w_ukv):
    count = len(pieces)
    rows = count * pieces[0].shape[0]
    return pl.pallas_call(
        functools.partial(lift_kernel, count),
        out_shape=[
            jax.ShapeDtypeStruct((rows, HPD * 256), BF),
            jax.ShapeDtypeStruct((rows, 128), BF),
        ],
        in_specs=[VMEM] * (count + 1),
        out_specs=[VMEM] * 2,
        compiler_params=params(24),
        cost_estimate=SHORT,
        name="lift",
    )(*pieces, w_ukv)


def group_scores(q, kv, rope):
    keys = jnp.concatenate([kv[:, :NOPE], rope], 1)
    return lax.dot_general(q, keys, NT, preferred_element_type=F32)


def group_sum(weight, kv):
    values = jnp.concatenate([kv[:, NOPE:], jnp.ones((kv.shape[0], 128), BF)], 1)
    return jnp.dot(weight, values, preferred_element_type=F32)


LARGE = 2.0**60


def weights_of(s, top):
    return jnp.exp2((s - top) * SCALE).astype(BF)


def row_max(s):
    return jnp.max(s, axis=1, keepdims=True)


def new_scores(half, q, kv_new, rope_new):
    count = HALF * (half + 1)
    n = group_scores(q, kv_new[:count, :], rope_new[:count, :])
    key = lax.broadcasted_iota(jnp.int32, n.shape, 1)
    row = lax.broadcasted_iota(jnp.int32, n.shape, 0) + half * HALF
    return jnp.where(key <= row, n, BLOCKED)


def near_kernel(q_ref, kv_ref, rope_ref, kv_new, rope_new, sum_ref, top_ref):
    def work(exact):
        for half in range(2):
            rows = slice(half * HALF, (half + 1) * HALF)
            count = HALF * (half + 1)
            q = q_ref[rows, :]
            n = new_scores(half, q, kv_new, rope_new)
            top = row_max(n)
            s = group_scores(q, kv_ref[...], rope_ref[...])
            if exact:
                top = jnp.maximum(top, row_max(s))
            sum_ref[rows, :] = group_sum(weights_of(s, top), kv_ref[...]) + group_sum(
                weights_of(n, top), kv_new[:count, :]
            )
            top_ref[rows, :] = jnp.broadcast_to(top, (HALF, 128))

    work(False)
    fine = jnp.max(sum_ref[:, VD:]) < LARGE

    @pl.when(jnp.logical_not(fine))
    def _():
        work(True)


def attend_near(q_ext, kv, rope, kv_new, rope_new):
    head = pl.BlockSpec((NEW, 256), lambda h: (0, h))
    whole = pl.BlockSpec((NEW, 128), lambda h: (0, 0))
    return pl.pallas_call(
        near_kernel,
        out_shape=[
            jax.ShapeDtypeStruct((NEW, HPD * 256), F32),
            jax.ShapeDtypeStruct((NEW, HPD * 128), F32),
        ],
        grid=(HPD,),
        in_specs=[head, head, whole, head, whole],
        out_specs=[head, pl.BlockSpec((NEW, 128), lambda h: (0, h))],
        compiler_params=params(16),
        cost_estimate=SHORT,
        name="attend_near",
    )(q_ext, kv, rope, kv_new, rope_new)


def far_kernel(groups, q_ref, sum_ref, top_ref, order_ref, *refs):
    out_ref, total_ref = refs[-2:]
    old = top_ref[:, :1]

    def work(exact):
        q = q_ref[...]
        scores = [group_scores(q, refs[2 * g][...], refs[2 * g + 1][...]) for g in range(groups)]
        total = sum_ref[...]
        top = old
        if exact:
            top = functools.reduce(jnp.maximum, [row_max(s) for s in scores] + [old])
            total = total * jnp.exp2((old - top) * SCALE)
        for g, s in enumerate(scores):
            total = total + group_sum(weights_of(s, top), refs[2 * g][...])
        total_ref[...] = total

    work(False)
    fine = jnp.max(total_ref[:, VD:]) < LARGE

    @pl.when(jnp.logical_not(fine))
    def _():
        work(True)

    out_ref[...] = (total_ref[:, :VD] / total_ref[:, VD:]).astype(BF)


def attend_far(q_ext, sums, tops, order, far):
    specs, operands, keys = [], [], 0
    for kv, rope in far:
        rows = kv.shape[0]
        keys += rows
        specs += [
            pl.BlockSpec((rows, 256), lambda h: (0, h)),
            pl.BlockSpec((rows, 128), lambda h: (0, 0)),
        ]
        operands += [kv, rope]
    head = pl.BlockSpec((NEW, 256), lambda h: (0, h))
    return pl.pallas_call(
        functools.partial(far_kernel, len(far)),
        out_shape=jax.ShapeDtypeStruct((NEW, HPD * VD), BF),
        grid=(HPD,),
        in_specs=[head, head, pl.BlockSpec((NEW, 128), lambda h: (0, h)), pl.BlockSpec((8, 128), lambda h: (0, 0))] + specs,
        out_specs=pl.BlockSpec((NEW, VD), lambda h: (0, h)),
        scratch_shapes=[pltpu.VMEM((NEW, 256), F32)],
        compiler_params=params(20),
        cost_estimate=LONG,
        name="attend_far",
    )(q_ext, sums, tops, order, *operands)


def project_kernel(att_ref, other_ref, keep_ref, got_ref, out_ref):
    rows = 2 * COLS
    out = lax.dot_general(
        keep_ref[...].reshape(rows, HPD * VD), att_ref[...], NT, preferred_element_type=F32
    ) + lax.dot_general(
        got_ref[...].reshape(rows, HPD * VD), other_ref[...], NT, preferred_element_type=F32
    )
    out_ref[...] = out.reshape(2, COLS, NEW).astype(BF)


def project(a, pair, att, other, keep, got):
    spec = pl.BlockSpec((1, 2, COLS, HPD * VD), lambda i: (a, pair, 0, 0))
    whole = pl.BlockSpec((NEW, HPD * VD), lambda i: (0, 0))
    rows = 2 * COLS
    return pl.pallas_call(
        project_kernel,
        out_shape=jax.ShapeDtypeStruct((2, COLS, NEW), BF),
        grid=(1,),
        in_specs=[whole, whole, spec, spec],
        out_specs=pl.BlockSpec((2, COLS, NEW), lambda i: (0, 0, 0)),
        compiler_params=params(16),
        cost_estimate=SHORT,
        name="project",
    )(att, other, keep, got)


def add(*terms):
    total = terms[0].astype(F32)
    for term in terms[1:]:
        total = total + term.astype(F32)
    return total.astype(BF)


def per_device(queries, new_latent, latent_pool, w_ukv, w_out, cached_len, page_loc):
    place = jnp.stack([lax.axis_index("pool"), lax.axis_index(PLANE)]).astype(jnp.int32)
    outgoing = own_pages(place, cached_len, page_loc, latent_pool)
    arrived = lax.all_to_all(outgoing, "pool", split_axis=0, concat_axis=0, tiled=True)
    own = arrived.reshape(REQ * PAGE, PAY)
    own, new_latent = lax.optimization_barrier((own, new_latent))
    q_ext, kv_new, rope_new = new_tokens(queries, new_latent.T, w_ukv)
    line = [own, send_first(own, 2), send_first(own, 1), send_first(own, -1)]
    *line, kv_new = lax.optimization_barrier((*line, kv_new))
    line, place = lax.optimization_barrier((jnp.concatenate(line, 0), place))
    pieces = [send_second(line, d) for d in (2, 1, -1)]
    near = lift([line, swap(line)], w_ukv)
    sums, tops = attend_near(q_ext, *near, kv_new, rope_new)
    keep, give, order = turned_weights(place, w_out)
    got = swap(give)
    *pieces, sums, order = lax.optimization_barrier((*pieces, sums, order))
    far = [lift(pieces, w_ukv), lift([swap(piece) for piece in pieces], w_ukv)]
    att = attend_far(q_ext, sums, tops, order, far)
    other = swap(att)
    sent = [
        [send_first(project(a, pair, att, other, keep, got), d) for a, d in ((2, 2), (1, 1), (3, -1))]
        for pair in range(2)
    ]
    one = add(project(0, 0, att, other, keep, got), *sent[0])
    one = [send_second(one[1], 2), send_second(one[0], 1)]
    *sent[1], one[0], one[1] = lax.optimization_barrier((*sent[1], *one))
    two = add(project(0, 1, att, other, keep, got), *sent[1])
    out = add(two[1], *one, send_second(two[0], -1))
    return out.T


def solution(mesh):
    fine = jax.sharding.Mesh(
        mesh.devices.reshape(mesh.shape["pool"], 2, 2, 2, 2, 2), ("pool",) + PLANE
    )
    placed = (
        P("pool", PLANE),
        P("pool", None),
        P(("pool",) + PLANE, None),
        P(None, PLANE),
        P(PLANE, None),
        P(),
        P(),
    )
    return jax.shard_map(
        per_device, mesh=fine, in_specs=placed, out_specs=P("pool", PLANE), check_vma=False
    )
```

time: 116 us -> 100 us (0.86)
  waiting for transfers between devices: 32.1 us -> 20.1 us
  starting transfers between devices: 30.9 us -> 25.7 us
  Pallas kernels: 31.6 us -> 34.3 us
  local copies, waits for them, and re-layouts: 3.29 us -> 1.28 us
    ppermute x27 -> x21, waiting for transfers between devices: 32.1 us -> 20.1 us  [the longest x9 13.1 us: send_first(): return lax.ppermute(value, PLANE, perm)]
    ppermute x27 -> x21, starting transfers between devices: 30.9 us -> 25.7 us  [the longest x9 14.6 us: send_first(): return lax.ppermute(value, PLANE, perm)]
    unnamed x14 -> x4, local copies, waits for them, and re-layouts: 3.11 us -> 1.23 us
    pallas_call x1, Pallas kernels: 0.84 us -> 2.13 us  [new_tokens(): pl.pallas_call(new_kernel, out_shape=[jax.ShapeDtypeStruct((NEW, HPD * 25...]
    pallas_call x7 -> x11, Pallas kernels: 26.6 us -> 27 us  [the longest x1 9.54 us: attend_near(): pl.pallas_call(near_kernel, out_shape=[jax.ShapeDtypeStruct((NEW, HPD * 2...]
    pallas_call x2 -> x3, Pallas kernels: 2.51 us -> 2.67 us  [lift(): pl.pallas_call(functools.partial(lift_kernel, count), out_shape=[jax.Shap...]
  transfers between devices with their start and end apart: 27 -> 21, of which waited for: 10 -> 8; matrix products, arithmetic and copies ran while one was open for 1% -> 0% of each run, Pallas kernels for 24% -> 32%
where the time goes in v2:
time: 100 us; the launch traced here: 98.4 us
  Pallas kernels  34.3 us (34%)
  starting transfers between devices  25.7 us (26%)
  waiting for transfers between devices  20.1 us (20%)
  blocking collectives  15.5 us (16%)
  other arithmetic  1.39 us (1%)
  local copies, waits for them, and re-layouts  1.28 us (1%)
    all_to_all x1, blocking collectives, per_device(): lax.all_to_all(outgoing, 'pool', split_axis=0, concat_axis=0, tiled=True)  15.5 us
    ppermute x9, starting transfers between devices, send_first(): return lax.ppermute(value, PLANE, perm)  14.6 us
    ppermute x9, waiting for transfers between devices, send_first(): return lax.ppermute(value, PLANE, perm)  13.1 us
    ppermute x6, starting transfers between devices, send_second(): return lax.ppermute(value, PLANE, perm)  9.7 us
    pallas_call x1, Pallas kernels, attend_near(): pl.pallas_call(near_kernel, out_shape=[jax.ShapeDtypeStruct((NEW, HPD * 2...  9.54 us
    pallas_call x1, Pallas kernels, attend_far(): pl.pallas_call(functools.partial(far_kernel, len(far)), out_shape=jax.Sha...  6.19 us
    pallas_call x1, Pallas kernels, turned_weights(): pl.pallas_call(turn_kernel, out_shape=[part, part, jax.ShapeDtypeStruct((...  5.93 us
    pallas_call x8, Pallas kernels, project(): pl.pallas_call(project_kernel, out_shape=jax.ShapeDtypeStruct((2, COLS, N...  5.35 us
  transfers between devices with their start and end apart: 21, of which 8 were waited for; matrix products, arithmetic and copies ran while one was open for 0% of the time, Pallas kernels for 32%

profile of v2, /device:TPU:32, one launch (start us, length us, event | category | flops | bytes accessed | tf_op | source)
XLA Modules:
  0.0 98.4 jit_solution(1456452815806618739)
XLA Ops:
  0.1 2.5 %own_pages.1 = bf16[8,8,640]{2,1,0:T(8,128)(2,1)S(1)} custom-call(s32[2]{0:T(128)S(1)} %pad_add_fusion.place, s32[8]{0:T(128)} %lens_in.1, s32[8,256]{1,0:T(8,128)} %locs_in.1, bf16[16,4608]{1,0:T(8,128)(2,1)} %pool_in.1), custom_call_target="tpu_custom_call" | custom-call | bytes 1024 | tf_op jit(solution)/shard_map/own_pages/pallas_call | solution.py:119
  2.5 15.5 %all_to_all.5 = bf16[8,8,640]{2,1,0:T(8,128)(2,1)S(1)} all-to-all(bf16[8,8,640]{2,1,0:T(8,128)(2,1)S(1)} %own_pages.1), channel_id=1, replica_groups=mesh['pool'=8,'y_hi'=2,'y_lo'=2,'x_hi'=2,'x_lo'=2,'core'=2] {'pool'}, dimensions={0} | all-to-all | bytes 163840 | tf_op jit(solution)/shard_map/all_to_all | solution.py:396
  18.0 2.8 %collective-permute-start.2 = (bf16[64,640]{1,0:T(8,128)(2,1)S(1)}, bf16[64,640]{1,0:T(8,128)(2,1)S(1)}, u32[]{:S(2)}, u32[]{:S(2)}) collective-permute-start(bf16[64,640]{1,0:T(8,128)(2,1)S(1)} %bitcast.18), channel_id=1, source_target_pairs={{0,6},{1,25},{2,0},{3,27},{4,2},{5,29},{6,4},{7,31},{8,14},{9,1},{... | collective-permute-start | bytes 245768 | tf_op jit(solution)/shard_map/ppermute | solution.py:56
  20.8 2.3 %collective-permute-start = (bf16[64,640]{1,0:T(8,128)(2,1)S(1)}, bf16[64,640]{1,0:T(8,128)(2,1)S(1)}, u32[]{:S(2)}, u32[]{:S(2)}) collective-permute-start(bf16[64,640]{1,0:T(8,128)(2,1)S(1)} %bitcast.20), channel_id=1, source_target_pairs={{0,4},{1,17},{2,6},{3,19},{4,0},{5,21},{6,2},{7,23},{8,12},{9,25},... | collective-permute-start | bytes 245768 | tf_op jit(solution)/shard_map/ppermute | solution.py:56
  23.1 1.2 %copy-done = bf16[512,1024]{1,0:T(8,128)(2,1)S(1)} copy-done((bf16[512,1024]{1,0:T(8,128)(2,1)S(1)}, bf16[512,1024]{1,0:T(8,128)(2,1)}, u32[]{:S(2)}) %copy-start) | copy-done | bytes 1048600
  24.3 2.1 %new_tokens.1 = (bf16[512,1024]{1,0:T(8,128)(2,1)S(1)}, bf16[512,1024]{1,0:T(8,128)(2,1)S(1)}, bf16[512,128]{1,0:T(8,128)(2,1)S(1)}) custom-call(bf16[512,768]{1,0:T(8,128)(2,1)} %q_ref.1, bf16[576,512]{1,0:T(8,128)(2,1)} %bitcast.17, bf16[512,1024]{1,0:T(8,128)(2,1)S(1)} %copy-done), custom_call_target="tpu_custom_call" | custom-call | bytes 1024 | tf_op jit(solution)/shard_map/new_tokens/pallas_call | solution.py:155
  27.4 3.1 %collective-permute-start.5 = (bf16[256,640]{1,0:T(8,128)(2,1)S(1)}, bf16[256,640]{1,0:T(8,128)(2,1)S(1)}, u32[]{:S(2)}, u32[]{:S(2)}) collective-permute-start(bf16[256,640]{1,0:T(8,128)(2,1)S(1)} %pad_maximum_fusion.refs_0_), channel_id=1, source_target_pairs={{0,24},{1,7},{2,26},{3,1},{4,28},{5,3},{6,30},{7,5},{8,0},{9,15},{... | collective-permute-start | bytes 983048 | tf_op jit(solution)/shard_map/ppermute | solution.py:61
  30.5 2.2 %collective-permute-start.3 = (bf16[256,640]{1,0:T(8,128)(2,1)S(1)}, bf16[256,640]{1,0:T(8,128)(2,1)S(1)}, u32[]{:S(2)}, u32[]{:S(2)}) collective-permute-start(bf16[256,640]{1,0:T(8,128)(2,1)S(1)} %pad_maximum_fusion.refs_0_), channel_id=1, source_target_pairs={{0,16},{1,5},{2,18},{3,7},{4,20},{5,1},{6,22},{7,3},{8,24},{9,13},... | collective-permute-start | bytes 983048 | tf_op jit(solution)/shard_map/ppermute | solution.py:61
  32.7 5.9 %turned_weights.1 = (bf16[4,4,224,512]{3,2,1,0:T(8,128)(2,1)S(1)}, bf16[4,4,224,512]{3,2,1,0:T(8,128)(2,1)S(1)}, f32[8,128]{1,0:T(8,128)S(1)}) custom-call(s32[2]{0:T(128)S(1)} %pad_add_fusion.place, bf16[512,7168]{1,0:T(8,128)(2,1)} %w_ref.3), custom_call_target="tpu_custom_call" | custom-call | bytes 1024 | tf_op jit(solution)/shard_map/turned_weights/pallas_call | solution.py:195
  39.4 9.5 %attend_near.1 = (f32[512,1024]{1,0:T(8,128)S(1)}, f32[512,512]{1,0:T(8,128)S(1)}) custom-call(bf16[512,1024]{1,0:T(8,128)(2,1)S(1)} %get-tuple-element.39.q_ref, bf16[512,1024]{1,0:T(8,128)(2,1)S(1)} %get-tuple-element.47.kv_ref, bf16[512,128]{1,0:T(8,128)(2,1)S(1)} %get-tuple-element.48.rope_ref, bf16[512,1024]{1,0:T(8,128)(2,1)S(1)} %get-tuple-element.49.kv_new, ...), custom_call_target="tpu_custom_call" | custom-call | bytes 1024 | tf_op jit(solution)/shard_map/attend_near/pallas_call | solution.py:295
  51.7 1.0 lift.5
  52.7 6.2 %attend_far.1.att_ref = bf16[512,512]{1,0:T(8,128)(2,1)S(1)} custom-call(bf16[512,1024]{1,0:T(8,128)(2,1)S(1)} %get-tuple-element.39.q_ref, f32[512,1024]{1,0:T(8,128)S(1)} %get-tuple-element.54.sum_ref, f32[512,512]{1,0:T(8,128)S(1)} %get-tuple-element.55.top_ref, f32[8,128]{1,0:T(8,128)S(1)} %get-tuple-element.56.order_ref, ...), custom_call_target="tpu_custom_call" | custom-call | flops 99999997952 | bytes 1024 | tf_op jit(solution)/shard_map/attend_far/pallas_call | solution.py:347
  59.1 1.8 %collective-permute-done.10.other_ref = bf16[512,512]{1,0:T(8,128)(2,1)S(1)} collective-permute-done((bf16[512,512]{1,0:T(8,128)(2,1)S(1)}, bf16[512,512]{1,0:T(8,128)(2,1)S(1)}, u32[]{:S(2)}, u32[]{:S(2)}) %collective-permute-start.10) | collective-permute-done | bytes 524320 | tf_op jit(solution)/shard_map/ppermute | solution.py:65
  61.5 1.8 %collective-permute-start.15 = (bf16[2,224,512]{2,1,0:T(8,128)(2,1)S(1)}, bf16[2,224,512]{2,1,0:T(8,128)(2,1)S(1)}, u32[]{:S(2)}, u32[]{:S(2)}) collective-permute-start(bf16[2,224,512]{2,1,0:T(8,128)(2,1)S(1)} %project.13), channel_id=1, source_target_pairs={{0,4},{1,17},{2,6},{3,19},{4,0},{5,21},{6,2},{7,23},{8,12},{9,25},... | collective-permute-start | bytes 1376264 | tf_op jit(solution)/shard_map/ppermute | solution.py:56
  64.0 1.9 %collective-permute-start.16 = (bf16[2,224,512]{2,1,0:T(8,128)(2,1)S(1)}, bf16[2,224,512]{2,1,0:T(8,128)(2,1)S(1)}, u32[]{:S(2)}, u32[]{:S(2)}) collective-permute-start(bf16[2,224,512]{2,1,0:T(8,128)(2,1)S(1)} %project.14), channel_id=1, source_target_pairs={{0,2},{1,9},{2,4},{3,11},{4,6},{5,13},{6,0},{7,15},{8,10},{9,17},{... | collective-permute-start | bytes 1376264 | tf_op jit(solution)/shard_map/ppermute | solution.py:56
  66.5 1.5 %collective-permute-start.17 = (bf16[2,224,512]{2,1,0:T(8,128)(2,1)S(1)}, bf16[2,224,512]{2,1,0:T(8,128)(2,1)S(1)}, u32[]{:S(2)}, u32[]{:S(2)}) collective-permute-start(bf16[2,224,512]{2,1,0:T(8,128)(2,1)S(1)} %project.15), channel_id=1, source_target_pairs={{0,6},{1,25},{2,0},{3,27},{4,2},{5,29},{6,4},{7,31},{8,14},{9,1},{... | collective-permute-start | bytes 1376264 | tf_op jit(solution)/shard_map/ppermute | solution.py:56
  70.1 1.0 %collective-permute-start.13 = (bf16[2,224,512]{2,1,0:T(8,128)(2,1)S(1)}, bf16[2,224,512]{2,1,0:T(8,128)(2,1)S(1)}, u32[]{:S(2)}, u32[]{:S(2)}) collective-permute-start(bf16[2,224,512]{2,1,0:T(8,128)(2,1)S(1)} %project.10), channel_id=1, source_target_pairs={{0,2},{1,9},{2,4},{3,11},{4,6},{5,13},{6,0},{7,15},{8,10},{9,17},{... | collective-permute-start | bytes 1376264 | tf_op jit(solution)/shard_map/ppermute | solution.py:56
  72.5 2.6 %collective-permute-start.14 = (bf16[2,224,512]{2,1,0:T(8,128)(2,1)S(1)}, bf16[2,224,512]{2,1,0:T(8,128)(2,1)S(1)}, u32[]{:S(2)}, u32[]{:S(2)}) collective-permute-start(bf16[2,224,512]{2,1,0:T(8,128)(2,1)S(1)} %project.11), channel_id=1, source_target_pairs={{0,6},{1,25},{2,0},{3,27},{4,2},{5,29},{6,4},{7,31},{8,14},{9,1},{... | collective-permute-start | bytes 1376264 | tf_op jit(solution)/shard_map/ppermute | solution.py:56
  75.1 1.4 %collective-permute-done.16 = bf16[2,224,512]{2,1,0:T(8,128)(2,1)S(1)} collective-permute-done((bf16[2,224,512]{2,1,0:T(8,128)(2,1)S(1)}, bf16[2,224,512]{2,1,0:T(8,128)(2,1)S(1)}, u32[]{:S(2)}, u32[]{:S(2)}) %collective-permute-start.16) | collective-permute-done | bytes 458784 | tf_op jit(solution)/shard_map/ppermute | solution.py:56
  76.8 2.0 %collective-permute-start.19 = (bf16[224,512]{1,0:T(8,128)(2,1)S(1)}, bf16[224,512]{1,0:T(8,128)(2,1)S(1)}, u32[]{:S(2)}, u32[]{:S(2)}) collective-permute-start(bf16[224,512]{1,0:T(8,128)(2,1)S(1)} %get-tuple-element.71), channel_id=1, source_target_pairs={{0,8},{1,3},{2,10},{3,5},{4,12},{5,7},{6,14},{7,1},{8,16},{9,11},{... | collective-permute-start | bytes 688136 | tf_op jit(solution)/shard_map/ppermute | solution.py:61
  80.4 1.7 %collective-permute-done.12 = bf16[2,224,512]{2,1,0:T(8,128)(2,1)S(1)} collective-permute-done((bf16[2,224,512]{2,1,0:T(8,128)(2,1)S(1)}, bf16[2,224,512]{2,1,0:T(8,128)(2,1)S(1)}, u32[]{:S(2)}, u32[]{:S(2)}) %collective-permute-start.12) | collective-permute-done | bytes 458784 | tf_op jit(solution)/shard_map/ppermute | solution.py:56
  82.1 9.1 %collective-permute-done.13 = bf16[2,224,512]{2,1,0:T(8,128)(2,1)S(1)} collective-permute-done((bf16[2,224,512]{2,1,0:T(8,128)(2,1)S(1)}, bf16[2,224,512]{2,1,0:T(8,128)(2,1)S(1)}, u32[]{:S(2)}, u32[]{:S(2)}) %collective-permute-start.13) | collective-permute-done | bytes 458784 | tf_op jit(solution)/shard_map/ppermute | solution.py:56
  91.5 1.5 %collective-permute-start.20 = (bf16[224,512]{1,0:T(8,128)(2,1)S(1)}, bf16[224,512]{1,0:T(8,128)(2,1)S(1)}, u32[]{:S(2)}, u32[]{:S(2)}) collective-permute-start(bf16[224,512]{1,0:T(8,128)(2,1)S(1)} %slice_bitcast_fusion), channel_id=1, source_target_pairs={{0,24},{1,7},{2,26},{3,1},{4,28},{5,3},{6,30},{7,5},{8,0},{9,15},{... | collective-permute-start | bytes 688136 | tf_op jit(solution)/shard_map/ppermute | solution.py:61
  93.0 4.6 %collective-permute-done.20 = bf16[224,512]{1,0:T(8,128)(2,1)S(1)} collective-permute-done((bf16[224,512]{1,0:T(8,128)(2,1)S(1)}, bf16[224,512]{1,0:T(8,128)(2,1)S(1)}, u32[]{:S(2)}, u32[]{:S(2)}) %collective-permute-start.20) | collective-permute-done | bytes 229408 | tf_op jit(solution)/shard_map/ppermute | solution.py:61
  (46 shorter events, 13.0 us)
Async XLA Ops:
  18.0 8.4 %collective-permute-start.2 = (bf16[64,640]{1,0:T(8,128)(2,1)S(1)}, bf16[64,640]{1,0:T(8,128)(2,1)S(1)}, u32[]{:S(2)}, u32[]{:S(2)}) collective-permute-start(bf16[64,640]{1,0:T(8,128)(2,1)S(1)} %bitcast.18), channel_id=1, source_target_pairs={{0,6},{1,25},{2,0},{3,27},{4,2},{5,29},{6,4},{7,31},{8,14},{9,1},{... | collective-permute-start | bytes 245768 | tf_op jit(solution)/shard_map/ppermute | solution.py:56
  20.8 6.5 %collective-permute-start.1 = (bf16[64,640]{1,0:T(8,128)(2,1)S(1)}, bf16[64,640]{1,0:T(8,128)(2,1)S(1)}, u32[]{:S(2)}, u32[]{:S(2)}) collective-permute-start(bf16[64,640]{1,0:T(8,128)(2,1)S(1)} %bitcast.19), channel_id=1, source_target_pairs={{0,2},{1,9},{2,4},{3,11},{4,6},{5,13},{6,0},{7,15},{8,10},{9,17},{... | collective-permute-start | bytes 245768 | tf_op jit(solution)/shard_map/ppermute | solution.py:56
  20.8 6.5 %collective-permute-start = (bf16[64,640]{1,0:T(8,128)(2,1)S(1)}, bf16[64,640]{1,0:T(8,128)(2,1)S(1)}, u32[]{:S(2)}, u32[]{:S(2)}) collective-permute-start(bf16[64,640]{1,0:T(8,128)(2,1)S(1)} %bitcast.20), channel_id=1, source_target_pairs={{0,4},{1,17},{2,6},{3,19},{4,0},{5,21},{6,2},{7,23},{8,12},{9,25},... | collective-permute-start | bytes 245768 | tf_op jit(solution)/shard_map/ppermute | solution.py:56
  23.1 1.2 %copy-start = (bf16[512,1024]{1,0:T(8,128)(2,1)S(1)}, bf16[512,1024]{1,0:T(8,128)(2,1)}, u32[]{:S(2)}) copy-start(bf16[512,1024]{1,0:T(8,128)(2,1)} %refs_3_.3) | copy-start | bytes 3145732
  27.3 11.4 %copy-start.1 = (bf16[512,1024]{1,0:T(8,128)(2,1)S(1)}, bf16[512,1024]{1,0:T(8,128)(2,1)}, u32[]{:S(2)}) copy-start(bf16[512,1024]{1,0:T(8,128)(2,1)} %refs_3_.3) | copy-start | bytes 3145732
  27.3 11.3 %collective-permute-start.6 = (bf16[256,640]{1,0:T(8,128)(2,1)S(1)}, bf16[256,640]{1,0:T(8,128)(2,1)S(1)}, u32[]{:S(2)}, u32[]{:S(2)}) collective-permute-start(bf16[256,640]{1,0:T(8,128)(2,1)S(1)} %pad_maximum_fusion.refs_0_), channel_id=1, source_target_pairs={{0,1},{1,0},{2,3},{3,2},{4,5},{5,4},{6,7},{7,6},{8,9},{9,8},{10,11... | collective-permute-start | bytes 983048 | tf_op jit(solution)/shard_map/ppermute | solution.py:65
  27.4 21.5 %collective-permute-start.5 = (bf16[256,640]{1,0:T(8,128)(2,1)S(1)}, bf16[256,640]{1,0:T(8,128)(2,1)S(1)}, u32[]{:S(2)}, u32[]{:S(2)}) collective-permute-start(bf16[256,640]{1,0:T(8,128)(2,1)S(1)} %pad_maximum_fusion.refs_0_), channel_id=1, source_target_pairs={{0,24},{1,7},{2,26},{3,1},{4,28},{5,3},{6,30},{7,5},{8,0},{9,15},{... | collective-permute-start | bytes 983048 | tf_op jit(solution)/shard_map/ppermute | solution.py:61
  30.5 18.4 %collective-permute-start.4 = (bf16[256,640]{1,0:T(8,128)(2,1)S(1)}, bf16[256,640]{1,0:T(8,128)(2,1)S(1)}, u32[]{:S(2)}, u32[]{:S(2)}) collective-permute-start(bf16[256,640]{1,0:T(8,128)(2,1)S(1)} %pad_maximum_fusion.refs_0_), channel_id=1, source_target_pairs={{0,8},{1,3},{2,10},{3,5},{4,12},{5,7},{6,14},{7,1},{8,16},{9,11},{... | collective-permute-start | bytes 983048 | tf_op jit(solution)/shard_map/ppermute | solution.py:61
  30.5 18.5 %collective-permute-start.3 = (bf16[256,640]{1,0:T(8,128)(2,1)S(1)}, bf16[256,640]{1,0:T(8,128)(2,1)S(1)}, u32[]{:S(2)}, u32[]{:S(2)}) collective-permute-start(bf16[256,640]{1,0:T(8,128)(2,1)S(1)} %pad_maximum_fusion.refs_0_), channel_id=1, source_target_pairs={{0,16},{1,5},{2,18},{3,7},{4,20},{5,1},{6,22},{7,3},{8,24},{9,13},... | collective-permute-start | bytes 983048 | tf_op jit(solution)/shard_map/ppermute | solution.py:61
  49.0 2.1 %collective-permute-start.7 = (bf16[256,640]{1,0:T(8,128)(2,1)S(1)}, bf16[256,640]{1,0:T(8,128)(2,1)S(1)}, u32[]{:S(2)}, u32[]{:S(2)}) collective-permute-start(bf16[256,640]{1,0:T(8,128)(2,1)S(1)} %collective-permute-done.3.refs_0_), channel_id=1, source_target_pairs={{0,1},{1,0},{2,3},{3,2},{4,5},{5,4},{6,7},{7,6},{8,9},{9,8},{10,11... | collective-permute-start | bytes 983048 | tf_op jit(solution)/shard_map/ppermute | solution.py:65
  49.1 2.1 %collective-permute-start.8 = (bf16[256,640]{1,0:T(8,128)(2,1)S(1)}, bf16[256,640]{1,0:T(8,128)(2,1)S(1)}, u32[]{:S(2)}, u32[]{:S(2)}) collective-permute-start(bf16[256,640]{1,0:T(8,128)(2,1)S(1)} %collective-permute-done.4.refs_1_), channel_id=1, source_target_pairs={{0,1},{1,0},{2,3},{3,2},{4,5},{5,4},{6,7},{7,6},{8,9},{9,8},{10,11... | collective-permute-start | bytes 983048 | tf_op jit(solution)/shard_map/ppermute | solution.py:65
  49.6 2.1 %collective-permute-start.9 = (bf16[256,640]{1,0:T(8,128)(2,1)S(1)}, bf16[256,640]{1,0:T(8,128)(2,1)S(1)}, u32[]{:S(2)}, u32[]{:S(2)}) collective-permute-start(bf16[256,640]{1,0:T(8,128)(2,1)S(1)} %collective-permute-done.5.refs_2_), channel_id=1, source_target_pairs={{0,1},{1,0},{2,3},{3,2},{4,5},{5,4},{6,7},{7,6},{8,9},{9,8},{10,11... | collective-permute-start | bytes 983048 | tf_op jit(solution)/shard_map/ppermute | solution.py:65
  49.7 11.1 %collective-permute-start.11 = (bf16[4,4,224,512]{3,2,1,0:T(8,128)(2,1)S(1)}, bf16[4,4,224,512]{3,2,1,0:T(8,128)(2,1)S(1)}, u32[]{:S(2)}, u32[]{:S(2)}) collective-permute-start(bf16[4,4,224,512]{3,2,1,0:T(8,128)(2,1)S(1)} %get-tuple-element.65), channel_id=1, source_target_pairs={{0,1},{1,0},{2,3},{3,2},{4,5},{5,4},{6,7},{7,6},{8,9},{9,8},{10,11... | collective-permute-start | bytes 11010056 | tf_op jit(solution)/shard_map/ppermute | solution.py:65
  58.8 2.0 %collective-permute-start.10 = (bf16[512,512]{1,0:T(8,128)(2,1)S(1)}, bf16[512,512]{1,0:T(8,128)(2,1)S(1)}, u32[]{:S(2)}, u32[]{:S(2)}) collective-permute-start(bf16[512,512]{1,0:T(8,128)(2,1)S(1)} %attend_far.1.att_ref), channel_id=1, source_target_pairs={{0,1},{1,0},{2,3},{3,2},{4,5},{5,4},{6,7},{7,6},{8,9},{9,8},{10,11... | collective-permute-start | bytes 1572872 | tf_op jit(solution)/shard_map/ppermute | solution.py:65
  61.5 11.0 %collective-permute-start.15 = (bf16[2,224,512]{2,1,0:T(8,128)(2,1)S(1)}, bf16[2,224,512]{2,1,0:T(8,128)(2,1)S(1)}, u32[]{:S(2)}, u32[]{:S(2)}) collective-permute-start(bf16[2,224,512]{2,1,0:T(8,128)(2,1)S(1)} %project.13), channel_id=1, source_target_pairs={{0,4},{1,17},{2,6},{3,19},{4,0},{5,21},{6,2},{7,23},{8,12},{9,25},... | collective-permute-start | bytes 1376264 | tf_op jit(solution)/shard_map/ppermute | solution.py:56
  64.0 12.5 %collective-permute-start.16 = (bf16[2,224,512]{2,1,0:T(8,128)(2,1)S(1)}, bf16[2,224,512]{2,1,0:T(8,128)(2,1)S(1)}, u32[]{:S(2)}, u32[]{:S(2)}) collective-permute-start(bf16[2,224,512]{2,1,0:T(8,128)(2,1)S(1)} %project.14), channel_id=1, source_target_pairs={{0,2},{1,9},{2,4},{3,11},{4,6},{5,13},{6,0},{7,15},{8,10},{9,17},{... | collective-permute-start | bytes 1376264 | tf_op jit(solution)/shard_map/ppermute | solution.py:56
  66.5 10.0 %collective-permute-start.17 = (bf16[2,224,512]{2,1,0:T(8,128)(2,1)S(1)}, bf16[2,224,512]{2,1,0:T(8,128)(2,1)S(1)}, u32[]{:S(2)}, u32[]{:S(2)}) collective-permute-start(bf16[2,224,512]{2,1,0:T(8,128)(2,1)S(1)} %project.15), channel_id=1, source_target_pairs={{0,6},{1,25},{2,0},{3,27},{4,2},{5,29},{6,4},{7,31},{8,14},{9,1},{... | collective-permute-start | bytes 1376264 | tf_op jit(solution)/shard_map/ppermute | solution.py:56
  68.7 13.4 %collective-permute-start.12 = (bf16[2,224,512]{2,1,0:T(8,128)(2,1)S(1)}, bf16[2,224,512]{2,1,0:T(8,128)(2,1)S(1)}, u32[]{:S(2)}, u32[]{:S(2)}) collective-permute-start(bf16[2,224,512]{2,1,0:T(8,128)(2,1)S(1)} %project.9), channel_id=1, source_target_pairs={{0,4},{1,17},{2,6},{3,19},{4,0},{5,21},{6,2},{7,23},{8,12},{9,25},... | collective-permute-start | bytes 1376264 | tf_op jit(solution)/shard_map/ppermute | solution.py:56
  70.1 21.1 %collective-permute-start.13 = (bf16[2,224,512]{2,1,0:T(8,128)(2,1)S(1)}, bf16[2,224,512]{2,1,0:T(8,128)(2,1)S(1)}, u32[]{:S(2)}, u32[]{:S(2)}) collective-permute-start(bf16[2,224,512]{2,1,0:T(8,128)(2,1)S(1)} %project.10), channel_id=1, source_target_pairs={{0,2},{1,9},{2,4},{3,11},{4,6},{5,13},{6,0},{7,15},{8,10},{9,17},{... | collective-permute-start | bytes 1376264 | tf_op jit(solution)/shard_map/ppermute | solution.py:56
  72.5 18.8 %collective-permute-start.14 = (bf16[2,224,512]{2,1,0:T(8,128)(2,1)S(1)}, bf16[2,224,512]{2,1,0:T(8,128)(2,1)S(1)}, u32[]{:S(2)}, u32[]{:S(2)}) collective-permute-start(bf16[2,224,512]{2,1,0:T(8,128)(2,1)S(1)} %project.11), channel_id=1, source_target_pairs={{0,6},{1,25},{2,0},{3,27},{4,2},{5,29},{6,4},{7,31},{8,14},{9,1},{... | collective-permute-start | bytes 1376264 | tf_op jit(solution)/shard_map/ppermute | solution.py:56
  76.8 14.5 %collective-permute-start.19 = (bf16[224,512]{1,0:T(8,128)(2,1)S(1)}, bf16[224,512]{1,0:T(8,128)(2,1)S(1)}, u32[]{:S(2)}, u32[]{:S(2)}) collective-permute-start(bf16[224,512]{1,0:T(8,128)(2,1)S(1)} %get-tuple-element.71), channel_id=1, source_target_pairs={{0,8},{1,3},{2,10},{3,5},{4,12},{5,7},{6,14},{7,1},{8,16},{9,11},{... | collective-permute-start | bytes 688136 | tf_op jit(solution)/shard_map/ppermute | solution.py:61
  78.8 12.5 %collective-permute-start.18 = (bf16[224,512]{1,0:T(8,128)(2,1)S(1)}, bf16[224,512]{1,0:T(8,128)(2,1)S(1)}, u32[]{:S(2)}, u32[]{:S(2)}) collective-permute-start(bf16[224,512]{1,0:T(8,128)(2,1)S(1)} %get-tuple-element.72), channel_id=1, source_target_pairs={{0,16},{1,5},{2,18},{3,7},{4,20},{5,1},{6,22},{7,3},{8,24},{9,13},... | collective-permute-start | bytes 688136 | tf_op jit(solution)/shard_map/ppermute | solution.py:61
  91.5 6.1 %collective-permute-start.20 = (bf16[224,512]{1,0:T(8,128)(2,1)S(1)}, bf16[224,512]{1,0:T(8,128)(2,1)S(1)}, u32[]{:S(2)}, u32[]{:S(2)}) collective-permute-start(bf16[224,512]{1,0:T(8,128)(2,1)S(1)} %slice_bitcast_fusion), channel_id=1, source_target_pairs={{0,24},{1,7},{2,26},{3,1},{4,28},{5,3},{6,30},{7,5},{8,0},{9,15},{... | collective-permute-start | bytes 688136 | tf_op jit(solution)/shard_map/ppermute | solution.py:61

commit v3 on v2

--- a/solution.py
+++ b/solution.py
@@ -77,21 +77,22 @@
 LONG = pl.CostEstimate(flops=10**11, bytes_accessed=1024, transcendentals=0)
 
 
-def pages_kernel(place, lens_in, locs_in, pool_in, out_ref, lens, locs, pool_ref, wide, rows, sems):
+def pages_kernel(place, lens_in, locs_in, pool_in, out_ref, lens, locs, pool_ref, wide, chosen, rows, sems):
     copies = [
         pltpu.make_async_copy(source, target, sems.at[k])
         for k, (source, target) in enumerate([(lens_in, lens), (locs_in, locs), (pool_in, pool_ref)])
     ]
     for copy in copies:
         copy.start()
-    for copy in copies:
-        copy.wait()
-    wide[...] = pool_ref[...].astype(F32)
+    copies[0].wait()
+    copies[1].wait()
     pool_id = place[0]
     head_id = place[1]
-    lane = lax.broadcasted_iota(jnp.int32, (1, 128), 1)
-
-    def one_request(r, carry):
+    request = lax.broadcasted_iota(jnp.int32, (REQ, 128), 0)
+    lane = lax.broadcasted_iota(jnp.int32, (REQ, 128), 1)
+    past = jnp.zeros((REQ, 128), jnp.int32)
+    picks = []
+    for r in range(REQ):
         sel = jnp.int32(0)
         slot = jnp.int32(0)
         for i in range(MAXP // N_HEAD):
@@ -99,20 +100,24 @@
             mine = lax.shift_right_logical(loc, 9) == pool_id
             sel = jnp.where(mine, loc & (PAGES_DEV - 1), sel)
             slot = jnp.where(mine, head_id + i * N_HEAD, slot)
-        length = lens[r]
-        for u in range(PAGE // 2):
-            two = wide[pl.ds(sel, 1), 2 * WIDTH * u : 2 * WIDTH * (u + 1)]
-            for odd in range(2):
-                t = 2 * u + odd
-                token = pltpu.roll(two, WIDTH, 1) if odd else two
-                extra = jnp.where(slot * PAGE + t < length, 0.0, BLOCKED)
-                tail = jnp.where(lane < ROPE, token[:, KV:PAY], jnp.where(lane == ROPE, extra, 0.0))
-                rows[r, t : t + 1, :KV] = token[:, :KV]
-                rows[r, t : t + 1, KV:] = tail
-        return carry
-
-    lax.fori_loop(0, REQ, one_request, 0)
-    out_ref[...] = rows[...].astype(BF)
+        picks.append(sel)
+        past = jnp.where(request == r, slot * PAGE - lens[r], past)
+    copies[2].wait()
+    wide[...] = pool_ref[...].astype(F32)
+    for r in range(REQ):
+        chosen[r : r + 1, :] = wide[pl.ds(picks[r], 1), :]
+    for u in range(PAGE // 2):
+        two = chosen[:, 2 * WIDTH * u : 2 * WIDTH * (u + 1)]
+        for odd in range(2):
+            t = 2 * u + odd
+            token = pltpu.roll(two, WIDTH, 1) if odd else two
+            extra = jnp.where(past + t < 0, 0.0, BLOCKED)
+            tail = jnp.where(lane < ROPE, token[:, KV:PAY], jnp.where(lane == ROPE, extra, 0.0))
+            for k in range(PAY // 128):
+                part = token[:, 128 * k : 128 * (k + 1)] if 128 * k < KV else tail
+                rows[k, pl.ds(t, REQ, stride=PAGE), :] = part
+    for k in range(PAY // 128):
+        out_ref[:, :, 128 * k : 128 * (k + 1)] = rows[k].reshape(REQ, PAGE, 128).astype(BF)
 
 
 def own_pages(place, cached_len, page_loc, latent_pool):
@@ -126,7 +131,8 @@
             pltpu.SMEM((REQ, MAXP), jnp.int32),
             pltpu.VMEM((PAGES_DEV, PAGE * WIDTH), BF),
             pltpu.VMEM((PAGES_DEV, PAGE * WIDTH), F32),
-            pltpu.VMEM((REQ, PAGE, PAY), F32),
+            pltpu.VMEM((REQ, PAGE * WIDTH), F32),
+            pltpu.VMEM((PAY // 128, REQ * PAGE, 128), F32),
             pltpu.SemaphoreType.DMA((3,)),
         ],
         compiler_params=params(8),
@@ -167,47 +173,6 @@
     )(in_hbm(queries), in_hbm(latent_t), w_ukv)
 
 
-def turn_kernel(place, w_ref, keep_ref, give_ref, flag_ref, turned):
-    flag_ref[...] = jnp.zeros_like(flag_ref)
-    width = 2 * SIDE * COLS
-    for k in range(width // 256):
-        turned[256 * k : 256 * (k + 1), :] = w_ref[:, 256 * k : 256 * (k + 1)].T
-    head_id = place[1]
-    core = head_id & 1
-    x = lax.shift_right_logical(head_id, 1) & (SIDE - 1)
-    dy = pl.program_id(0)
-    for dx in range(SIDE):
-        at = ((x + dx) & (SIDE - 1)) * 2
-        mine = (jnp.where(core == 0, dx, dy), jnp.where(core == 0, dy + 3, dx + 3) & (SIDE - 1))
-        theirs = (jnp.where(core == 0, dy, dx), jnp.where(core == 0, dx + 3, dy + 3) & (SIDE - 1))
-        keep_ref[mine] = turned[pl.ds(pl.multiple_of((at + core) * COLS, 32), COLS), :]
-        give_ref[theirs] = turned[pl.ds(pl.multiple_of((at + 1 - core) * COLS, 32), COLS), :]
-
-
-def turned_weights(place, w_out):
-    rows = HPD * VD
-    part = jax.ShapeDtypeStruct((SIDE, SIDE, COLS, rows), BF)
-    whole = pl.BlockSpec((SIDE, SIDE, COLS, rows), lambda g, s: (0, 0, 0, 0))
-
-    def column(g, s):
-        return (0, (lax.shift_right_logical(s[1], 3) + g) & (SIDE - 1))
-
-    return pl.pallas_call(
-        turn_kernel,
-        out_shape=[part, part, jax.ShapeDtypeStruct((8, 128), F32)],
-        grid_spec=pltpu.PrefetchScalarGridSpec(
-            num_scalar_prefetch=1,
-            grid=(SIDE,),
-            in_specs=[pl.BlockSpec((rows, 2 * SIDE * COLS), column)],
-            out_specs=[whole, whole, pl.BlockSpec((8, 128), lambda g, s: (0, 0))],
-            scratch_shapes=[pltpu.VMEM((2 * SIDE * COLS, rows), BF)],
-        ),
-        compiler_params=params(28),
-        cost_estimate=SHORT,
-        name="turned_weights",
-    )(place, in_hbm(w_out))
-
-
 def lift_kernel(count, *refs):
     w_ref = refs[count]
     kv_out, rope_out = refs[count + 1 :]
@@ -265,7 +230,9 @@
     return jnp.where(key <= row, n, BLOCKED)
 
 
-def near_kernel(q_ref, kv_ref, rope_ref, kv_new, rope_new, sum_ref, top_ref):
+def near_kernel(
+    place, q_ref, kv_ref, rope_ref, kv_new, rope_new, w_ref, sum_ref, top_ref, keep_ref, give_ref, turned
+):
     def work(exact):
         for half in range(2):
             rows = slice(half * HALF, (half + 1) * HALF)
@@ -281,7 +248,19 @@
             )
             top_ref[rows, :] = jnp.broadcast_to(top, (HALF, 128))
 
+    for k in range(2 * SIDE * COLS // 256):
+        turned[256 * k : 256 * (k + 1), :] = w_ref[:, 256 * k : 256 * (k + 1)].T
     work(False)
+    head_id = place[1]
+    core = head_id & 1
+    x = lax.shift_right_logical(head_id, 1) & (SIDE - 1)
+    dy = pl.program_id(0)
+    for dx in range(SIDE):
+        at = ((x + dx) & (SIDE - 1)) * 2
+        mine = (jnp.where(core == 0, dx, dy), jnp.where(core == 0, dy + 3, dx + 3) & (SIDE - 1))
+        theirs = (jnp.where(core == 0, dy, dx), jnp.where(core == 0, dx + 3, dy + 3) & (SIDE - 1))
+        keep_ref[mine] = turned[pl.ds(pl.multiple_of((at + core) * COLS, 32), COLS), :]
+        give_ref[theirs] = turned[pl.ds(pl.multiple_of((at + 1 - core) * COLS, 32), COLS), :]
     fine = jnp.max(sum_ref[:, VD:]) < LARGE
 
     @pl.when(jnp.logical_not(fine))
@@ -289,25 +268,38 @@
         work(True)
 
 
-def attend_near(q_ext, kv, rope, kv_new, rope_new):
-    head = pl.BlockSpec((NEW, 256), lambda h: (0, h))
-    whole = pl.BlockSpec((NEW, 128), lambda h: (0, 0))
+def attend_near(place, q_ext, kv, rope, kv_new, rope_new, w_out):
+    head = pl.BlockSpec((NEW, 256), lambda h, s: (0, h))
+    rope_spec = pl.BlockSpec((NEW, 128), lambda h, s: (0, 0))
+    rows = HPD * VD
+    part = jax.ShapeDtypeStruct((SIDE, SIDE, COLS, rows), BF)
+    whole = pl.BlockSpec((SIDE, SIDE, COLS, rows), lambda h, s: (0, 0, 0, 0))
+
+    def column(h, s):
+        return (0, (lax.shift_right_logical(s[1], 3) + h) & (SIDE - 1))
+
     return pl.pallas_call(
         near_kernel,
         out_shape=[
             jax.ShapeDtypeStruct((NEW, HPD * 256), F32),
             jax.ShapeDtypeStruct((NEW, HPD * 128), F32),
+            part,
+            part,
         ],
-        grid=(HPD,),
-        in_specs=[head, head, whole, head, whole],
-        out_specs=[head, pl.BlockSpec((NEW, 128), lambda h: (0, h))],
-        compiler_params=params(16),
+        grid_spec=pltpu.PrefetchScalarGridSpec(
+            num_scalar_prefetch=1,
+            grid=(HPD,),
+            in_specs=[head, head, rope_spec, head, rope_spec, pl.BlockSpec((rows, 2 * SIDE * COLS), column)],
+            out_specs=[head, pl.BlockSpec((NEW, 128), lambda h, s: (0, h)), whole, whole],
+            scratch_shapes=[pltpu.VMEM((2 * SIDE * COLS, rows), BF)],
+        ),
+        compiler_params=params(36),
         cost_estimate=SHORT,
         name="attend_near",
-    )(q_ext, kv, rope, kv_new, rope_new)
-
-
-def far_kernel(groups, q_ref, sum_ref, top_ref, order_ref, *refs):
+    )(place, q_ext, kv, rope, kv_new, rope_new, in_hbm(w_out))
+
+
+def far_kernel(groups, q_ref, sum_ref, top_ref, *refs):
     out_ref, total_ref = refs[-2:]
     old = top_ref[:, :1]
 
@@ -333,7 +325,7 @@
     out_ref[...] = (total_ref[:, :VD] / total_ref[:, VD:]).astype(BF)
 
 
-def attend_far(q_ext, sums, tops, order, far):
+def attend_far(q_ext, sums, tops, far):
     specs, operands, keys = [], [], 0
     for kv, rope in far:
         rows = kv.shape[0]
@@ -348,35 +340,34 @@
         functools.partial(far_kernel, len(far)),
         out_shape=jax.ShapeDtypeStruct((NEW, HPD * VD), BF),
         grid=(HPD,),
-        in_specs=[head, head, pl.BlockSpec((NEW, 128), lambda h: (0, h)), pl.BlockSpec((8, 128), lambda h: (0, 0))] + specs,
+        in_specs=[head, head, pl.BlockSpec((NEW, 128), lambda h: (0, h))] + specs,
         out_specs=pl.BlockSpec((NEW, VD), lambda h: (0, h)),
         scratch_shapes=[pltpu.VMEM((NEW, 256), F32)],
         compiler_params=params(20),
         cost_estimate=LONG,
         name="attend_far",
-    )(q_ext, sums, tops, order, *operands)
+    )(q_ext, sums, tops, *operands)
 
 
 def project_kernel(att_ref, other_ref, keep_ref, got_ref, out_ref):
-    rows = 2 * COLS
+    rows = out_ref.shape[0] * COLS
     out = lax.dot_general(
         keep_ref[...].reshape(rows, HPD * VD), att_ref[...], NT, preferred_element_type=F32
     ) + lax.dot_general(
         got_ref[...].reshape(rows, HPD * VD), other_ref[...], NT, preferred_element_type=F32
     )
-    out_ref[...] = out.reshape(2, COLS, NEW).astype(BF)
-
-
-def project(a, pair, att, other, keep, got):
-    spec = pl.BlockSpec((1, 2, COLS, HPD * VD), lambda i: (a, pair, 0, 0))
+    out_ref[...] = out.reshape(out_ref.shape).astype(BF)
+
+
+def project(a, first, count, att, other, keep, got):
+    spec = pl.BlockSpec((1, count, COLS, HPD * VD), lambda i: (a, first // count, 0, 0))
     whole = pl.BlockSpec((NEW, HPD * VD), lambda i: (0, 0))
-    rows = 2 * COLS
     return pl.pallas_call(
         project_kernel,
-        out_shape=jax.ShapeDtypeStruct((2, COLS, NEW), BF),
+        out_shape=jax.ShapeDtypeStruct((count, COLS, NEW), BF),
         grid=(1,),
         in_specs=[whole, whole, spec, spec],
-        out_specs=pl.BlockSpec((2, COLS, NEW), lambda i: (0, 0, 0)),
+        out_specs=pl.BlockSpec((count, COLS, NEW), lambda i: (0, 0, 0)),
         compiler_params=params(16),
         cost_estimate=SHORT,
         name="project",
@@ -399,25 +390,31 @@
     q_ext, kv_new, rope_new = new_tokens(queries, new_latent.T, w_ukv)
     line = [own, send_first(own, 2), send_first(own, 1), send_first(own, -1)]
     *line, kv_new = lax.optimization_barrier((*line, kv_new))
-    line, place = lax.optimization_barrier((jnp.concatenate(line, 0), place))
+    line = jnp.concatenate(line, 0)
     pieces = [send_second(line, d) for d in (2, 1, -1)]
     near = lift([line, swap(line)], w_ukv)
-    sums, tops = attend_near(q_ext, *near, kv_new, rope_new)
-    keep, give, order = turned_weights(place, w_out)
+    sums, tops, keep, give = attend_near(place, q_ext, *near, kv_new, rope_new, w_out)
     got = swap(give)
-    *pieces, sums, order = lax.optimization_barrier((*pieces, sums, order))
+    *pieces, sums = lax.optimization_barrier((*pieces, sums))
     far = [lift(pieces, w_ukv), lift([swap(piece) for piece in pieces], w_ukv)]
-    att = attend_far(q_ext, sums, tops, order, far)
+    att = attend_far(q_ext, sums, tops, far)
     other = swap(att)
-    sent = [
-        [send_first(project(a, pair, att, other, keep, got), d) for a, d in ((2, 2), (1, 1), (3, -1))]
-        for pair in range(2)
-    ]
-    one = add(project(0, 0, att, other, keep, got), *sent[0])
-    one = [send_second(one[1], 2), send_second(one[0], 1)]
-    *sent[1], one[0], one[1] = lax.optimization_barrier((*sent[1], *one))
-    two = add(project(0, 1, att, other, keep, got), *sent[1])
-    out = add(two[1], *one, send_second(two[0], -1))
+    def partial_sums(a, half):
+        return project(a, 2 * half, 2, att, other, keep, got)
+
+    far_parts = [partial_sums(2, half) for half in range(2)]
+    att, far_parts[1] = lax.optimization_barrier((att, far_parts[1]))
+    passing = send_first(far_parts[0], 1), send_first(far_parts[1], -1)
+    early = send_first(partial_sums(1, 1), 1), send_first(partial_sums(3, 0), -1)
+    late = (
+        send_first(add(partial_sums(1, 0), passing[0]), 1),
+        send_first(add(partial_sums(3, 1), passing[1]), -1),
+    )
+    one, two = add(partial_sums(0, 0), late[0], early[1])
+    rest = partial_sums(0, 1), early[0], late[1]
+    three = add(*[value[0] for value in rest])
+    moved = [send_second(two, 2), send_second(one, 1), send_second(three, -1)]
+    out = add(*[value[1] for value in rest], *moved)
     return out.T
 
 

time: 100 us -> 92.6 us (0.926); the launches traced: 98.4 us -> 92.4 us
  Pallas kernels: 34.3 us -> 30.7 us
  waiting for transfers between devices: 20.1 us -> 17.3 us
    pallas_call x9 -> x8, Pallas kernels: 11.3 us -> 5.35 us  [project(): pl.pallas_call(project_kernel, out_shape=jax.ShapeDtypeStruct((count, COL...]
    ppermute x9, waiting for transfers between devices: 13.1 us -> 7.24 us  [send_first(): return lax.ppermute(value, PLANE, perm)]
    ppermute x6, waiting for transfers between devices: 4.64 us -> 8.03 us  [send_second(): return lax.ppermute(value, PLANE, perm)]
    pallas_call x1, Pallas kernels: 9.54 us -> 12.6 us  [attend_near(): pl.pallas_call(near_kernel, out_shape=[jax.ShapeDtypeStruct((NEW, HPD * 2...]
  transfers between devices with their start and end apart: 21 -> 21, of which waited for: 8 -> 9; matrix products, arithmetic and copies ran while one was open for 0% -> 1% of each run, Pallas kernels for 32% -> 31%
where the time goes in v3:
time: 92.6 us; the launch traced here: 92.4 us
  Pallas kernels  30.7 us (33%)
  starting transfers between devices  25.9 us (28%)
  waiting for transfers between devices  17.3 us (19%)
  blocking collectives  15.5 us (17%)
  other arithmetic  1.44 us (2%)
  local copies, waits for them, and re-layouts  1.32 us (1%)
    all_to_all x1, blocking collectives, per_device(): lax.all_to_all(outgoing, 'pool', split_axis=0, concat_axis=0, tiled=True)  15.5 us
    ppermute x9, starting transfers between devices, send_first(): return lax.ppermute(value, PLANE, perm)  14.5 us
    pallas_call x1, Pallas kernels, attend_near(): pl.pallas_call(near_kernel, out_shape=[jax.ShapeDtypeStruct((NEW, HPD * 2...  12.6 us
    ppermute x6, starting transfers between devices, send_second(): return lax.ppermute(value, PLANE, perm)  9.76 us
    ppermute x6, waiting for transfers between devices, send_second(): return lax.ppermute(value, PLANE, perm)  8.03 us
    ppermute x9, waiting for transfers between devices, send_first(): return lax.ppermute(value, PLANE, perm)  7.24 us
    pallas_call x1, Pallas kernels, attend_far(): pl.pallas_call(functools.partial(far_kernel, len(far)), out_shape=jax.Sha...  6.17 us
    pallas_call x8, Pallas kernels, project(): pl.pallas_call(project_kernel, out_shape=jax.ShapeDtypeStruct((count, COL...  5.35 us
  transfers between devices with their start and end apart: 21, of which 9 were waited for; matrix products, arithmetic and copies ran while one was open for 1% of the time, Pallas kernels for 31%

profile of v3, /device:TPU:32, one launch (start us, length us, event | category | flops | bytes accessed | tf_op | source)
XLA Modules:
  0.0 92.4 jit_solution(3886467859526645162)
XLA Ops:
  0.1 1.8 %own_pages.1 = bf16[8,8,640]{2,1,0:T(8,128)(2,1)S(1)} custom-call(s32[2]{0:T(128)S(1)} %pad_add_fusion.place, s32[8]{0:T(128)} %lens_in.1, s32[8,256]{1,0:T(8,128)} %locs_in.1, bf16[16,4608]{1,0:T(8,128)(2,1)} %pool_in.1), custom_call_target="tpu_custom_call" | custom-call | bytes 1024 | tf_op jit(solution)/shard_map/own_pages/pallas_call | solution.py:124
  1.8 15.5 %all_to_all.5 = bf16[8,8,640]{2,1,0:T(8,128)(2,1)S(1)} all-to-all(bf16[8,8,640]{2,1,0:T(8,128)(2,1)S(1)} %own_pages.1), channel_id=1, replica_groups=mesh['pool'=8,'y_hi'=2,'y_lo'=2,'x_hi'=2,'x_lo'=2,'core'=2] {'pool'}, dimensions={0} | all-to-all | bytes 163840 | tf_op jit(solution)/shard_map/all_to_all | solution.py:387
  17.3 2.8 %collective-permute-start.2 = (bf16[64,640]{1,0:T(8,128)(2,1)S(1)}, bf16[64,640]{1,0:T(8,128)(2,1)S(1)}, u32[]{:S(2)}, u32[]{:S(2)}) collective-permute-start(bf16[64,640]{1,0:T(8,128)(2,1)S(1)} %bitcast.23), channel_id=1, source_target_pairs={{0,6},{1,25},{2,0},{3,27},{4,2},{5,29},{6,4},{7,31},{8,14},{9,1},{... | collective-permute-start | bytes 245768 | tf_op jit(solution)/shard_map/ppermute | solution.py:56
  20.1 2.3 %collective-permute-start = (bf16[64,640]{1,0:T(8,128)(2,1)S(1)}, bf16[64,640]{1,0:T(8,128)(2,1)S(1)}, u32[]{:S(2)}, u32[]{:S(2)}) collective-permute-start(bf16[64,640]{1,0:T(8,128)(2,1)S(1)} %bitcast.25), channel_id=1, source_target_pairs={{0,4},{1,17},{2,6},{3,19},{4,0},{5,21},{6,2},{7,23},{8,12},{9,25},... | collective-permute-start | bytes 245768 | tf_op jit(solution)/shard_map/ppermute | solution.py:56
  22.4 1.2 %copy-done = bf16[512,1024]{1,0:T(8,128)(2,1)S(1)} copy-done((bf16[512,1024]{1,0:T(8,128)(2,1)S(1)}, bf16[512,1024]{1,0:T(8,128)(2,1)}, u32[]{:S(2)}) %copy-start) | copy-done | bytes 1048600
  23.6 2.1 %new_tokens.1 = (bf16[512,1024]{1,0:T(8,128)(2,1)S(1)}, bf16[512,1024]{1,0:T(8,128)(2,1)S(1)}, bf16[512,128]{1,0:T(8,128)(2,1)S(1)}) custom-call(bf16[512,768]{1,0:T(8,128)(2,1)} %q_ref.1, bf16[576,512]{1,0:T(8,128)(2,1)} %bitcast.22, bf16[512,1024]{1,0:T(8,128)(2,1)S(1)} %copy-done), custom_call_target="tpu_custom_call" | custom-call | bytes 1024 | tf_op jit(solution)/shard_map/new_tokens/pallas_call | solution.py:161
  25.7 0.9 collective-permute-done.1
  26.8 3.1 %collective-permute-start.5 = (bf16[256,640]{1,0:T(8,128)(2,1)S(1)}, bf16[256,640]{1,0:T(8,128)(2,1)S(1)}, u32[]{:S(2)}, u32[]{:S(2)}) collective-permute-start(bf16[256,640]{1,0:T(8,128)(2,1)S(1)} %constant_dynamic-update-slice_fusion.refs_0_), channel_id=1, source_target_pairs={{0,24},{1,7},{2,26},{3,1},{4,28},{5,3},{6,30},{7,5},{8,0},{9,15},{... | collective-permute-start | bytes 983048 | tf_op jit(solution)/shard_map/ppermute | solution.py:61
  29.9 2.2 %collective-permute-start.3 = (bf16[256,640]{1,0:T(8,128)(2,1)S(1)}, bf16[256,640]{1,0:T(8,128)(2,1)S(1)}, u32[]{:S(2)}, u32[]{:S(2)}) collective-permute-start(bf16[256,640]{1,0:T(8,128)(2,1)S(1)} %constant_dynamic-update-slice_fusion.refs_0_), channel_id=1, source_target_pairs={{0,16},{1,5},{2,18},{3,7},{4,20},{5,1},{6,22},{7,3},{8,24},{9,13},... | collective-permute-start | bytes 983048 | tf_op jit(solution)/shard_map/ppermute | solution.py:61
  32.8 12.6 %attend_near.1 = (f32[512,1024]{1,0:T(8,128)S(1)}, f32[512,512]{1,0:T(8,128)S(1)}, bf16[4,4,224,512]{3,2,1,0:T(8,128)(2,1)S(1)}, bf16[4,4,224,512]{3,2,1,0:T(8,128)(2,1)S(1)}) custom-call(s32[2]{0:T(128)S(1)} %pad_add_fusion.place, bf16[512,1024]{1,0:T(8,128)(2,1)S(1)} %get-tuple-element.32.q_ref, bf16[512,1024]{1,0:T(8,128)(2,1)S(1)} %get-tuple-element.39.kv_ref, ...), custom_call_target="tpu_custom_call" | custom-call | bytes 1024 | tf_op jit(solution)/shard_map/attend_near/pallas_call | solution.py:281
  46.2 1.0 %lift.4 = (bf16[768,1024]{1,0:T(8,128)(2,1)S(1)}, bf16[768,128]{1,0:T(8,128)(2,1)S(1)}) custom-call(bf16[256,640]{1,0:T(8,128)(2,1)S(1)} %collective-permute-done.3.refs_0_, bf16[256,640]{1,0:T(8,128)(2,1)S(1)} %collective-permute-done.4.refs_1_, bf16[256,640]{1,0:T(8,128)(2,1)S(1)} %collective-permute-done.5.refs_2_, bf16[512,1024]{1,0:T(8,128)(2,1)S(1)} %copy-done.1), custom_call_target="tpu_custom_call" | custom-call | bytes 1024 | tf_op jit(solution)/shard_map/lift/pallas_call | solution.py:190
  48.1 1.0 %lift.5 = (bf16[768,1024]{1,0:T(8,128)(2,1)S(1)}, bf16[768,128]{1,0:T(8,128)(2,1)S(1)}) custom-call(bf16[256,640]{1,0:T(8,128)(2,1)S(1)} %collective-permute-done.7.refs_0_, bf16[256,640]{1,0:T(8,128)(2,1)S(1)} %collective-permute-done.8.refs_1_, bf16[256,640]{1,0:T(8,128)(2,1)S(1)} %collective-permute-done.9.refs_2_, bf16[512,1024]{1,0:T(8,128)(2,1)S(1)} %copy-done.1), custom_call_target="tpu_custom_call" | custom-call | bytes 1024 | tf_op jit(solution)/shard_map/lift/pallas_call | solution.py:190
  49.1 6.2 %attend_far.1.att_ref = bf16[512,512]{1,0:T(8,128)(2,1)S(1)} custom-call(bf16[512,1024]{1,0:T(8,128)(2,1)S(1)} %get-tuple-element.32.q_ref, f32[512,1024]{1,0:T(8,128)S(1)} %get-tuple-element.44.sum_ref, f32[512,512]{1,0:T(8,128)S(1)} %get-tuple-element.45.top_ref, bf16[768,1024]{1,0:T(8,128)(2,1)S(1)} %get-tuple-element.49.refs_0_, ...), custom_call_target="tpu_custom_call" | custom-call | flops 99999997952 | bytes 1024 | tf_op jit(solution)/shard_map/attend_far/pallas_call | solution.py:339
  55.5 1.8 %collective-permute-done.10.other_ref = bf16[512,512]{1,0:T(8,128)(2,1)S(1)} collective-permute-done((bf16[512,512]{1,0:T(8,128)(2,1)S(1)}, bf16[512,512]{1,0:T(8,128)(2,1)S(1)}, u32[]{:S(2)}, u32[]{:S(2)}) %collective-permute-start.10) | collective-permute-done | bytes 524320 | tf_op jit(solution)/shard_map/ppermute | solution.py:65
  58.0 2.7 %collective-permute-start.13 = (bf16[2,224,512]{2,1,0:T(8,128)(2,1)S(1)}, bf16[2,224,512]{2,1,0:T(8,128)(2,1)S(1)}, u32[]{:S(2)}, u32[]{:S(2)}) collective-permute-start(bf16[2,224,512]{2,1,0:T(8,128)(2,1)S(1)} %project.8), channel_id=1, source_target_pairs={{0,6},{1,25},{2,0},{3,27},{4,2},{5,29},{6,4},{7,31},{8,14},{9,1},{... | collective-permute-start | bytes 1376264 | tf_op jit(solution)/shard_map/ppermute | solution.py:56
  63.2 3.0 %collective-permute-start.17 = (bf16[2,224,512]{2,1,0:T(8,128)(2,1)S(1)}, bf16[2,224,512]{2,1,0:T(8,128)(2,1)S(1)}, u32[]{:S(2)}, u32[]{:S(2)}) collective-permute-start(bf16[2,224,512]{2,1,0:T(8,128)(2,1)S(1)} %project.15), channel_id=1, source_target_pairs={{0,6},{1,25},{2,0},{3,27},{4,2},{5,29},{6,4},{7,31},{8,14},{9,1},{... | collective-permute-start | bytes 1376264 | tf_op jit(solution)/shard_map/ppermute | solution.py:56
  67.7 2.9 %collective-permute-start.14 = (bf16[2,224,512]{2,1,0:T(8,128)(2,1)S(1)}, bf16[2,224,512]{2,1,0:T(8,128)(2,1)S(1)}, u32[]{:S(2)}, u32[]{:S(2)}) collective-permute-start(bf16[2,224,512]{2,1,0:T(8,128)(2,1)S(1)} %add_convert_fusion.2), channel_id=1, source_target_pairs={{0,6},{1,25},{2,0},{3,27},{4,2},{5,29},{6,4},{7,31},{8,14},{9,1},{... | collective-permute-start | bytes 1376264 | tf_op jit(solution)/shard_map/ppermute | solution.py:56
  72.9 3.1 %collective-permute-done.12 = bf16[2,224,512]{2,1,0:T(8,128)(2,1)S(1)} collective-permute-done((bf16[2,224,512]{2,1,0:T(8,128)(2,1)S(1)}, bf16[2,224,512]{2,1,0:T(8,128)(2,1)S(1)}, u32[]{:S(2)}, u32[]{:S(2)}) %collective-permute-start.12) | collective-permute-done | bytes 458784 | tf_op jit(solution)/shard_map/ppermute | solution.py:56
  76.1 1.1 %collective-permute-done.14 = bf16[2,224,512]{2,1,0:T(8,128)(2,1)S(1)} collective-permute-done((bf16[2,224,512]{2,1,0:T(8,128)(2,1)S(1)}, bf16[2,224,512]{2,1,0:T(8,128)(2,1)S(1)}, u32[]{:S(2)}, u32[]{:S(2)}) %collective-permute-start.14) | collective-permute-done | bytes 458784 | tf_op jit(solution)/shard_map/ppermute | solution.py:56
  77.2 2.4 %collective-permute-start.20 = (bf16[224,512]{1,0:T(8,128)(2,1)S(1)}, bf16[224,512]{1,0:T(8,128)(2,1)S(1)}, u32[]{:S(2)}, u32[]{:S(2)}) collective-permute-start(bf16[224,512]{1,0:T(8,128)(2,1)S(1)} %fusion.3), channel_id=1, source_target_pairs={{0,24},{1,7},{2,26},{3,1},{4,28},{5,3},{6,30},{7,5},{8,0},{9,15},{... | collective-permute-start | bytes 688136 | tf_op jit(solution)/shard_map/ppermute | solution.py:61
  79.6 1.6 %collective-permute-done.16 = bf16[2,224,512]{2,1,0:T(8,128)(2,1)S(1)} collective-permute-done((bf16[2,224,512]{2,1,0:T(8,128)(2,1)S(1)}, bf16[2,224,512]{2,1,0:T(8,128)(2,1)S(1)}, u32[]{:S(2)}, u32[]{:S(2)}) %collective-permute-start.16) | collective-permute-done | bytes 458784 | tf_op jit(solution)/shard_map/ppermute | solution.py:56
  81.5 1.4 %collective-permute-start.18 = (bf16[224,512]{1,0:T(8,128)(2,1)S(1)}, bf16[224,512]{1,0:T(8,128)(2,1)S(1)}, u32[]{:S(2)}, u32[]{:S(2)}) collective-permute-start(bf16[224,512]{1,0:T(8,128)(2,1)S(1)} %get-tuple-element.57), channel_id=1, source_target_pairs={{0,16},{1,5},{2,18},{3,7},{4,20},{5,1},{6,22},{7,3},{8,24},{9,13},... | collective-permute-start | bytes 688136 | tf_op jit(solution)/shard_map/ppermute | solution.py:61
  83.5 5.7 %collective-permute-done.18 = bf16[224,512]{1,0:T(8,128)(2,1)S(1)} collective-permute-done((bf16[224,512]{1,0:T(8,128)(2,1)S(1)}, bf16[224,512]{1,0:T(8,128)(2,1)S(1)}, u32[]{:S(2)}, u32[]{:S(2)}) %collective-permute-start.18) | collective-permute-done | bytes 229408 | tf_op jit(solution)/shard_map/ppermute | solution.py:61
  89.2 2.4 %collective-permute-done.19 = bf16[224,512]{1,0:T(8,128)(2,1)S(1)} collective-permute-done((bf16[224,512]{1,0:T(8,128)(2,1)S(1)}, bf16[224,512]{1,0:T(8,128)(2,1)S(1)}, u32[]{:S(2)}, u32[]{:S(2)}) %collective-permute-start.19) | collective-permute-done | bytes 229408 | tf_op jit(solution)/shard_map/ppermute | solution.py:61
  (49 shorter events, 11.6 us)
Async XLA Ops:
  17.3 8.4 %collective-permute-start.2 = (bf16[64,640]{1,0:T(8,128)(2,1)S(1)}, bf16[64,640]{1,0:T(8,128)(2,1)S(1)}, u32[]{:S(2)}, u32[]{:S(2)}) collective-permute-start(bf16[64,640]{1,0:T(8,128)(2,1)S(1)} %bitcast.23), channel_id=1, source_target_pairs={{0,6},{1,25},{2,0},{3,27},{4,2},{5,29},{6,4},{7,31},{8,14},{9,1},{... | collective-permute-start | bytes 245768 | tf_op jit(solution)/shard_map/ppermute | solution.py:56
  20.1 6.5 %collective-permute-start.1 = (bf16[64,640]{1,0:T(8,128)(2,1)S(1)}, bf16[64,640]{1,0:T(8,128)(2,1)S(1)}, u32[]{:S(2)}, u32[]{:S(2)}) collective-permute-start(bf16[64,640]{1,0:T(8,128)(2,1)S(1)} %bitcast.24), channel_id=1, source_target_pairs={{0,2},{1,9},{2,4},{3,11},{4,6},{5,13},{6,0},{7,15},{8,10},{9,17},{... | collective-permute-start | bytes 245768 | tf_op jit(solution)/shard_map/ppermute | solution.py:56
  20.1 6.5 %collective-permute-start = (bf16[64,640]{1,0:T(8,128)(2,1)S(1)}, bf16[64,640]{1,0:T(8,128)(2,1)S(1)}, u32[]{:S(2)}, u32[]{:S(2)}) collective-permute-start(bf16[64,640]{1,0:T(8,128)(2,1)S(1)} %bitcast.25), channel_id=1, source_target_pairs={{0,4},{1,17},{2,6},{3,19},{4,0},{5,21},{6,2},{7,23},{8,12},{9,25},... | collective-permute-start | bytes 245768 | tf_op jit(solution)/shard_map/ppermute | solution.py:56
  22.4 1.2 %copy-start = (bf16[512,1024]{1,0:T(8,128)(2,1)S(1)}, bf16[512,1024]{1,0:T(8,128)(2,1)}, u32[]{:S(2)}) copy-start(bf16[512,1024]{1,0:T(8,128)(2,1)} %refs_3_.3) | copy-start | bytes 3145732
  26.7 5.4 %collective-permute-start.6 = (bf16[256,640]{1,0:T(8,128)(2,1)S(1)}, bf16[256,640]{1,0:T(8,128)(2,1)S(1)}, u32[]{:S(2)}, u32[]{:S(2)}) collective-permute-start(bf16[256,640]{1,0:T(8,128)(2,1)S(1)} %constant_dynamic-update-slice_fusion.refs_0_), channel_id=1, source_target_pairs={{0,1},{1,0},{2,3},{3,2},{4,5},{5,4},{6,7},{7,6},{8,9},{9,8},{10,11... | collective-permute-start | bytes 983048 | tf_op jit(solution)/shard_map/ppermute | solution.py:65
  26.8 18.7 %collective-permute-start.5 = (bf16[256,640]{1,0:T(8,128)(2,1)S(1)}, bf16[256,640]{1,0:T(8,128)(2,1)S(1)}, u32[]{:S(2)}, u32[]{:S(2)}) collective-permute-start(bf16[256,640]{1,0:T(8,128)(2,1)S(1)} %constant_dynamic-update-slice_fusion.refs_0_), channel_id=1, source_target_pairs={{0,24},{1,7},{2,26},{3,1},{4,28},{5,3},{6,30},{7,5},{8,0},{9,15},{... | collective-permute-start | bytes 983048 | tf_op jit(solution)/shard_map/ppermute | solution.py:61
  29.9 15.6 %collective-permute-start.4 = (bf16[256,640]{1,0:T(8,128)(2,1)S(1)}, bf16[256,640]{1,0:T(8,128)(2,1)S(1)}, u32[]{:S(2)}, u32[]{:S(2)}) collective-permute-start(bf16[256,640]{1,0:T(8,128)(2,1)S(1)} %constant_dynamic-update-slice_fusion.refs_0_), channel_id=1, source_target_pairs={{0,8},{1,3},{2,10},{3,5},{4,12},{5,7},{6,14},{7,1},{8,16},{9,11},{... | collective-permute-start | bytes 983048 | tf_op jit(solution)/shard_map/ppermute | solution.py:61
  29.9 15.6 %collective-permute-start.3 = (bf16[256,640]{1,0:T(8,128)(2,1)S(1)}, bf16[256,640]{1,0:T(8,128)(2,1)S(1)}, u32[]{:S(2)}, u32[]{:S(2)}) collective-permute-start(bf16[256,640]{1,0:T(8,128)(2,1)S(1)} %constant_dynamic-update-slice_fusion.refs_0_), channel_id=1, source_target_pairs={{0,16},{1,5},{2,18},{3,7},{4,20},{5,1},{6,22},{7,3},{8,24},{9,13},... | collective-permute-start | bytes 983048 | tf_op jit(solution)/shard_map/ppermute | solution.py:61
  32.8 13.4 %copy-start.1 = (bf16[512,1024]{1,0:T(8,128)(2,1)S(1)}, bf16[512,1024]{1,0:T(8,128)(2,1)}, u32[]{:S(2)}) copy-start(bf16[512,1024]{1,0:T(8,128)(2,1)} %refs_3_.3) | copy-start | bytes 3145732
  45.5 2.4 %collective-permute-start.7 = (bf16[256,640]{1,0:T(8,128)(2,1)S(1)}, bf16[256,640]{1,0:T(8,128)(2,1)S(1)}, u32[]{:S(2)}, u32[]{:S(2)}) collective-permute-start(bf16[256,640]{1,0:T(8,128)(2,1)S(1)} %collective-permute-done.3.refs_0_), channel_id=1, source_target_pairs={{0,1},{1,0},{2,3},{3,2},{4,5},{5,4},{6,7},{7,6},{8,9},{9,8},{10,11... | collective-permute-start | bytes 983048 | tf_op jit(solution)/shard_map/ppermute | solution.py:65
  45.6 2.3 %collective-permute-start.8 = (bf16[256,640]{1,0:T(8,128)(2,1)S(1)}, bf16[256,640]{1,0:T(8,128)(2,1)S(1)}, u32[]{:S(2)}, u32[]{:S(2)}) collective-permute-start(bf16[256,640]{1,0:T(8,128)(2,1)S(1)} %collective-permute-done.4.refs_1_), channel_id=1, source_target_pairs={{0,1},{1,0},{2,3},{3,2},{4,5},{5,4},{6,7},{7,6},{8,9},{9,8},{10,11... | collective-permute-start | bytes 983048 | tf_op jit(solution)/shard_map/ppermute | solution.py:65
  46.1 2.1 %collective-permute-start.9 = (bf16[256,640]{1,0:T(8,128)(2,1)S(1)}, bf16[256,640]{1,0:T(8,128)(2,1)S(1)}, u32[]{:S(2)}, u32[]{:S(2)}) collective-permute-start(bf16[256,640]{1,0:T(8,128)(2,1)S(1)} %collective-permute-done.5.refs_2_), channel_id=1, source_target_pairs={{0,1},{1,0},{2,3},{3,2},{4,5},{5,4},{6,7},{7,6},{8,9},{9,8},{10,11... | collective-permute-start | bytes 983048 | tf_op jit(solution)/shard_map/ppermute | solution.py:65
  47.2 10.2 %collective-permute-start.11 = (bf16[4,4,224,512]{3,2,1,0:T(8,128)(2,1)S(1)}, bf16[4,4,224,512]{3,2,1,0:T(8,128)(2,1)S(1)}, u32[]{:S(2)}, u32[]{:S(2)}) collective-permute-start(bf16[4,4,224,512]{3,2,1,0:T(8,128)(2,1)S(1)} %get-tuple-element.54), channel_id=1, source_target_pairs={{0,1},{1,0},{2,3},{3,2},{4,5},{5,4},{6,7},{7,6},{8,9},{9,8},{10,11... | collective-permute-start | bytes 11010056 | tf_op jit(solution)/shard_map/ppermute | solution.py:65
  55.3 2.0 %collective-permute-start.10 = (bf16[512,512]{1,0:T(8,128)(2,1)S(1)}, bf16[512,512]{1,0:T(8,128)(2,1)S(1)}, u32[]{:S(2)}, u32[]{:S(2)}) collective-permute-start(bf16[512,512]{1,0:T(8,128)(2,1)S(1)} %attend_far.1.att_ref), channel_id=1, source_target_pairs={{0,1},{1,0},{2,3},{3,2},{4,5},{5,4},{6,7},{7,6},{8,9},{9,8},{10,11... | collective-permute-start | bytes 1572872 | tf_op jit(solution)/shard_map/ppermute | solution.py:65
  58.0 9.6 %collective-permute-start.13 = (bf16[2,224,512]{2,1,0:T(8,128)(2,1)S(1)}, bf16[2,224,512]{2,1,0:T(8,128)(2,1)S(1)}, u32[]{:S(2)}, u32[]{:S(2)}) collective-permute-start(bf16[2,224,512]{2,1,0:T(8,128)(2,1)S(1)} %project.8), channel_id=1, source_target_pairs={{0,6},{1,25},{2,0},{3,27},{4,2},{5,29},{6,4},{7,31},{8,14},{9,1},{... | collective-permute-start | bytes 1376264 | tf_op jit(solution)/shard_map/ppermute | solution.py:56
  61.4 9.8 %collective-permute-start.15 = (bf16[2,224,512]{2,1,0:T(8,128)(2,1)S(1)}, bf16[2,224,512]{2,1,0:T(8,128)(2,1)S(1)}, u32[]{:S(2)}, u32[]{:S(2)}) collective-permute-start(bf16[2,224,512]{2,1,0:T(8,128)(2,1)S(1)} %project.14), channel_id=1, source_target_pairs={{0,2},{1,9},{2,4},{3,11},{4,6},{5,13},{6,0},{7,15},{8,10},{9,17},{... | collective-permute-start | bytes 1376264 | tf_op jit(solution)/shard_map/ppermute | solution.py:56
  62.2 13.9 %collective-permute-start.12 = (bf16[2,224,512]{2,1,0:T(8,128)(2,1)S(1)}, bf16[2,224,512]{2,1,0:T(8,128)(2,1)S(1)}, u32[]{:S(2)}, u32[]{:S(2)}) collective-permute-start(bf16[2,224,512]{2,1,0:T(8,128)(2,1)S(1)} %project.10), channel_id=1, source_target_pairs={{0,2},{1,9},{2,4},{3,11},{4,6},{5,13},{6,0},{7,15},{8,10},{9,17},{... | collective-permute-start | bytes 1376264 | tf_op jit(solution)/shard_map/ppermute | solution.py:56
  63.2 16.4 %collective-permute-start.17 = (bf16[2,224,512]{2,1,0:T(8,128)(2,1)S(1)}, bf16[2,224,512]{2,1,0:T(8,128)(2,1)S(1)}, u32[]{:S(2)}, u32[]{:S(2)}) collective-permute-start(bf16[2,224,512]{2,1,0:T(8,128)(2,1)S(1)} %project.15), channel_id=1, source_target_pairs={{0,6},{1,25},{2,0},{3,27},{4,2},{5,29},{6,4},{7,31},{8,14},{9,1},{... | collective-permute-start | bytes 1376264 | tf_op jit(solution)/shard_map/ppermute | solution.py:56
  67.7 9.4 %collective-permute-start.14 = (bf16[2,224,512]{2,1,0:T(8,128)(2,1)S(1)}, bf16[2,224,512]{2,1,0:T(8,128)(2,1)S(1)}, u32[]{:S(2)}, u32[]{:S(2)}) collective-permute-start(bf16[2,224,512]{2,1,0:T(8,128)(2,1)S(1)} %add_convert_fusion.2), channel_id=1, source_target_pairs={{0,6},{1,25},{2,0},{3,27},{4,2},{5,29},{6,4},{7,31},{8,14},{9,1},{... | collective-permute-start | bytes 1376264 | tf_op jit(solution)/shard_map/ppermute | solution.py:56
  71.3 10.0 %collective-permute-start.16 = (bf16[2,224,512]{2,1,0:T(8,128)(2,1)S(1)}, bf16[2,224,512]{2,1,0:T(8,128)(2,1)S(1)}, u32[]{:S(2)}, u32[]{:S(2)}) collective-permute-start(bf16[2,224,512]{2,1,0:T(8,128)(2,1)S(1)} %add_convert_fusion.1), channel_id=1, source_target_pairs={{0,2},{1,9},{2,4},{3,11},{4,6},{5,13},{6,0},{7,15},{8,10},{9,17},{... | collective-permute-start | bytes 1376264 | tf_op jit(solution)/shard_map/ppermute | solution.py:56
  77.2 6.3 %collective-permute-start.20 = (bf16[224,512]{1,0:T(8,128)(2,1)S(1)}, bf16[224,512]{1,0:T(8,128)(2,1)S(1)}, u32[]{:S(2)}, u32[]{:S(2)}) collective-permute-start(bf16[224,512]{1,0:T(8,128)(2,1)S(1)} %fusion.3), channel_id=1, source_target_pairs={{0,24},{1,7},{2,26},{3,1},{4,28},{5,3},{6,30},{7,5},{8,0},{9,15},{... | collective-permute-start | bytes 688136 | tf_op jit(solution)/shard_map/ppermute | solution.py:61
  81.5 7.7 %collective-permute-start.18 = (bf16[224,512]{1,0:T(8,128)(2,1)S(1)}, bf16[224,512]{1,0:T(8,128)(2,1)S(1)}, u32[]{:S(2)}, u32[]{:S(2)}) collective-permute-start(bf16[224,512]{1,0:T(8,128)(2,1)S(1)} %get-tuple-element.57), channel_id=1, source_target_pairs={{0,16},{1,5},{2,18},{3,7},{4,20},{5,1},{6,22},{7,3},{8,24},{9,13},... | collective-permute-start | bytes 688136 | tf_op jit(solution)/shard_map/ppermute | solution.py:61
  82.9 8.7 %collective-permute-start.19 = (bf16[224,512]{1,0:T(8,128)(2,1)S(1)}, bf16[224,512]{1,0:T(8,128)(2,1)S(1)}, u32[]{:S(2)}, u32[]{:S(2)}) collective-permute-start(bf16[224,512]{1,0:T(8,128)(2,1)S(1)} %get-tuple-element.58), channel_id=1, source_target_pairs={{0,8},{1,3},{2,10},{3,5},{4,12},{5,7},{6,14},{7,1},{8,16},{9,11},{... | collective-permute-start | bytes 688136 | tf_op jit(solution)/shard_map/ppermute | solution.py:61

commit v4 on v3

--- a/solution.py
+++ b/solution.py
@@ -141,8 +141,15 @@
     )(place, in_hbm(cached_len), in_hbm(page_loc), in_hbm(latent_pool))
 
 
-def new_kernel(q_ref, lat_ref, w_ref, q_out, kv_out, rope_out):
+def new_kernel(q_in, lat_in, w_in, q_out, kv_out, rope_out, q_ref, lat_ref, w_ref, sems):
+    copies = [
+        pltpu.make_async_copy(source, target, sems.at[k])
+        for k, (source, target) in enumerate([(q_in, q_ref), (lat_in, lat_ref), (w_in, w_ref)])
+    ]
+    for copy in copies:
+        copy.start()
     lane = lax.broadcasted_iota(jnp.int32, (NEW, 128), 1)
+    copies[0].wait()
     for pair in range(HPD // 2):
         two = q_ref[:, 384 * pair : 384 * (pair + 1)].astype(F32)
         for odd in range(2):
@@ -151,13 +158,16 @@
             tail = jnp.where(lane < ROPE, one[:, NOPE : NOPE + 128], jnp.where(lane == ROPE, 1.0, 0.0))
             q_out[:, 256 * head : 256 * head + 128] = one[:, :NOPE].astype(BF)
             q_out[:, 256 * head + 128 : 256 * head + 256] = tail.astype(BF)
+    copies[1].wait()
     rope = jnp.concatenate([lat_ref[KV:, :].astype(F32), jnp.zeros((128 - ROPE, NEW), F32)], 0)
     rope_out[...] = rope.T.astype(BF)
     latent = lat_ref[:KV, :].astype(F32).T.astype(BF)
+    copies[2].wait()
     kv_out[...] = jnp.dot(latent, w_ref[...], preferred_element_type=F32).astype(BF)
 
 
 def new_tokens(queries, latent_t, w_ukv):
+    operands = queries, latent_t, w_ukv
     return pl.pallas_call(
         new_kernel,
         out_shape=[
@@ -165,12 +175,14 @@
             jax.ShapeDtypeStruct((NEW, HPD * 256), BF),
             jax.ShapeDtypeStruct((NEW, 128), BF),
         ],
-        in_specs=[VMEM] * 3,
+        in_specs=[pl.BlockSpec(memory_space=pltpu.HBM)] * 3,
         out_specs=[VMEM] * 3,
+        scratch_shapes=[pltpu.VMEM(operand.shape, BF) for operand in operands]
+        + [pltpu.SemaphoreType.DMA((3,))],
         compiler_params=params(24),
         cost_estimate=SHORT,
         name="new_tokens",
-    )(in_hbm(queries), in_hbm(latent_t), w_ukv)
+    )(*[in_hbm(operand) for operand in operands])
 
 
 def lift_kernel(count, *refs):
@@ -230,54 +242,74 @@
     return jnp.where(key <= row, n, BLOCKED)
 
 
+def columns(h, width):
+    if isinstance(h, int):
+        return slice(h * width, (h + 1) * width)
+    return pl.ds(pl.multiple_of(h * width, width), width)
+
+
 def near_kernel(
-    place, q_ref, kv_ref, rope_ref, kv_new, rope_new, w_ref, sum_ref, top_ref, keep_ref, give_ref, turned
+    place, q_ref, kv_ref, rope_ref, kv_new, rope_new, w_in, sum_ref, top_ref, keep_ref, give_ref, w_ref, turned, sems
 ):
-    def work(exact):
+    head_id = place[1]
+    core = head_id & 1
+    x = lax.shift_right_logical(head_id, 1) & (SIDE - 1)
+    y = lax.shift_right_logical(head_id, 3)
+    width = 2 * SIDE * COLS
+    copies = [
+        pltpu.make_async_copy(
+            w_in.at[:, pl.ds(pl.multiple_of(((y + dy) & (SIDE - 1)) * width, 256), width)],
+            w_ref.at[dy],
+            sems.at[dy],
+        )
+        for dy in range(SIDE)
+    ]
+    for copy in copies:
+        copy.start()
+
+    def work(h, exact):
+        head = columns(h, 256)
+        kv = kv_ref[:, head]
         for half in range(2):
             rows = slice(half * HALF, (half + 1) * HALF)
             count = HALF * (half + 1)
-            q = q_ref[rows, :]
-            n = new_scores(half, q, kv_new, rope_new)
-            top = row_max(n)
-            s = group_scores(q, kv_ref[...], rope_ref[...])
+            q = q_ref[rows, head]
+            new = kv_new[:count, head]
+            n = new_scores(half, q, new, rope_new)
+            s = group_scores(q, kv, rope_ref[...])
             if exact:
-                top = jnp.maximum(top, row_max(s))
-            sum_ref[rows, :] = group_sum(weights_of(s, top), kv_ref[...]) + group_sum(
-                weights_of(n, top), kv_new[:count, :]
-            )
-            top_ref[rows, :] = jnp.broadcast_to(top, (HALF, 128))
-
-    for k in range(2 * SIDE * COLS // 256):
-        turned[256 * k : 256 * (k + 1), :] = w_ref[:, 256 * k : 256 * (k + 1)].T
-    work(False)
-    head_id = place[1]
-    core = head_id & 1
-    x = lax.shift_right_logical(head_id, 1) & (SIDE - 1)
-    dy = pl.program_id(0)
-    for dx in range(SIDE):
-        at = ((x + dx) & (SIDE - 1)) * 2
-        mine = (jnp.where(core == 0, dx, dy), jnp.where(core == 0, dy + 3, dx + 3) & (SIDE - 1))
-        theirs = (jnp.where(core == 0, dy, dx), jnp.where(core == 0, dx + 3, dy + 3) & (SIDE - 1))
-        keep_ref[mine] = turned[pl.ds(pl.multiple_of((at + core) * COLS, 32), COLS), :]
-        give_ref[theirs] = turned[pl.ds(pl.multiple_of((at + 1 - core) * COLS, 32), COLS), :]
-    fine = jnp.max(sum_ref[:, VD:]) < LARGE
-
-    @pl.when(jnp.logical_not(fine))
+                top = jnp.maximum(row_max(n), row_max(s))
+            else:
+                own_keys = jnp.concatenate([new[half * HALF :, :NOPE], rope_new[rows, :]], 1)
+                top = jnp.sum(q.astype(F32) * own_keys.astype(F32), axis=1, keepdims=True)
+            sum_ref[rows, head] = group_sum(weights_of(s, top), kv) + group_sum(weights_of(n, top), new)
+            top_ref[rows, columns(h, 128)] = jnp.broadcast_to(top, (HALF, 128))
+
+    def turn(dy):
+        for k in range(width // 256):
+            turned[256 * k : 256 * (k + 1), :] = w_ref[dy, :, 256 * k : 256 * (k + 1)].T
+        for dx in range(SIDE):
+            at = ((x + dx) & (SIDE - 1)) * 2
+            mine = (jnp.where(core == 0, dx, dy), (jnp.where(core == 0, dy, dx) + 3) & (SIDE - 1))
+            theirs = (jnp.where(core == 0, dy, dx), (jnp.where(core == 0, dx, dy) + 3) & (SIDE - 1))
+            keep_ref[mine] = turned[pl.ds(pl.multiple_of((at + core) * COLS, 32), COLS), :]
+            give_ref[theirs] = turned[pl.ds(pl.multiple_of((at + 1 - core) * COLS, 32), COLS), :]
+
+    for h in range(HPD):
+        work(h, False)
+        copies[h].wait()
+        turn(h)
+
+    worst = functools.reduce(jnp.maximum, [sum_ref[:, 256 * h + VD : 256 * (h + 1)] for h in range(HPD)])
+
+    @pl.when(jnp.logical_not(jnp.max(worst) < LARGE))
     def _():
-        work(True)
+        lax.fori_loop(0, HPD, lambda h, carry: work(h, True), None)
 
 
 def attend_near(place, q_ext, kv, rope, kv_new, rope_new, w_out):
-    head = pl.BlockSpec((NEW, 256), lambda h, s: (0, h))
-    rope_spec = pl.BlockSpec((NEW, 128), lambda h, s: (0, 0))
     rows = HPD * VD
     part = jax.ShapeDtypeStruct((SIDE, SIDE, COLS, rows), BF)
-    whole = pl.BlockSpec((SIDE, SIDE, COLS, rows), lambda h, s: (0, 0, 0, 0))
-
-    def column(h, s):
-        return (0, (lax.shift_right_logical(s[1], 3) + h) & (SIDE - 1))
-
     return pl.pallas_call(
         near_kernel,
         out_shape=[
@@ -286,14 +318,14 @@
             part,
             part,
         ],
-        grid_spec=pltpu.PrefetchScalarGridSpec(
-            num_scalar_prefetch=1,
-            grid=(HPD,),
-            in_specs=[head, head, rope_spec, head, rope_spec, pl.BlockSpec((rows, 2 * SIDE * COLS), column)],
-            out_specs=[head, pl.BlockSpec((NEW, 128), lambda h, s: (0, h)), whole, whole],
-            scratch_shapes=[pltpu.VMEM((2 * SIDE * COLS, rows), BF)],
-        ),
-        compiler_params=params(36),
+        in_specs=[SMEM] + [VMEM] * 5 + [pl.BlockSpec(memory_space=pltpu.HBM)],
+        out_specs=[VMEM] * 4,
+        scratch_shapes=[
+            pltpu.VMEM((SIDE, rows, 2 * SIDE * COLS), BF),
+            pltpu.VMEM((2 * SIDE * COLS, rows), BF),
+            pltpu.SemaphoreType.DMA((SIDE,)),
+        ],
+        compiler_params=params(28),
         cost_estimate=SHORT,
         name="attend_near",
     )(place, q_ext, kv, rope, kv_new, rope_new, in_hbm(w_out))
@@ -301,49 +333,45 @@
 
 def far_kernel(groups, q_ref, sum_ref, top_ref, *refs):
     out_ref, total_ref = refs[-2:]
-    old = top_ref[:, :1]
-
-    def work(exact):
-        q = q_ref[...]
-        scores = [group_scores(q, refs[2 * g][...], refs[2 * g + 1][...]) for g in range(groups)]
-        total = sum_ref[...]
-        top = old
+
+    def work(h, exact):
+        head = columns(h, 256)
+        q = q_ref[:, head]
+        top = top_ref[:, columns(h, 128)][:, :1]
+        total = sum_ref[:, head]
         if exact:
+            scores = [group_scores(q, refs[2 * g][:, head], refs[2 * g + 1][...]) for g in range(groups)]
+            old = top
             top = functools.reduce(jnp.maximum, [row_max(s) for s in scores] + [old])
             total = total * jnp.exp2((old - top) * SCALE)
-        for g, s in enumerate(scores):
-            total = total + group_sum(weights_of(s, top), refs[2 * g][...])
-        total_ref[...] = total
-
-    work(False)
-    fine = jnp.max(total_ref[:, VD:]) < LARGE
-
-    @pl.when(jnp.logical_not(fine))
+        for g in range(groups):
+            kv = refs[2 * g][:, head]
+            s = scores[g] if exact else group_scores(q, kv, refs[2 * g + 1][...])
+            total = total + group_sum(weights_of(s, top), kv)
+        total_ref[:, head] = total
+
+    for h in range(HPD):
+        work(h, False)
+    worst = functools.reduce(jnp.maximum, [total_ref[:, 256 * h + VD : 256 * (h + 1)] for h in range(HPD)])
+
+    @pl.when(jnp.logical_not(jnp.max(worst) < LARGE))
     def _():
-        work(True)
-
-    out_ref[...] = (total_ref[:, :VD] / total_ref[:, VD:]).astype(BF)
+        lax.fori_loop(0, HPD, lambda h, carry: work(h, True), None)
+
+    for h in range(HPD):
+        total = total_ref[:, columns(h, 256)]
+        out_ref[:, columns(h, VD)] = (total[:, :VD] / total[:, VD:]).astype(BF)
 
 
 def attend_far(q_ext, sums, tops, far):
-    specs, operands, keys = [], [], 0
-    for kv, rope in far:
-        rows = kv.shape[0]
-        keys += rows
-        specs += [
-            pl.BlockSpec((rows, 256), lambda h: (0, h)),
-            pl.BlockSpec((rows, 128), lambda h: (0, 0)),
-        ]
-        operands += [kv, rope]
-    head = pl.BlockSpec((NEW, 256), lambda h: (0, h))
+    operands = [array for pair in far for array in pair]
     return pl.pallas_call(
         functools.partial(far_kernel, len(far)),
         out_shape=jax.ShapeDtypeStruct((NEW, HPD * VD), BF),
-        grid=(HPD,),
-        in_specs=[head, head, pl.BlockSpec((NEW, 128), lambda h: (0, h))] + specs,
-        out_specs=pl.BlockSpec((NEW, VD), lambda h: (0, h)),
-        scratch_shapes=[pltpu.VMEM((NEW, 256), F32)],
-        compiler_params=params(20),
+        in_specs=[VMEM] * (3 + len(operands)),
+        out_specs=VMEM,
+        scratch_shapes=[pltpu.VMEM((NEW, HPD * 256), F32)],
+        compiler_params=params(24),
         cost_estimate=LONG,
         name="attend_far",
     )(q_ext, sums, tops, *operands)

time: 92.6 us -> 88.9 us (0.960)
  Pallas kernels: 30.7 us -> 27.5 us
  local copies, waits for them, and re-layouts: 1.32 us -> 0.09 us
  waiting for transfers between devices: 17.3 us -> 18.3 us
    pallas_call x1, Pallas kernels: 6.17 us -> 3.96 us  [attend_far(): pl.pallas_call(functools.partial(far_kernel, len(far)), out_shape=jax.Sha...]
    pallas_call x1, Pallas kernels: 12.6 us -> 11.2 us  [attend_near(): pl.pallas_call(near_kernel, out_shape=[jax.ShapeDtypeStruct((NEW, HPD * 2...]
    unnamed x7 -> x5, local copies, waits for them, and re-layouts: 1.27 us -> 0.04 us
  transfers between devices with their start and end apart: 21 -> 21, of which waited for: 9 -> 9; matrix products, arithmetic and copies ran while one was open for 1% -> 1% of each run, Pallas kernels for 31% -> 28%
where the time goes in v4:
time: 88.9 us; the launch traced here: 88.8 us
  Pallas kernels  27.5 us (31%)
  starting transfers between devices  25.7 us (29%)
  waiting for transfers between devices  18.3 us (21%)
  blocking collectives  15.5 us (17%)
  other arithmetic  1.44 us (2%)
    all_to_all x1, blocking collectives, per_device(): lax.all_to_all(outgoing, 'pool', split_axis=0, concat_axis=0, tiled=True)  15.5 us
    ppermute x9, starting transfers between devices, send_first(): return lax.ppermute(value, PLANE, perm)  14.5 us
    pallas_call x1, Pallas kernels, attend_near(): pl.pallas_call(near_kernel, out_shape=[jax.ShapeDtypeStruct((NEW, HPD * 2...  11.2 us
    ppermute x6, starting transfers between devices, send_second(): return lax.ppermute(value, PLANE, perm)  9.77 us
    ppermute x9, waiting for transfers between devices, send_first(): return lax.ppermute(value, PLANE, perm)  8.1 us
    ppermute x6, waiting for transfers between devices, send_second(): return lax.ppermute(value, PLANE, perm)  8.02 us
    pallas_call x8, Pallas kernels, project(): pl.pallas_call(project_kernel, out_shape=jax.ShapeDtypeStruct((count, COL...  5.35 us
    pallas_call x1, Pallas kernels, attend_far(): pl.pallas_call(functools.partial(far_kernel, len(far)), out_shape=jax.Sha...  3.96 us
  transfers between devices with their start and end apart: 21, of which 9 were waited for; matrix products, arithmetic and copies ran while one was open for 1% of the time, Pallas kernels for 28%

profile of v4, /device:TPU:32, one launch (start us, length us, event | category | flops | bytes accessed | tf_op | source)
XLA Modules:
  0.0 88.8 jit_solution(12177395114545153471)
XLA Ops:
  0.1 1.8 %own_pages.1 = bf16[8,8,640]{2,1,0:T(8,128)(2,1)S(1)} custom-call(s32[2]{0:T(128)S(1)} %pad_add_fusion.place, s32[8]{0:T(128)} %lens_in.1, s32[8,256]{1,0:T(8,128)} %locs_in.1, bf16[16,4608]{1,0:T(8,128)(2,1)} %pool_in.1), custom_call_target="tpu_custom_call" | custom-call | bytes 1024 | tf_op jit(solution)/shard_map/own_pages/pallas_call | solution.py:124
  1.8 15.5 %all_to_all.5 = bf16[8,8,640]{2,1,0:T(8,128)(2,1)S(1)} all-to-all(bf16[8,8,640]{2,1,0:T(8,128)(2,1)S(1)} %own_pages.1), channel_id=1, replica_groups=mesh['pool'=8,'y_hi'=2,'y_lo'=2,'x_hi'=2,'x_lo'=2,'core'=2] {'pool'}, dimensions={0} | all-to-all | bytes 163840 | tf_op jit(solution)/shard_map/all_to_all | solution.py:415
  17.3 2.8 %collective-permute-start.2 = (bf16[64,640]{1,0:T(8,128)(2,1)S(1)}, bf16[64,640]{1,0:T(8,128)(2,1)S(1)}, u32[]{:S(2)}, u32[]{:S(2)}) collective-permute-start(bf16[64,640]{1,0:T(8,128)(2,1)S(1)} %bitcast.23), channel_id=1, source_target_pairs={{0,6},{1,25},{2,0},{3,27},{4,2},{5,29},{6,4},{7,31},{8,14},{9,1},{... | collective-permute-start | bytes 245768 | tf_op jit(solution)/shard_map/ppermute | solution.py:56
  20.1 2.3 %collective-permute-start = (bf16[64,640]{1,0:T(8,128)(2,1)S(1)}, bf16[64,640]{1,0:T(8,128)(2,1)S(1)}, u32[]{:S(2)}, u32[]{:S(2)}) collective-permute-start(bf16[64,640]{1,0:T(8,128)(2,1)S(1)} %bitcast.25), channel_id=1, source_target_pairs={{0,4},{1,17},{2,6},{3,19},{4,0},{5,21},{6,2},{7,23},{8,12},{9,25},... | collective-permute-start | bytes 245768 | tf_op jit(solution)/shard_map/ppermute | solution.py:56
  22.4 2.5 %new_tokens.1 = (bf16[512,1024]{1,0:T(8,128)(2,1)S(1)}, bf16[512,1024]{1,0:T(8,128)(2,1)S(1)}, bf16[512,128]{1,0:T(8,128)(2,1)S(1)}) custom-call(bf16[512,768]{1,0:T(8,128)(2,1)} %q_in.1, bf16[576,512]{1,0:T(8,128)(2,1)} %bitcast.22, bf16[512,1024]{1,0:T(8,128)(2,1)} %refs_3_.3), custom_call_target="tpu_custom_call" | custom-call | bytes 1024 | tf_op jit(solution)/shard_map/new_tokens/pallas_call | solution.py:171
  24.9 1.7 %collective-permute-done.1 = bf16[64,640]{1,0:T(8,128)(2,1)S(1)} collective-permute-done((bf16[64,640]{1,0:T(8,128)(2,1)S(1)}, bf16[64,640]{1,0:T(8,128)(2,1)S(1)}, u32[]{:S(2)}, u32[]{:S(2)}) %collective-permute-start.1) | collective-permute-done | bytes 81952 | tf_op jit(solution)/shard_map/ppermute | solution.py:56
  26.8 3.1 %collective-permute-start.5 = (bf16[256,640]{1,0:T(8,128)(2,1)S(1)}, bf16[256,640]{1,0:T(8,128)(2,1)S(1)}, u32[]{:S(2)}, u32[]{:S(2)}) collective-permute-start(bf16[256,640]{1,0:T(8,128)(2,1)S(1)} %constant_dynamic-update-slice_fusion.refs_0_), channel_id=1, source_target_pairs={{0,24},{1,7},{2,26},{3,1},{4,28},{5,3},{6,30},{7,5},{8,0},{9,15},{... | collective-permute-start | bytes 983048 | tf_op jit(solution)/shard_map/ppermute | solution.py:61
  29.9 2.2 %collective-permute-start.3 = (bf16[256,640]{1,0:T(8,128)(2,1)S(1)}, bf16[256,640]{1,0:T(8,128)(2,1)S(1)}, u32[]{:S(2)}, u32[]{:S(2)}) collective-permute-start(bf16[256,640]{1,0:T(8,128)(2,1)S(1)} %constant_dynamic-update-slice_fusion.refs_0_), channel_id=1, source_target_pairs={{0,16},{1,5},{2,18},{3,7},{4,20},{5,1},{6,22},{7,3},{8,24},{9,13},... | collective-permute-start | bytes 983048 | tf_op jit(solution)/shard_map/ppermute | solution.py:61
  32.8 11.2 %attend_near.1 = (f32[512,1024]{1,0:T(8,128)S(1)}, f32[512,512]{1,0:T(8,128)S(1)}, bf16[4,4,224,512]{3,2,1,0:T(8,128)(2,1)S(1)}, bf16[4,4,224,512]{3,2,1,0:T(8,128)(2,1)S(1)}) custom-call(s32[2]{0:T(128)S(1)} %pad_add_fusion.place, bf16[512,1024]{1,0:T(8,128)(2,1)S(1)} %get-tuple-element.32.q_ref, bf16[512,1024]{1,0:T(8,128)(2,1)S(1)} %get-tuple-element.39.kv_ref, ...), custom_call_target="tpu_custom_call" | custom-call | bytes 1024 | tf_op jit(solution)/shard_map/attend_near/pallas_call | solution.py:313
  44.7 1.0 %lift.4 = (bf16[768,1024]{1,0:T(8,128)(2,1)S(1)}, bf16[768,128]{1,0:T(8,128)(2,1)S(1)}) custom-call(bf16[256,640]{1,0:T(8,128)(2,1)S(1)} %collective-permute-done.3.refs_0_, bf16[256,640]{1,0:T(8,128)(2,1)S(1)} %collective-permute-done.4.refs_1_, bf16[256,640]{1,0:T(8,128)(2,1)S(1)} %collective-permute-done.5.refs_2_, bf16[512,1024]{1,0:T(8,128)(2,1)S(1)} %copy-done), custom_call_target="tpu_custom_call" | custom-call | bytes 1024 | tf_op jit(solution)/shard_map/lift/pallas_call | solution.py:202
  46.7 1.0 %lift.5 = (bf16[768,1024]{1,0:T(8,128)(2,1)S(1)}, bf16[768,128]{1,0:T(8,128)(2,1)S(1)}) custom-call(bf16[256,640]{1,0:T(8,128)(2,1)S(1)} %collective-permute-done.7.refs_0_, bf16[256,640]{1,0:T(8,128)(2,1)S(1)} %collective-permute-done.8.refs_1_, bf16[256,640]{1,0:T(8,128)(2,1)S(1)} %collective-permute-done.9.refs_2_, bf16[512,1024]{1,0:T(8,128)(2,1)S(1)} %copy-done), custom_call_target="tpu_custom_call" | custom-call | bytes 1024 | tf_op jit(solution)/shard_map/lift/pallas_call | solution.py:202
  47.7 4.0 %attend_far.1.att_ref = bf16[512,512]{1,0:T(8,128)(2,1)S(1)} custom-call(bf16[512,1024]{1,0:T(8,128)(2,1)S(1)} %get-tuple-element.32.q_ref, f32[512,1024]{1,0:T(8,128)S(1)} %get-tuple-element.44.sum_ref, f32[512,512]{1,0:T(8,128)S(1)} %get-tuple-element.45.top_ref, bf16[768,1024]{1,0:T(8,128)(2,1)S(1)} %get-tuple-element.49.refs_0_, ...), custom_call_target="tpu_custom_call" | custom-call | flops 99999997952 | bytes 1024 | tf_op jit(solution)/shard_map/attend_far/pallas_call | solution.py:368
  51.9 1.8 %collective-permute-done.10.other_ref = bf16[512,512]{1,0:T(8,128)(2,1)S(1)} collective-permute-done((bf16[512,512]{1,0:T(8,128)(2,1)S(1)}, bf16[512,512]{1,0:T(8,128)(2,1)S(1)}, u32[]{:S(2)}, u32[]{:S(2)}) %collective-permute-start.10) | collective-permute-done | bytes 524320 | tf_op jit(solution)/shard_map/ppermute | solution.py:65
  54.3 3.0 %collective-permute-start.13 = (bf16[2,224,512]{2,1,0:T(8,128)(2,1)S(1)}, bf16[2,224,512]{2,1,0:T(8,128)(2,1)S(1)}, u32[]{:S(2)}, u32[]{:S(2)}) collective-permute-start(bf16[2,224,512]{2,1,0:T(8,128)(2,1)S(1)} %project.8), channel_id=1, source_target_pairs={{0,6},{1,25},{2,0},{3,27},{4,2},{5,29},{6,4},{7,31},{8,14},{9,1},{... | collective-permute-start | bytes 1376264 | tf_op jit(solution)/shard_map/ppermute | solution.py:56
  59.5 3.2 %collective-permute-start.17 = (bf16[2,224,512]{2,1,0:T(8,128)(2,1)S(1)}, bf16[2,224,512]{2,1,0:T(8,128)(2,1)S(1)}, u32[]{:S(2)}, u32[]{:S(2)}) collective-permute-start(bf16[2,224,512]{2,1,0:T(8,128)(2,1)S(1)} %project.15), channel_id=1, source_target_pairs={{0,6},{1,25},{2,0},{3,27},{4,2},{5,29},{6,4},{7,31},{8,14},{9,1},{... | collective-permute-start | bytes 1376264 | tf_op jit(solution)/shard_map/ppermute | solution.py:56
  64.3 2.9 %collective-permute-start.14 = (bf16[2,224,512]{2,1,0:T(8,128)(2,1)S(1)}, bf16[2,224,512]{2,1,0:T(8,128)(2,1)S(1)}, u32[]{:S(2)}, u32[]{:S(2)}) collective-permute-start(bf16[2,224,512]{2,1,0:T(8,128)(2,1)S(1)} %add_convert_fusion.2), channel_id=1, source_target_pairs={{0,6},{1,25},{2,0},{3,27},{4,2},{5,29},{6,4},{7,31},{8,14},{9,1},{... | collective-permute-start | bytes 1376264 | tf_op jit(solution)/shard_map/ppermute | solution.py:56
  69.3 3.4 %collective-permute-done.12 = bf16[2,224,512]{2,1,0:T(8,128)(2,1)S(1)} collective-permute-done((bf16[2,224,512]{2,1,0:T(8,128)(2,1)S(1)}, bf16[2,224,512]{2,1,0:T(8,128)(2,1)S(1)}, u32[]{:S(2)}, u32[]{:S(2)}) %collective-permute-start.12) | collective-permute-done | bytes 458784 | tf_op jit(solution)/shard_map/ppermute | solution.py:56
  72.6 1.1 %collective-permute-done.14 = bf16[2,224,512]{2,1,0:T(8,128)(2,1)S(1)} collective-permute-done((bf16[2,224,512]{2,1,0:T(8,128)(2,1)S(1)}, bf16[2,224,512]{2,1,0:T(8,128)(2,1)S(1)}, u32[]{:S(2)}, u32[]{:S(2)}) %collective-permute-start.14) | collective-permute-done | bytes 458784 | tf_op jit(solution)/shard_map/ppermute | solution.py:56
  73.8 2.4 %collective-permute-start.20 = (bf16[224,512]{1,0:T(8,128)(2,1)S(1)}, bf16[224,512]{1,0:T(8,128)(2,1)S(1)}, u32[]{:S(2)}, u32[]{:S(2)}) collective-permute-start(bf16[224,512]{1,0:T(8,128)(2,1)S(1)} %fusion.3), channel_id=1, source_target_pairs={{0,24},{1,7},{2,26},{3,1},{4,28},{5,3},{6,30},{7,5},{8,0},{9,15},{... | collective-permute-start | bytes 688136 | tf_op jit(solution)/shard_map/ppermute | solution.py:61
  76.2 1.4 %collective-permute-done.16 = bf16[2,224,512]{2,1,0:T(8,128)(2,1)S(1)} collective-permute-done((bf16[2,224,512]{2,1,0:T(8,128)(2,1)S(1)}, bf16[2,224,512]{2,1,0:T(8,128)(2,1)S(1)}, u32[]{:S(2)}, u32[]{:S(2)}) %collective-permute-start.16) | collective-permute-done | bytes 458784 | tf_op jit(solution)/shard_map/ppermute | solution.py:56
  77.8 1.4 %collective-permute-start.18 = (bf16[224,512]{1,0:T(8,128)(2,1)S(1)}, bf16[224,512]{1,0:T(8,128)(2,1)S(1)}, u32[]{:S(2)}, u32[]{:S(2)}) collective-permute-start(bf16[224,512]{1,0:T(8,128)(2,1)S(1)} %get-tuple-element.57), channel_id=1, source_target_pairs={{0,16},{1,5},{2,18},{3,7},{4,20},{5,1},{6,22},{7,3},{8,24},{9,13},... | collective-permute-start | bytes 688136 | tf_op jit(solution)/shard_map/ppermute | solution.py:61
  79.9 5.7 %collective-permute-done.18 = bf16[224,512]{1,0:T(8,128)(2,1)S(1)} collective-permute-done((bf16[224,512]{1,0:T(8,128)(2,1)S(1)}, bf16[224,512]{1,0:T(8,128)(2,1)S(1)}, u32[]{:S(2)}, u32[]{:S(2)}) %collective-permute-start.18) | collective-permute-done | bytes 229408 | tf_op jit(solution)/shard_map/ppermute | solution.py:61
  85.6 2.4 %collective-permute-done.19 = bf16[224,512]{1,0:T(8,128)(2,1)S(1)} collective-permute-done((bf16[224,512]{1,0:T(8,128)(2,1)S(1)}, bf16[224,512]{1,0:T(8,128)(2,1)S(1)}, u32[]{:S(2)}, u32[]{:S(2)}) %collective-permute-start.19) | collective-permute-done | bytes 229408 | tf_op jit(solution)/shard_map/ppermute | solution.py:61
  87.9 0.9 fusion.4
  (47 shorter events, 10.2 us)
Async XLA Ops:
  0.0 32.1 %copy-start = (bf16[512,1024]{1,0:T(8,128)(2,1)S(1)}, bf16[512,1024]{1,0:T(8,128)(2,1)}, u32[]{:S(2)}) copy-start(bf16[512,1024]{1,0:T(8,128)(2,1)} %refs_3_.3) | copy-start | bytes 3145732
  17.3 7.6 %collective-permute-start.2 = (bf16[64,640]{1,0:T(8,128)(2,1)S(1)}, bf16[64,640]{1,0:T(8,128)(2,1)S(1)}, u32[]{:S(2)}, u32[]{:S(2)}) collective-permute-start(bf16[64,640]{1,0:T(8,128)(2,1)S(1)} %bitcast.23), channel_id=1, source_target_pairs={{0,6},{1,25},{2,0},{3,27},{4,2},{5,29},{6,4},{7,31},{8,14},{9,1},{... | collective-permute-start | bytes 245768 | tf_op jit(solution)/shard_map/ppermute | solution.py:56
  20.1 6.5 %collective-permute-start.1 = (bf16[64,640]{1,0:T(8,128)(2,1)S(1)}, bf16[64,640]{1,0:T(8,128)(2,1)S(1)}, u32[]{:S(2)}, u32[]{:S(2)}) collective-permute-start(bf16[64,640]{1,0:T(8,128)(2,1)S(1)} %bitcast.24), channel_id=1, source_target_pairs={{0,2},{1,9},{2,4},{3,11},{4,6},{5,13},{6,0},{7,15},{8,10},{9,17},{... | collective-permute-start | bytes 245768 | tf_op jit(solution)/shard_map/ppermute | solution.py:56
  20.1 6.5 %collective-permute-start = (bf16[64,640]{1,0:T(8,128)(2,1)S(1)}, bf16[64,640]{1,0:T(8,128)(2,1)S(1)}, u32[]{:S(2)}, u32[]{:S(2)}) collective-permute-start(bf16[64,640]{1,0:T(8,128)(2,1)S(1)} %bitcast.25), channel_id=1, source_target_pairs={{0,4},{1,17},{2,6},{3,19},{4,0},{5,21},{6,2},{7,23},{8,12},{9,25},... | collective-permute-start | bytes 245768 | tf_op jit(solution)/shard_map/ppermute | solution.py:56
  26.7 5.4 %collective-permute-start.6 = (bf16[256,640]{1,0:T(8,128)(2,1)S(1)}, bf16[256,640]{1,0:T(8,128)(2,1)S(1)}, u32[]{:S(2)}, u32[]{:S(2)}) collective-permute-start(bf16[256,640]{1,0:T(8,128)(2,1)S(1)} %constant_dynamic-update-slice_fusion.refs_0_), channel_id=1, source_target_pairs={{0,1},{1,0},{2,3},{3,2},{4,5},{5,4},{6,7},{7,6},{8,9},{9,8},{10,11... | collective-permute-start | bytes 983048 | tf_op jit(solution)/shard_map/ppermute | solution.py:65
  26.8 17.2 %collective-permute-start.5 = (bf16[256,640]{1,0:T(8,128)(2,1)S(1)}, bf16[256,640]{1,0:T(8,128)(2,1)S(1)}, u32[]{:S(2)}, u32[]{:S(2)}) collective-permute-start(bf16[256,640]{1,0:T(8,128)(2,1)S(1)} %constant_dynamic-update-slice_fusion.refs_0_), channel_id=1, source_target_pairs={{0,24},{1,7},{2,26},{3,1},{4,28},{5,3},{6,30},{7,5},{8,0},{9,15},{... | collective-permute-start | bytes 983048 | tf_op jit(solution)/shard_map/ppermute | solution.py:61
  29.9 14.1 %collective-permute-start.4 = (bf16[256,640]{1,0:T(8,128)(2,1)S(1)}, bf16[256,640]{1,0:T(8,128)(2,1)S(1)}, u32[]{:S(2)}, u32[]{:S(2)}) collective-permute-start(bf16[256,640]{1,0:T(8,128)(2,1)S(1)} %constant_dynamic-update-slice_fusion.refs_0_), channel_id=1, source_target_pairs={{0,8},{1,3},{2,10},{3,5},{4,12},{5,7},{6,14},{7,1},{8,16},{9,11},{... | collective-permute-start | bytes 983048 | tf_op jit(solution)/shard_map/ppermute | solution.py:61
  29.9 14.2 %collective-permute-start.3 = (bf16[256,640]{1,0:T(8,128)(2,1)S(1)}, bf16[256,640]{1,0:T(8,128)(2,1)S(1)}, u32[]{:S(2)}, u32[]{:S(2)}) collective-permute-start(bf16[256,640]{1,0:T(8,128)(2,1)S(1)} %constant_dynamic-update-slice_fusion.refs_0_), channel_id=1, source_target_pairs={{0,16},{1,5},{2,18},{3,7},{4,20},{5,1},{6,22},{7,3},{8,24},{9,13},... | collective-permute-start | bytes 983048 | tf_op jit(solution)/shard_map/ppermute | solution.py:61
  44.0 2.2 %collective-permute-start.7 = (bf16[256,640]{1,0:T(8,128)(2,1)S(1)}, bf16[256,640]{1,0:T(8,128)(2,1)S(1)}, u32[]{:S(2)}, u32[]{:S(2)}) collective-permute-start(bf16[256,640]{1,0:T(8,128)(2,1)S(1)} %collective-permute-done.3.refs_0_), channel_id=1, source_target_pairs={{0,1},{1,0},{2,3},{3,2},{4,5},{5,4},{6,7},{7,6},{8,9},{9,8},{10,11... | collective-permute-start | bytes 983048 | tf_op jit(solution)/shard_map/ppermute | solution.py:65
  44.1 2.1 %collective-permute-start.8 = (bf16[256,640]{1,0:T(8,128)(2,1)S(1)}, bf16[256,640]{1,0:T(8,128)(2,1)S(1)}, u32[]{:S(2)}, u32[]{:S(2)}) collective-permute-start(bf16[256,640]{1,0:T(8,128)(2,1)S(1)} %collective-permute-done.4.refs_1_), channel_id=1, source_target_pairs={{0,1},{1,0},{2,3},{3,2},{4,5},{5,4},{6,7},{7,6},{8,9},{9,8},{10,11... | collective-permute-start | bytes 983048 | tf_op jit(solution)/shard_map/ppermute | solution.py:65
  44.6 2.1 %collective-permute-start.9 = (bf16[256,640]{1,0:T(8,128)(2,1)S(1)}, bf16[256,640]{1,0:T(8,128)(2,1)S(1)}, u32[]{:S(2)}, u32[]{:S(2)}) collective-permute-start(bf16[256,640]{1,0:T(8,128)(2,1)S(1)} %collective-permute-done.5.refs_2_), channel_id=1, source_target_pairs={{0,1},{1,0},{2,3},{3,2},{4,5},{5,4},{6,7},{7,6},{8,9},{9,8},{10,11... | collective-permute-start | bytes 983048 | tf_op jit(solution)/shard_map/ppermute | solution.py:65
  45.8 7.9 %collective-permute-start.11 = (bf16[4,4,224,512]{3,2,1,0:T(8,128)(2,1)S(1)}, bf16[4,4,224,512]{3,2,1,0:T(8,128)(2,1)S(1)}, u32[]{:S(2)}, u32[]{:S(2)}) collective-permute-start(bf16[4,4,224,512]{3,2,1,0:T(8,128)(2,1)S(1)} %get-tuple-element.54), channel_id=1, source_target_pairs={{0,1},{1,0},{2,3},{3,2},{4,5},{5,4},{6,7},{7,6},{8,9},{9,8},{10,11... | collective-permute-start | bytes 11010056 | tf_op jit(solution)/shard_map/ppermute | solution.py:65
  51.6 2.0 %collective-permute-start.10 = (bf16[512,512]{1,0:T(8,128)(2,1)S(1)}, bf16[512,512]{1,0:T(8,128)(2,1)S(1)}, u32[]{:S(2)}, u32[]{:S(2)}) collective-permute-start(bf16[512,512]{1,0:T(8,128)(2,1)S(1)} %attend_far.1.att_ref), channel_id=1, source_target_pairs={{0,1},{1,0},{2,3},{3,2},{4,5},{5,4},{6,7},{7,6},{8,9},{9,8},{10,11... | collective-permute-start | bytes 1572872 | tf_op jit(solution)/shard_map/ppermute | solution.py:65
  54.3 9.8 %collective-permute-start.13 = (bf16[2,224,512]{2,1,0:T(8,128)(2,1)S(1)}, bf16[2,224,512]{2,1,0:T(8,128)(2,1)S(1)}, u32[]{:S(2)}, u32[]{:S(2)}) collective-permute-start(bf16[2,224,512]{2,1,0:T(8,128)(2,1)S(1)} %project.8), channel_id=1, source_target_pairs={{0,6},{1,25},{2,0},{3,27},{4,2},{5,29},{6,4},{7,31},{8,14},{9,1},{... | collective-permute-start | bytes 1376264 | tf_op jit(solution)/shard_map/ppermute | solution.py:56
  58.0 9.8 %collective-permute-start.15 = (bf16[2,224,512]{2,1,0:T(8,128)(2,1)S(1)}, bf16[2,224,512]{2,1,0:T(8,128)(2,1)S(1)}, u32[]{:S(2)}, u32[]{:S(2)}) collective-permute-start(bf16[2,224,512]{2,1,0:T(8,128)(2,1)S(1)} %project.14), channel_id=1, source_target_pairs={{0,2},{1,9},{2,4},{3,11},{4,6},{5,13},{6,0},{7,15},{8,10},{9,17},{... | collective-permute-start | bytes 1376264 | tf_op jit(solution)/shard_map/ppermute | solution.py:56
  58.7 13.9 %collective-permute-start.12 = (bf16[2,224,512]{2,1,0:T(8,128)(2,1)S(1)}, bf16[2,224,512]{2,1,0:T(8,128)(2,1)S(1)}, u32[]{:S(2)}, u32[]{:S(2)}) collective-permute-start(bf16[2,224,512]{2,1,0:T(8,128)(2,1)S(1)} %project.10), channel_id=1, source_target_pairs={{0,2},{1,9},{2,4},{3,11},{4,6},{5,13},{6,0},{7,15},{8,10},{9,17},{... | collective-permute-start | bytes 1376264 | tf_op jit(solution)/shard_map/ppermute | solution.py:56
  59.5 16.7 %collective-permute-start.17 = (bf16[2,224,512]{2,1,0:T(8,128)(2,1)S(1)}, bf16[2,224,512]{2,1,0:T(8,128)(2,1)S(1)}, u32[]{:S(2)}, u32[]{:S(2)}) collective-permute-start(bf16[2,224,512]{2,1,0:T(8,128)(2,1)S(1)} %project.15), channel_id=1, source_target_pairs={{0,6},{1,25},{2,0},{3,27},{4,2},{5,29},{6,4},{7,31},{8,14},{9,1},{... | collective-permute-start | bytes 1376264 | tf_op jit(solution)/shard_map/ppermute | solution.py:56
  64.3 9.4 %collective-permute-start.14 = (bf16[2,224,512]{2,1,0:T(8,128)(2,1)S(1)}, bf16[2,224,512]{2,1,0:T(8,128)(2,1)S(1)}, u32[]{:S(2)}, u32[]{:S(2)}) collective-permute-start(bf16[2,224,512]{2,1,0:T(8,128)(2,1)S(1)} %add_convert_fusion.2), channel_id=1, source_target_pairs={{0,6},{1,25},{2,0},{3,27},{4,2},{5,29},{6,4},{7,31},{8,14},{9,1},{... | collective-permute-start | bytes 1376264 | tf_op jit(solution)/shard_map/ppermute | solution.py:56
  67.8 9.8 %collective-permute-start.16 = (bf16[2,224,512]{2,1,0:T(8,128)(2,1)S(1)}, bf16[2,224,512]{2,1,0:T(8,128)(2,1)S(1)}, u32[]{:S(2)}, u32[]{:S(2)}) collective-permute-start(bf16[2,224,512]{2,1,0:T(8,128)(2,1)S(1)} %add_convert_fusion.1), channel_id=1, source_target_pairs={{0,2},{1,9},{2,4},{3,11},{4,6},{5,13},{6,0},{7,15},{8,10},{9,17},{... | collective-permute-start | bytes 1376264 | tf_op jit(solution)/shard_map/ppermute | solution.py:56
  73.8 6.1 %collective-permute-start.20 = (bf16[224,512]{1,0:T(8,128)(2,1)S(1)}, bf16[224,512]{1,0:T(8,128)(2,1)S(1)}, u32[]{:S(2)}, u32[]{:S(2)}) collective-permute-start(bf16[224,512]{1,0:T(8,128)(2,1)S(1)} %fusion.3), channel_id=1, source_target_pairs={{0,24},{1,7},{2,26},{3,1},{4,28},{5,3},{6,30},{7,5},{8,0},{9,15},{... | collective-permute-start | bytes 688136 | tf_op jit(solution)/shard_map/ppermute | solution.py:61
  77.8 7.7 %collective-permute-start.18 = (bf16[224,512]{1,0:T(8,128)(2,1)S(1)}, bf16[224,512]{1,0:T(8,128)(2,1)S(1)}, u32[]{:S(2)}, u32[]{:S(2)}) collective-permute-start(bf16[224,512]{1,0:T(8,128)(2,1)S(1)} %get-tuple-element.57), channel_id=1, source_target_pairs={{0,16},{1,5},{2,18},{3,7},{4,20},{5,1},{6,22},{7,3},{8,24},{9,13},... | collective-permute-start | bytes 688136 | tf_op jit(solution)/shard_map/ppermute | solution.py:61
  79.2 8.7 %collective-permute-start.19 = (bf16[224,512]{1,0:T(8,128)(2,1)S(1)}, bf16[224,512]{1,0:T(8,128)(2,1)S(1)}, u32[]{:S(2)}, u32[]{:S(2)}) collective-permute-start(bf16[224,512]{1,0:T(8,128)(2,1)S(1)} %get-tuple-element.58), channel_id=1, source_target_pairs={{0,8},{1,3},{2,10},{3,5},{4,12},{5,7},{6,14},{7,1},{8,16},{9,11},{... | collective-permute-start | bytes 688136 | tf_op jit(solution)/shard_map/ppermute | solution.py:61

commit v5 on v4

--- a/solution.py
+++ b/solution.py
@@ -185,15 +185,15 @@
     )(*[in_hbm(operand) for operand in operands])
 
 
+def lift_into(pieces, w_ref, kv_ref, rope_ref):
+    for i, piece in enumerate(pieces):
+        rows = slice(piece.shape[0] * i, piece.shape[0] * (i + 1))
+        kv_ref[rows, :] = jnp.dot(piece[:, :KV], w_ref[...], preferred_element_type=F32).astype(BF)
+        rope_ref[rows, :] = piece[:, KV:]
+
+
 def lift_kernel(count, *refs):
-    w_ref = refs[count]
-    kv_out, rope_out = refs[count + 1 :]
-    for i in range(count):
-        rows = refs[i].shape[0]
-        kv_out[rows * i : rows * (i + 1), :] = jnp.dot(
-            refs[i][:, :KV], w_ref[...], preferred_element_type=F32
-        ).astype(BF)
-        rope_out[rows * i : rows * (i + 1), :] = refs[i][:, KV:]
+    lift_into(refs[:count], *refs[count:])
 
 
 def lift(pieces, w_ukv):
@@ -249,7 +249,9 @@
 
 
 def near_kernel(
-    place, q_ref, kv_ref, rope_ref, kv_new, rope_new, w_in, sum_ref, top_ref, keep_ref, give_ref, w_ref, turned, sems
+    place, q_ref, line_ref, other_ref, up_ref, kv_new, rope_new, w_in,
+    sum_ref, top_ref, keep_ref, give_ref,
+    kv_ref, rope_ref, w_ref, turned, sems,
 ):
     head_id = place[1]
     core = head_id & 1
@@ -266,6 +268,7 @@
     ]
     for copy in copies:
         copy.start()
+    lift_into((line_ref, other_ref), up_ref, kv_ref, rope_ref)
 
     def work(h, exact):
         head = columns(h, 256)
@@ -307,7 +310,7 @@
         lax.fori_loop(0, HPD, lambda h, carry: work(h, True), None)
 
 
-def attend_near(place, q_ext, kv, rope, kv_new, rope_new, w_out):
+def attend_near(place, q_ext, line, other, w_ukv, kv_new, rope_new, w_out):
     rows = HPD * VD
     part = jax.ShapeDtypeStruct((SIDE, SIDE, COLS, rows), BF)
     return pl.pallas_call(
@@ -318,9 +321,11 @@
             part,
             part,
         ],
-        in_specs=[SMEM] + [VMEM] * 5 + [pl.BlockSpec(memory_space=pltpu.HBM)],
+        in_specs=[SMEM] + [VMEM] * 6 + [pl.BlockSpec(memory_space=pltpu.HBM)],
         out_specs=[VMEM] * 4,
         scratch_shapes=[
+            pltpu.VMEM((2 * line.shape[0], HPD * 256), BF),
+            pltpu.VMEM((2 * line.shape[0], 128), BF),
             pltpu.VMEM((SIDE, rows, 2 * SIDE * COLS), BF),
             pltpu.VMEM((2 * SIDE * COLS, rows), BF),
             pltpu.SemaphoreType.DMA((SIDE,)),
@@ -328,11 +333,14 @@
         compiler_params=params(28),
         cost_estimate=SHORT,
         name="attend_near",
-    )(place, q_ext, kv, rope, kv_new, rope_new, in_hbm(w_out))
-
-
-def far_kernel(groups, q_ref, sum_ref, top_ref, *refs):
-    out_ref, total_ref = refs[-2:]
+    )(place, q_ext, line, other, w_ukv, kv_new, rope_new, in_hbm(w_out))
+
+
+def far_kernel(
+    q_ref, sum_ref, top_ref, kv_ref, rope_ref, up_ref, piece_0, piece_1, piece_2, out_ref, total_ref, kv_more, rope_more
+):
+    lift_into((piece_0, piece_1, piece_2), up_ref, kv_more, rope_more)
+    groups = (kv_ref, rope_ref), (kv_more, rope_more)
 
     def work(h, exact):
         head = columns(h, 256)
@@ -340,14 +348,13 @@
         top = top_ref[:, columns(h, 128)][:, :1]
         total = sum_ref[:, head]
         if exact:
-            scores = [group_scores(q, refs[2 * g][:, head], refs[2 * g + 1][...]) for g in range(groups)]
+            scores = [group_scores(q, kv[:, head], rope[...]) for kv, rope in groups]
             old = top
             top = functools.reduce(jnp.maximum, [row_max(s) for s in scores] + [old])
             total = total * jnp.exp2((old - top) * SCALE)
-        for g in range(groups):
-            kv = refs[2 * g][:, head]
-            s = scores[g] if exact else group_scores(q, kv, refs[2 * g + 1][...])
-            total = total + group_sum(weights_of(s, top), kv)
+        for g, (kv, rope) in enumerate(groups):
+            s = scores[g] if exact else group_scores(q, kv[:, head], rope[...])
+            total = total + group_sum(weights_of(s, top), kv[:, head])
         total_ref[:, head] = total
 
     for h in range(HPD):
@@ -363,39 +370,40 @@
         out_ref[:, columns(h, VD)] = (total[:, :VD] / total[:, VD:]).astype(BF)
 
 
-def attend_far(q_ext, sums, tops, far):
-    operands = [array for pair in far for array in pair]
-    return pl.pallas_call(
-        functools.partial(far_kernel, len(far)),
+def attend_far(q_ext, sums, tops, kv, rope, w_ukv, pieces):
+    return pl.pallas_call(
+        far_kernel,
         out_shape=jax.ShapeDtypeStruct((NEW, HPD * VD), BF),
-        in_specs=[VMEM] * (3 + len(operands)),
+        in_specs=[VMEM] * (6 + len(pieces)),
         out_specs=VMEM,
-        scratch_shapes=[pltpu.VMEM((NEW, HPD * 256), F32)],
+        scratch_shapes=[
+            pltpu.VMEM((NEW, HPD * 256), F32),
+            pltpu.VMEM(kv.shape, BF),
+            pltpu.VMEM(rope.shape, BF),
+        ],
         compiler_params=params(24),
         cost_estimate=LONG,
         name="attend_far",
-    )(q_ext, sums, tops, *operands)
-
-
-def project_kernel(att_ref, other_ref, keep_ref, got_ref, out_ref):
-    rows = out_ref.shape[0] * COLS
+    )(q_ext, sums, tops, kv, rope, w_ukv, *pieces)
+
+
+def project_kernel(a, half, att_ref, other_ref, keep_ref, got_ref, out_ref):
+    rows = 2 * COLS
+    blocks = slice(2 * half, 2 * half + 2)
     out = lax.dot_general(
-        keep_ref[...].reshape(rows, HPD * VD), att_ref[...], NT, preferred_element_type=F32
+        keep_ref[a, blocks].reshape(rows, HPD * VD), att_ref[...], NT, preferred_element_type=F32
     ) + lax.dot_general(
-        got_ref[...].reshape(rows, HPD * VD), other_ref[...], NT, preferred_element_type=F32
+        got_ref[a, blocks].reshape(rows, HPD * VD), other_ref[...], NT, preferred_element_type=F32
     )
     out_ref[...] = out.reshape(out_ref.shape).astype(BF)
 
 
-def project(a, first, count, att, other, keep, got):
-    spec = pl.BlockSpec((1, count, COLS, HPD * VD), lambda i: (a, first // count, 0, 0))
-    whole = pl.BlockSpec((NEW, HPD * VD), lambda i: (0, 0))
-    return pl.pallas_call(
-        project_kernel,
-        out_shape=jax.ShapeDtypeStruct((count, COLS, NEW), BF),
-        grid=(1,),
-        in_specs=[whole, whole, spec, spec],
-        out_specs=pl.BlockSpec((count, COLS, NEW), lambda i: (0, 0, 0)),
+def project(a, half, att, other, keep, got):
+    return pl.pallas_call(
+        functools.partial(project_kernel, a, half),
+        out_shape=jax.ShapeDtypeStruct((2, COLS, NEW), BF),
+        in_specs=[VMEM] * 4,
+        out_specs=VMEM,
         compiler_params=params(16),
         cost_estimate=SHORT,
         name="project",
@@ -420,28 +428,25 @@
     *line, kv_new = lax.optimization_barrier((*line, kv_new))
     line = jnp.concatenate(line, 0)
     pieces = [send_second(line, d) for d in (2, 1, -1)]
-    near = lift([line, swap(line)], w_ukv)
-    sums, tops, keep, give = attend_near(place, q_ext, *near, kv_new, rope_new, w_out)
+    sums, tops, keep, give = attend_near(place, q_ext, line, swap(line), w_ukv, kv_new, rope_new, w_out)
     got = swap(give)
     *pieces, sums = lax.optimization_barrier((*pieces, sums))
-    far = [lift(pieces, w_ukv), lift([swap(piece) for piece in pieces], w_ukv)]
-    att = attend_far(q_ext, sums, tops, far)
+    swapped = [swap(piece) for piece in pieces]
+    att = attend_far(q_ext, sums, tops, *lift(pieces, w_ukv), w_ukv, swapped)
     other = swap(att)
     def partial_sums(a, half):
-        return project(a, 2 * half, 2, att, other, keep, got)
-
-    far_parts = [partial_sums(2, half) for half in range(2)]
+        return project(a, half, att, other, keep, got)
+
+    far_parts = [partial_sums(2, half) for half in (1, 0)]
     att, far_parts[1] = lax.optimization_barrier((att, far_parts[1]))
-    passing = send_first(far_parts[0], 1), send_first(far_parts[1], -1)
-    early = send_first(partial_sums(1, 1), 1), send_first(partial_sums(3, 0), -1)
-    late = (
-        send_first(add(partial_sums(1, 0), passing[0]), 1),
-        send_first(add(partial_sums(3, 1), passing[1]), -1),
-    )
-    one, two = add(partial_sums(0, 0), late[0], early[1])
-    rest = partial_sums(0, 1), early[0], late[1]
+    high, low = send_first(far_parts[0], -1), send_first(far_parts[1], 1)
+    early_down, early_up = send_first(partial_sums(3, 0), -1), send_first(partial_sums(1, 1), 1)
+    late_down = send_first(add(partial_sums(3, 1), high), -1)
+    late_up = send_first(add(partial_sums(1, 0), low), 1)
+    rest = partial_sums(0, 1), early_up, late_down
     three = add(*[value[0] for value in rest])
-    moved = [send_second(two, 2), send_second(one, 1), send_second(three, -1)]
+    one, two = add(partial_sums(0, 0), late_up, early_down)
+    moved = [send_second(three, -1), send_second(two, 2), send_second(one, 1)]
     out = add(*[value[1] for value in rest], *moved)
     return out.T
 

time: 88.9 us -> 89.8 us (1.010)
  waiting for transfers between devices: 18.3 us -> 20.1 us
    ppermute x6, starting transfers between devices: 9.77 us -> 7.53 us  [send_second(): return lax.ppermute(value, PLANE, perm)]
    pallas_call x3 -> x1, Pallas kernels: 2.73 us -> 1.01 us  [lift(): pl.pallas_call(functools.partial(lift_kernel, count), out_shape=[jax.Shap...]
    ppermute x9, starting transfers between devices: 14.5 us -> 15.9 us  [send_first(): return lax.ppermute(value, PLANE, perm)]
    pallas_call x9, Pallas kernels: 9.31 us -> 10.3 us  [the longest x8 5.36 us: project(): pl.pallas_call(functools.partial(project_kernel, a, half), out_shape=jax....]
    ppermute x6, waiting for transfers between devices: 8.02 us -> 8.94 us  [send_second(): return lax.ppermute(value, PLANE, perm)]
where the time goes in v5:
time: 89.8 us; the launch traced here: 89.6 us
  Pallas kernels  27.2 us (30%)
  starting transfers between devices  25.1 us (28%)
  waiting for transfers between devices  20.1 us (22%)
  blocking collectives  15.5 us (17%)
  other arithmetic  1.44 us (2%)
    ppermute x9, starting transfers between devices, send_first(): return lax.ppermute(value, PLANE, perm)  15.9 us
    all_to_all x1, blocking collectives, per_device(): lax.all_to_all(outgoing, 'pool', split_axis=0, concat_axis=0, tiled=True)  15.5 us
    pallas_call x1, Pallas kernels, attend_near(): pl.pallas_call(near_kernel, out_shape=[jax.ShapeDtypeStruct((NEW, HPD * 2...  11.6 us
    ppermute x6, waiting for transfers between devices, send_second(): return lax.ppermute(value, PLANE, perm)  8.94 us
    ppermute x9, waiting for transfers between devices, send_first(): return lax.ppermute(value, PLANE, perm)  8.92 us
    ppermute x6, starting transfers between devices, send_second(): return lax.ppermute(value, PLANE, perm)  7.53 us
    pallas_call x8, Pallas kernels, project(): pl.pallas_call(functools.partial(project_kernel, a, half), out_shape=jax....  5.36 us
    pallas_call x1, Pallas kernels, attend_far(): pl.pallas_call(far_kernel, out_shape=jax.ShapeDtypeStruct((NEW, HPD * VD)...  4.92 us
  transfers between devices with their start and end apart: 21, of which 9 were waited for; matrix products, arithmetic and copies ran while one was open for 1% of the time, Pallas kernels for 28%

profile of v5, /device:TPU:32, one launch (start us, length us, event | category | flops | bytes accessed | tf_op | source)
XLA Modules:
  0.0 89.6 jit_solution(12628640883895104537)
XLA Ops:
  0.1 1.8 %own_pages.1 = bf16[8,8,640]{2,1,0:T(8,128)(2,1)S(1)} custom-call(s32[2]{0:T(128)S(1)} %pad_add_fusion.place, s32[8]{0:T(128)} %lens_in.1, s32[8,256]{1,0:T(8,128)} %locs_in.1, bf16[16,4608]{1,0:T(8,128)(2,1)} %pool_in.1), custom_call_target="tpu_custom_call" | custom-call | bytes 1024 | tf_op jit(solution)/shard_map/own_pages/pallas_call | solution.py:124
  1.8 15.5 %all_to_all.5 = bf16[8,8,640]{2,1,0:T(8,128)(2,1)S(1)} all-to-all(bf16[8,8,640]{2,1,0:T(8,128)(2,1)S(1)} %own_pages.1), channel_id=1, replica_groups=mesh['pool'=8,'y_hi'=2,'y_lo'=2,'x_hi'=2,'x_lo'=2,'core'=2] {'pool'}, dimensions={0} | all-to-all | bytes 163840 | tf_op jit(solution)/shard_map/all_to_all | solution.py:423
  17.3 3.0 %collective-permute-start = (bf16[64,640]{1,0:T(8,128)(2,1)S(1)}, bf16[64,640]{1,0:T(8,128)(2,1)S(1)}, u32[]{:S(2)}, u32[]{:S(2)}) collective-permute-start(bf16[64,640]{1,0:T(8,128)(2,1)S(1)} %bitcast.23), channel_id=1, source_target_pairs={{0,4},{1,17},{2,6},{3,19},{4,0},{5,21},{6,2},{7,23},{8,12},{9,25},... | collective-permute-start | bytes 245768 | tf_op jit(solution)/shard_map/ppermute | solution.py:56
  20.9 2.6 %collective-permute-start.2 = (bf16[64,640]{1,0:T(8,128)(2,1)S(1)}, bf16[64,640]{1,0:T(8,128)(2,1)S(1)}, u32[]{:S(2)}, u32[]{:S(2)}) collective-permute-start(bf16[64,640]{1,0:T(8,128)(2,1)S(1)} %bitcast.25), channel_id=1, source_target_pairs={{0,6},{1,25},{2,0},{3,27},{4,2},{5,29},{6,4},{7,31},{8,14},{9,1},{... | collective-permute-start | bytes 245768 | tf_op jit(solution)/shard_map/ppermute | solution.py:56
  23.6 2.5 %new_tokens.1 = (bf16[512,1024]{1,0:T(8,128)(2,1)S(1)}, bf16[512,1024]{1,0:T(8,128)(2,1)S(1)}, bf16[512,128]{1,0:T(8,128)(2,1)S(1)}) custom-call(bf16[512,768]{1,0:T(8,128)(2,1)} %q_in.1, bf16[576,512]{1,0:T(8,128)(2,1)} %bitcast.22, bf16[512,1024]{1,0:T(8,128)(2,1)} %up_ref.3), custom_call_target="tpu_custom_call" | custom-call | bytes 1024 | tf_op jit(solution)/shard_map/new_tokens/pallas_call | solution.py:171
  26.3 3.3 %collective-permute-start.3 = (bf16[256,640]{1,0:T(8,128)(2,1)S(1)}, bf16[256,640]{1,0:T(8,128)(2,1)S(1)}, u32[]{:S(2)}, u32[]{:S(2)}) collective-permute-start(bf16[256,640]{1,0:T(8,128)(2,1)S(1)} %constant_dynamic-update-slice_fusion.line_ref), channel_id=1, source_target_pairs={{0,16},{1,5},{2,18},{3,7},{4,20},{5,1},{6,22},{7,3},{8,24},{9,13},... | collective-permute-start | bytes 983048 | tf_op jit(solution)/shard_map/ppermute | solution.py:61
  29.6 0.7 collective-permute-start.4
  30.2 2.6 %collective-permute-start.5 = (bf16[256,640]{1,0:T(8,128)(2,1)S(1)}, bf16[256,640]{1,0:T(8,128)(2,1)S(1)}, u32[]{:S(2)}, u32[]{:S(2)}) collective-permute-start(bf16[256,640]{1,0:T(8,128)(2,1)S(1)} %constant_dynamic-update-slice_fusion.line_ref), channel_id=1, source_target_pairs={{0,24},{1,7},{2,26},{3,1},{4,28},{5,3},{6,30},{7,5},{8,0},{9,15},{... | collective-permute-start | bytes 983048 | tf_op jit(solution)/shard_map/ppermute | solution.py:61
  32.8 11.6 %attend_near.1 = (f32[512,1024]{1,0:T(8,128)S(1)}, f32[512,512]{1,0:T(8,128)S(1)}, bf16[4,4,224,512]{3,2,1,0:T(8,128)(2,1)S(1)}, bf16[4,4,224,512]{3,2,1,0:T(8,128)(2,1)S(1)}) custom-call(s32[2]{0:T(128)S(1)} %pad_add_fusion.place, bf16[512,1024]{1,0:T(8,128)(2,1)S(1)} %get-tuple-element.28.q_ref, ...), custom_call_target="tpu_custom_call" | custom-call | bytes 1024 | tf_op jit(solution)/shard_map/attend_near/pallas_call | solution.py:316
  45.3 1.0 %lift.1 = (bf16[768,1024]{1,0:T(8,128)(2,1)S(1)}, bf16[768,128]{1,0:T(8,128)(2,1)S(1)}) custom-call(bf16[256,640]{1,0:T(8,128)(2,1)S(1)} %collective-permute-done.3.refs_0_, bf16[256,640]{1,0:T(8,128)(2,1)S(1)} %collective-permute-done.4.refs_1_, bf16[256,640]{1,0:T(8,128)(2,1)S(1)} %collective-permute-done.5.refs_2_, bf16[512,1024]{1,0:T(8,128)(2,1)S(1)} %copy-done), custom_call_target="tpu_custom_call" | custom-call | bytes 1024 | tf_op jit(solution)/shard_map/lift/pallas_call | solution.py:202
  47.3 4.9 %attend_far.1.att_ref = bf16[512,512]{1,0:T(8,128)(2,1)S(1)} custom-call(bf16[512,1024]{1,0:T(8,128)(2,1)S(1)} %get-tuple-element.28.q_ref, f32[512,1024]{1,0:T(8,128)S(1)} %get-tuple-element.38.sum_ref, f32[512,512]{1,0:T(8,128)S(1)} %get-tuple-element.39.top_ref, bf16[768,1024]{1,0:T(8,128)(2,1)S(1)} %get-tuple-element.43.kv_ref, ...), custom_call_target="tpu_custom_call" | custom-call | flops 99999997952 | bytes 1024 | tf_op jit(solution)/shard_map/attend_far/pallas_call | solution.py:374
  52.5 1.8 %collective-permute-done.10.other_ref = bf16[512,512]{1,0:T(8,128)(2,1)S(1)} collective-permute-done((bf16[512,512]{1,0:T(8,128)(2,1)S(1)}, bf16[512,512]{1,0:T(8,128)(2,1)S(1)}, u32[]{:S(2)}, u32[]{:S(2)}) %collective-permute-start.10) | collective-permute-done | bytes 524320 | tf_op jit(solution)/shard_map/ppermute | solution.py:65
  54.9 3.2 %collective-permute-start.13 = (bf16[2,224,512]{2,1,0:T(8,128)(2,1)S(1)}, bf16[2,224,512]{2,1,0:T(8,128)(2,1)S(1)}, u32[]{:S(2)}, u32[]{:S(2)}) collective-permute-start(bf16[2,224,512]{2,1,0:T(8,128)(2,1)S(1)} %project.12), channel_id=1, source_target_pairs={{0,6},{1,25},{2,0},{3,27},{4,2},{5,29},{6,4},{7,31},{8,14},{9,1},{... | collective-permute-start | bytes 1376264 | tf_op jit(solution)/shard_map/ppermute | solution.py:56
  60.5 3.3 %collective-permute-start.18 = (bf16[2,224,512]{2,1,0:T(8,128)(2,1)S(1)}, bf16[2,224,512]{2,1,0:T(8,128)(2,1)S(1)}, u32[]{:S(2)}, u32[]{:S(2)}) collective-permute-start(bf16[2,224,512]{2,1,0:T(8,128)(2,1)S(1)} %project.15), channel_id=1, source_target_pairs={{0,6},{1,25},{2,0},{3,27},{4,2},{5,29},{6,4},{7,31},{8,14},{9,1},{... | collective-permute-start | bytes 1376264 | tf_op jit(solution)/shard_map/ppermute | solution.py:56
  65.3 2.7 %collective-permute-start.14 = (bf16[2,224,512]{2,1,0:T(8,128)(2,1)S(1)}, bf16[2,224,512]{2,1,0:T(8,128)(2,1)S(1)}, u32[]{:S(2)}, u32[]{:S(2)}) collective-permute-start(bf16[2,224,512]{2,1,0:T(8,128)(2,1)S(1)} %add_convert_fusion.2), channel_id=1, source_target_pairs={{0,6},{1,25},{2,0},{3,27},{4,2},{5,29},{6,4},{7,31},{8,14},{9,1},{... | collective-permute-start | bytes 1376264 | tf_op jit(solution)/shard_map/ppermute | solution.py:56
  68.0 0.8 collective-permute-done.16
  70.4 3.3 %collective-permute-done.12 = bf16[2,224,512]{2,1,0:T(8,128)(2,1)S(1)} collective-permute-done((bf16[2,224,512]{2,1,0:T(8,128)(2,1)S(1)}, bf16[2,224,512]{2,1,0:T(8,128)(2,1)S(1)}, u32[]{:S(2)}, u32[]{:S(2)}) %collective-permute-start.12) | collective-permute-done | bytes 458784 | tf_op jit(solution)/shard_map/ppermute | solution.py:56
  73.7 1.1 %collective-permute-done.14 = bf16[2,224,512]{2,1,0:T(8,128)(2,1)S(1)} collective-permute-done((bf16[2,224,512]{2,1,0:T(8,128)(2,1)S(1)}, bf16[2,224,512]{2,1,0:T(8,128)(2,1)S(1)}, u32[]{:S(2)}, u32[]{:S(2)}) %collective-permute-start.14) | collective-permute-done | bytes 458784 | tf_op jit(solution)/shard_map/ppermute | solution.py:56
  75.0 3.7 %collective-permute-done.17 = bf16[2,224,512]{2,1,0:T(8,128)(2,1)S(1)} collective-permute-done((bf16[2,224,512]{2,1,0:T(8,128)(2,1)S(1)}, bf16[2,224,512]{2,1,0:T(8,128)(2,1)S(1)}, u32[]{:S(2)}, u32[]{:S(2)}) %collective-permute-start.17) | collective-permute-done | bytes 458784 | tf_op jit(solution)/shard_map/ppermute | solution.py:56
  79.0 0.8 collective-permute-start.20
  79.8 1.1 %collective-permute-done.15 = bf16[224,512]{1,0:T(8,128)(2,1)S(1)} collective-permute-done((bf16[224,512]{1,0:T(8,128)(2,1)S(1)}, bf16[224,512]{1,0:T(8,128)(2,1)S(1)}, u32[]{:S(2)}, u32[]{:S(2)}) %collective-permute-start.15) | collective-permute-done | bytes 229408 | tf_op jit(solution)/shard_map/ppermute | solution.py:61
  81.0 5.7 %collective-permute-done.19 = bf16[224,512]{1,0:T(8,128)(2,1)S(1)} collective-permute-done((bf16[224,512]{1,0:T(8,128)(2,1)S(1)}, bf16[224,512]{1,0:T(8,128)(2,1)S(1)}, u32[]{:S(2)}, u32[]{:S(2)}) %collective-permute-start.19) | collective-permute-done | bytes 229408 | tf_op jit(solution)/shard_map/ppermute | solution.py:61
  86.6 2.1 %collective-permute-done.20 = bf16[224,512]{1,0:T(8,128)(2,1)S(1)} collective-permute-done((bf16[224,512]{1,0:T(8,128)(2,1)S(1)}, bf16[224,512]{1,0:T(8,128)(2,1)S(1)}, u32[]{:S(2)}, u32[]{:S(2)}) %collective-permute-start.20) | collective-permute-done | bytes 229408 | tf_op jit(solution)/shard_map/ppermute | solution.py:61
  88.8 0.9 fusion.4
  (45 shorter events, 9.4 us)
Async XLA Ops:
  0.0 32.8 %copy-start = (bf16[512,1024]{1,0:T(8,128)(2,1)S(1)}, bf16[512,1024]{1,0:T(8,128)(2,1)}, u32[]{:S(2)}) copy-start(bf16[512,1024]{1,0:T(8,128)(2,1)} %up_ref.3) | copy-start | bytes 3145732
  17.3 8.8 %collective-permute-start = (bf16[64,640]{1,0:T(8,128)(2,1)S(1)}, bf16[64,640]{1,0:T(8,128)(2,1)S(1)}, u32[]{:S(2)}, u32[]{:S(2)}) collective-permute-start(bf16[64,640]{1,0:T(8,128)(2,1)S(1)} %bitcast.23), channel_id=1, source_target_pairs={{0,4},{1,17},{2,6},{3,19},{4,0},{5,21},{6,2},{7,23},{8,12},{9,25},... | collective-permute-start | bytes 245768 | tf_op jit(solution)/shard_map/ppermute | solution.py:56
  20.3 5.8 %collective-permute-start.1 = (bf16[64,640]{1,0:T(8,128)(2,1)S(1)}, bf16[64,640]{1,0:T(8,128)(2,1)S(1)}, u32[]{:S(2)}, u32[]{:S(2)}) collective-permute-start(bf16[64,640]{1,0:T(8,128)(2,1)S(1)} %bitcast.24), channel_id=1, source_target_pairs={{0,2},{1,9},{2,4},{3,11},{4,6},{5,13},{6,0},{7,15},{8,10},{9,17},{... | collective-permute-start | bytes 245768 | tf_op jit(solution)/shard_map/ppermute | solution.py:56
  20.9 5.2 %collective-permute-start.2 = (bf16[64,640]{1,0:T(8,128)(2,1)S(1)}, bf16[64,640]{1,0:T(8,128)(2,1)S(1)}, u32[]{:S(2)}, u32[]{:S(2)}) collective-permute-start(bf16[64,640]{1,0:T(8,128)(2,1)S(1)} %bitcast.25), channel_id=1, source_target_pairs={{0,6},{1,25},{2,0},{3,27},{4,2},{5,29},{6,4},{7,31},{8,14},{9,1},{... | collective-permute-start | bytes 245768 | tf_op jit(solution)/shard_map/ppermute | solution.py:56
  26.2 6.6 %collective-permute-start.6 = (bf16[256,640]{1,0:T(8,128)(2,1)S(1)}, bf16[256,640]{1,0:T(8,128)(2,1)S(1)}, u32[]{:S(2)}, u32[]{:S(2)}) collective-permute-start(bf16[256,640]{1,0:T(8,128)(2,1)S(1)} %constant_dynamic-update-slice_fusion.line_ref), channel_id=1, source_target_pairs={{0,1},{1,0},{2,3},{3,2},{4,5},{5,4},{6,7},{7,6},{8,9},{9,8},{10,11... | collective-permute-start | bytes 983048 | tf_op jit(solution)/shard_map/ppermute | solution.py:65
  26.3 18.2 %collective-permute-start.3 = (bf16[256,640]{1,0:T(8,128)(2,1)S(1)}, bf16[256,640]{1,0:T(8,128)(2,1)S(1)}, u32[]{:S(2)}, u32[]{:S(2)}) collective-permute-start(bf16[256,640]{1,0:T(8,128)(2,1)S(1)} %constant_dynamic-update-slice_fusion.line_ref), channel_id=1, source_target_pairs={{0,16},{1,5},{2,18},{3,7},{4,20},{5,1},{6,22},{7,3},{8,24},{9,13},... | collective-permute-start | bytes 983048 | tf_op jit(solution)/shard_map/ppermute | solution.py:61
  29.6 14.9 %collective-permute-start.4 = (bf16[256,640]{1,0:T(8,128)(2,1)S(1)}, bf16[256,640]{1,0:T(8,128)(2,1)S(1)}, u32[]{:S(2)}, u32[]{:S(2)}) collective-permute-start(bf16[256,640]{1,0:T(8,128)(2,1)S(1)} %constant_dynamic-update-slice_fusion.line_ref), channel_id=1, source_target_pairs={{0,8},{1,3},{2,10},{3,5},{4,12},{5,7},{6,14},{7,1},{8,16},{9,11},{... | collective-permute-start | bytes 983048 | tf_op jit(solution)/shard_map/ppermute | solution.py:61
  30.2 14.2 %collective-permute-start.5 = (bf16[256,640]{1,0:T(8,128)(2,1)S(1)}, bf16[256,640]{1,0:T(8,128)(2,1)S(1)}, u32[]{:S(2)}, u32[]{:S(2)}) collective-permute-start(bf16[256,640]{1,0:T(8,128)(2,1)S(1)} %constant_dynamic-update-slice_fusion.line_ref), channel_id=1, source_target_pairs={{0,24},{1,7},{2,26},{3,1},{4,28},{5,3},{6,30},{7,5},{8,0},{9,15},{... | collective-permute-start | bytes 983048 | tf_op jit(solution)/shard_map/ppermute | solution.py:61
  44.5 2.4 %collective-permute-start.7 = (bf16[256,640]{1,0:T(8,128)(2,1)S(1)}, bf16[256,640]{1,0:T(8,128)(2,1)S(1)}, u32[]{:S(2)}, u32[]{:S(2)}) collective-permute-start(bf16[256,640]{1,0:T(8,128)(2,1)S(1)} %collective-permute-done.3.refs_0_), channel_id=1, source_target_pairs={{0,1},{1,0},{2,3},{3,2},{4,5},{5,4},{6,7},{7,6},{8,9},{9,8},{10,11... | collective-permute-start | bytes 983048 | tf_op jit(solution)/shard_map/ppermute | solution.py:65
  44.7 2.1 %collective-permute-start.8 = (bf16[256,640]{1,0:T(8,128)(2,1)S(1)}, bf16[256,640]{1,0:T(8,128)(2,1)S(1)}, u32[]{:S(2)}, u32[]{:S(2)}) collective-permute-start(bf16[256,640]{1,0:T(8,128)(2,1)S(1)} %collective-permute-done.4.refs_1_), channel_id=1, source_target_pairs={{0,1},{1,0},{2,3},{3,2},{4,5},{5,4},{6,7},{7,6},{8,9},{9,8},{10,11... | collective-permute-start | bytes 983048 | tf_op jit(solution)/shard_map/ppermute | solution.py:65
  45.2 2.1 %collective-permute-start.9 = (bf16[256,640]{1,0:T(8,128)(2,1)S(1)}, bf16[256,640]{1,0:T(8,128)(2,1)S(1)}, u32[]{:S(2)}, u32[]{:S(2)}) collective-permute-start(bf16[256,640]{1,0:T(8,128)(2,1)S(1)} %collective-permute-done.5.refs_2_), channel_id=1, source_target_pairs={{0,1},{1,0},{2,3},{3,2},{4,5},{5,4},{6,7},{7,6},{8,9},{9,8},{10,11... | collective-permute-start | bytes 983048 | tf_op jit(solution)/shard_map/ppermute | solution.py:65
  46.4 7.9 %collective-permute-start.11 = (bf16[4,4,224,512]{3,2,1,0:T(8,128)(2,1)S(1)}, bf16[4,4,224,512]{3,2,1,0:T(8,128)(2,1)S(1)}, u32[]{:S(2)}, u32[]{:S(2)}) collective-permute-start(bf16[4,4,224,512]{3,2,1,0:T(8,128)(2,1)S(1)} %get-tuple-element.46), channel_id=1, source_target_pairs={{0,1},{1,0},{2,3},{3,2},{4,5},{5,4},{6,7},{7,6},{8,9},{9,8},{10,11... | collective-permute-start | bytes 11010056 | tf_op jit(solution)/shard_map/ppermute | solution.py:65
  52.2 2.0 %collective-permute-start.10 = (bf16[512,512]{1,0:T(8,128)(2,1)S(1)}, bf16[512,512]{1,0:T(8,128)(2,1)S(1)}, u32[]{:S(2)}, u32[]{:S(2)}) collective-permute-start(bf16[512,512]{1,0:T(8,128)(2,1)S(1)} %attend_far.1.att_ref), channel_id=1, source_target_pairs={{0,1},{1,0},{2,3},{3,2},{4,5},{5,4},{6,7},{7,6},{8,9},{9,8},{10,11... | collective-permute-start | bytes 1572872 | tf_op jit(solution)/shard_map/ppermute | solution.py:65
  54.9 10.3 %collective-permute-start.13 = (bf16[2,224,512]{2,1,0:T(8,128)(2,1)S(1)}, bf16[2,224,512]{2,1,0:T(8,128)(2,1)S(1)}, u32[]{:S(2)}, u32[]{:S(2)}) collective-permute-start(bf16[2,224,512]{2,1,0:T(8,128)(2,1)S(1)} %project.12), channel_id=1, source_target_pairs={{0,6},{1,25},{2,0},{3,27},{4,2},{5,29},{6,4},{7,31},{8,14},{9,1},{... | collective-permute-start | bytes 1376264 | tf_op jit(solution)/shard_map/ppermute | solution.py:56
  58.8 10.0 %collective-permute-start.16 = (bf16[2,224,512]{2,1,0:T(8,128)(2,1)S(1)}, bf16[2,224,512]{2,1,0:T(8,128)(2,1)S(1)}, u32[]{:S(2)}, u32[]{:S(2)}) collective-permute-start(bf16[2,224,512]{2,1,0:T(8,128)(2,1)S(1)} %project.8), channel_id=1, source_target_pairs={{0,2},{1,9},{2,4},{3,11},{4,6},{5,13},{6,0},{7,15},{8,10},{9,17},{... | collective-permute-start | bytes 1376264 | tf_op jit(solution)/shard_map/ppermute | solution.py:56
  59.8 13.9 %collective-permute-start.12 = (bf16[2,224,512]{2,1,0:T(8,128)(2,1)S(1)}, bf16[2,224,512]{2,1,0:T(8,128)(2,1)S(1)}, u32[]{:S(2)}, u32[]{:S(2)}) collective-permute-start(bf16[2,224,512]{2,1,0:T(8,128)(2,1)S(1)} %project.10), channel_id=1, source_target_pairs={{0,2},{1,9},{2,4},{3,11},{4,6},{5,13},{6,0},{7,15},{8,10},{9,17},{... | collective-permute-start | bytes 1376264 | tf_op jit(solution)/shard_map/ppermute | solution.py:56
  60.5 14.4 %collective-permute-start.18 = (bf16[2,224,512]{2,1,0:T(8,128)(2,1)S(1)}, bf16[2,224,512]{2,1,0:T(8,128)(2,1)S(1)}, u32[]{:S(2)}, u32[]{:S(2)}) collective-permute-start(bf16[2,224,512]{2,1,0:T(8,128)(2,1)S(1)} %project.15), channel_id=1, source_target_pairs={{0,6},{1,25},{2,0},{3,27},{4,2},{5,29},{6,4},{7,31},{8,14},{9,1},{... | collective-permute-start | bytes 1376264 | tf_op jit(solution)/shard_map/ppermute | solution.py:56
  65.3 9.4 %collective-permute-start.14 = (bf16[2,224,512]{2,1,0:T(8,128)(2,1)S(1)}, bf16[2,224,512]{2,1,0:T(8,128)(2,1)S(1)}, u32[]{:S(2)}, u32[]{:S(2)}) collective-permute-start(bf16[2,224,512]{2,1,0:T(8,128)(2,1)S(1)} %add_convert_fusion.2), channel_id=1, source_target_pairs={{0,6},{1,25},{2,0},{3,27},{4,2},{5,29},{6,4},{7,31},{8,14},{9,1},{... | collective-permute-start | bytes 1376264 | tf_op jit(solution)/shard_map/ppermute | solution.py:56
  68.9 9.8 %collective-permute-start.17 = (bf16[2,224,512]{2,1,0:T(8,128)(2,1)S(1)}, bf16[2,224,512]{2,1,0:T(8,128)(2,1)S(1)}, u32[]{:S(2)}, u32[]{:S(2)}) collective-permute-start(bf16[2,224,512]{2,1,0:T(8,128)(2,1)S(1)} %add_convert_fusion.1), channel_id=1, source_target_pairs={{0,2},{1,9},{2,4},{3,11},{4,6},{5,13},{6,0},{7,15},{8,10},{9,17},{... | collective-permute-start | bytes 1376264 | tf_op jit(solution)/shard_map/ppermute | solution.py:56
  74.9 6.1 %collective-permute-start.15 = (bf16[224,512]{1,0:T(8,128)(2,1)S(1)}, bf16[224,512]{1,0:T(8,128)(2,1)S(1)}, u32[]{:S(2)}, u32[]{:S(2)}) collective-permute-start(bf16[224,512]{1,0:T(8,128)(2,1)S(1)} %fusion.3), channel_id=1, source_target_pairs={{0,24},{1,7},{2,26},{3,1},{4,28},{5,3},{6,30},{7,5},{8,0},{9,15},{... | collective-permute-start | bytes 688136 | tf_op jit(solution)/shard_map/ppermute | solution.py:61
  78.9 7.7 %collective-permute-start.19 = (bf16[224,512]{1,0:T(8,128)(2,1)S(1)}, bf16[224,512]{1,0:T(8,128)(2,1)S(1)}, u32[]{:S(2)}, u32[]{:S(2)}) collective-permute-start(bf16[224,512]{1,0:T(8,128)(2,1)S(1)} %get-tuple-element.49), channel_id=1, source_target_pairs={{0,16},{1,5},{2,18},{3,7},{4,20},{5,1},{6,22},{7,3},{8,24},{9,13},... | collective-permute-start | bytes 688136 | tf_op jit(solution)/shard_map/ppermute | solution.py:61
  79.0 9.8 %collective-permute-start.20 = (bf16[224,512]{1,0:T(8,128)(2,1)S(1)}, bf16[224,512]{1,0:T(8,128)(2,1)S(1)}, u32[]{:S(2)}, u32[]{:S(2)}) collective-permute-start(bf16[224,512]{1,0:T(8,128)(2,1)S(1)} %get-tuple-element.50), channel_id=1, source_target_pairs={{0,8},{1,3},{2,10},{3,5},{4,12},{5,7},{6,14},{7,1},{8,16},{9,11},{... | collective-permute-start | bytes 688136 | tf_op jit(solution)/shard_map/ppermute | solution.py:61
